TPU v7x, 32 devices: a whole 2x2x4 slice. The times are simulated.
32 devices in a mesh: clip: 16 (over z, x, core), seq: 2 (over y).
Axes of the slice: x: 2, y: 2, z: 4, core: 2. Of those that a mesh axis runs over, the one named last changes fastest.
Arguments:
- inputs: bfloat16 [32, 3136, 768], P('clip', 'seq'), may hold values from -6 to 6
- frame_tokens: int32 [32], P('clip'), may hold values from 98 to 196, as said below
- clip_frames: int32 [32], P('clip'), may hold values from 8 to 16, as said below
- norm1_gain: float32 [768], replicated, may hold values from 0.1 to 1.9
- norm1_bias: float32 [768], replicated, may hold values from -3 to 3
- qkv_weight: bfloat16 [768, 2304], replicated, may hold values from -0.3125 to 0.3125
- query_bias: float32 [768], replicated, may hold values from -3 to 3
- value_bias: float32 [768], replicated, may hold values from -3 to 3
- out_weight: bfloat16 [768, 768], replicated, may hold values from -0.875 to 0.875
- out_bias: float32 [768], replicated, may hold values from -3 to 3
- norm2_gain: float32 [768], replicated, may hold values from 0.1 to 1.9
- norm2_bias: float32 [768], replicated, may hold values from -3 to 3
- fc1_weight: bfloat16 [768, 3072], replicated, may hold values from -0.21875 to 0.21875
- fc1_bias: float32 [3072], replicated, may hold values from -3 to 3
- fc2_weight: bfloat16 [3072, 768], replicated, may hold values from -0.15625 to 0.15625
- fc2_bias: float32 [768], replicated, may hold values from -3 to 3
- learn_gain: float32 [768], replicated, may hold values from 0.1 to 1.9
- learn_bias: float32 [768], replicated, may hold values from -3 to 3
- map1_weight: bfloat16 [768, 64], replicated, may hold values from -0.21875 to 0.21875
- map1_bias: float32 [64], replicated, may hold values from -3 to 3
- map2_weight: bfloat16 [64, 8], replicated, may hold values from -1.5 to 1.5
- map2_bias: float32 [8], replicated, may hold values from -4 to 4
- cot_pooled: bfloat16 [32, 16, 8, 768], P('clip', 'seq'), may hold values from -6 to 6
Outputs:
- pooled: bfloat16 [32, 16, 8, 768], P('clip', 'seq')
- penalty: float32 [], replicated
- input_grad: float32 [32, 3136, 768], P('clip', 'seq')
- norm1_gain_grad: float32 [768], replicated
- norm1_bias_grad: float32 [768], replicated
- qkv_weight_grad: float32 [768, 2304], P('clip', 'seq')
- query_bias_grad: float32 [768], replicated
- value_bias_grad: float32 [768], replicated
- out_weight_grad: float32 [768, 768], P('clip', 'seq')
- out_bias_grad: float32 [768], replicated
- norm2_gain_grad: float32 [768], replicated
- norm2_bias_grad: float32 [768], replicated
- fc1_weight_grad: float32 [768, 3072], P('clip', 'seq')
- fc1_bias_grad: float32 [3072], replicated
- fc2_weight_grad: float32 [3072, 768], P('clip', 'seq')
- fc2_bias_grad: float32 [768], replicated
- learn_gain_grad: float32 [768], replicated
- learn_bias_grad: float32 [768], replicated
- map1_weight_grad: float32 [768, 64], replicated
- map1_bias_grad: float32 [64], replicated
- map2_weight_grad: float32 [64, 8], replicated
- map2_bias_grad: float32 [8], replicated
Inputs may be any that keep to these rules, and one draw needn't show every extreme that they name: `frame_tokens`: every 2 clips that one index of clip holds contain one whose frames hold 196 tokens. `clip_frames`: every 2 clips that one index of clip holds contain one of 16 frames.
All inputs are finite; a program needn't handle non-finite values.
Results may differ from a plain program's by a relative error of at most 0.028.
Values may be sent and summed in bfloat16 or wider, within the bound.
No kernel may reach another device: no remote copies, remote signals or barrier semaphores. Data moves between devices by JAX's collectives and lax.ppermute only.
A program may use at most 384 MiB of HBM per device.

v0:
```python
import jax
import jax.numpy as jnp
from jax import lax
from jax.sharding import PartitionSpec as P

HEADS = 12
HEAD = 64
NTOK = 8
PATCH = 196


epsilon = 1e-06
masked_score = -1e30


def normed(value, gain, bias):
    average = jnp.mean(value, axis=-1, keepdims=True)
    centered = value - average
    variance = jnp.mean(centered * centered, axis=-1, keepdims=True)
    return centered * lax.rsqrt(variance + epsilon) * gain + bias


def norm_back(value, gain, bias, grad):
    result, pullback = jax.vjp(normed, value, gain, bias)
    return pullback(grad)


def gelu_exact(value):
    return jax.nn.gelu(value, approximate=False)


def gelu_back(value, grad):
    result, pullback = jax.vjp(gelu_exact, value)
    return pullback(grad)[0]


def project(left, weight):
    flat = left.reshape(-1, left.shape[-1])
    result = jnp.dot(flat, weight, preferred_element_type=jnp.float32)
    return result.reshape(left.shape[:-1] + (weight.shape[1],))


def back_project(grad, weight):
    flat = grad.reshape(-1, grad.shape[-1])
    result = lax.dot_general(
        flat, weight, (((1,), (1,)), ((), ())), preferred_element_type=jnp.float32
    )
    return result.reshape(grad.shape[:-1] + (weight.shape[0],))


def weight_grad(left, grad):
    flat_left = left.reshape(-1, left.shape[-1])
    flat_grad = grad.reshape(-1, grad.shape[-1])
    return lax.dot_general(
        flat_left, flat_grad, (((0,), (0,)), ((), ())), preferred_element_type=jnp.float32
    )


def column_sums(grad):
    return jnp.sum(grad.astype(jnp.float32).reshape(-1, grad.shape[-1]), axis=0)


def split_heads(value):
    clip_count, row_count, model_width = value.shape
    return value.reshape(clip_count, row_count, HEADS, model_width // HEADS).transpose(2, 0, 1, 3)


def merge_heads(value):
    head_count, clip_count, row_count, size_head = value.shape
    return value.transpose(1, 2, 0, 3).reshape(clip_count, row_count, head_count * size_head)


def key_allowed(frame_tokens, clip_frames, count):
    row_ids = jnp.arange(count, dtype=jnp.int32)
    frame_ids = row_ids // PATCH
    slot_ids = row_ids - frame_ids * PATCH
    return (frame_ids[None, :] < clip_frames[:, None]) & (slot_ids[None, :] < frame_tokens[:, None])


def attend_fold(query_heads, frame_tokens, clip_frames):

    def attend_folding(state_in, pieces, offset):
        key_rows, value_rows = pieces
        allowed = key_allowed(frame_tokens, clip_frames, key_rows.shape[1])

        def attend_one_head(operands):
            query_head, key_head, value_head, running, totals, summed = operands
            scores = jnp.einsum(
                "crd,cpd->crp", query_head, key_head, preferred_element_type=jnp.float32
            )
            scores = jnp.where(allowed[:, None, :], scores, masked_score)
            newest = jnp.maximum(running, jnp.max(scores, axis=2))
            weights = jnp.where(allowed[:, None, :], jnp.exp(scores - newest[:, :, None]), 0.0)
            shrink = jnp.exp(running - newest)
            totals = totals * shrink + jnp.sum(weights, axis=2)
            summed = summed * shrink[:, :, None] + jnp.einsum(
                "crp,cpd->crd",
                weights.astype(jnp.bfloat16),
                value_head,
                preferred_element_type=jnp.float32,
            )
            return (newest, totals, summed)

        running, totals, summed = state_in
        return lax.map(
            attend_one_head,
            (query_heads, split_heads(key_rows), split_heads(value_rows), running, totals, summed),
        )

    return attend_folding


def grad_fold(query_heads, grad_heads, log_total, row_inner, frame_tokens, clip_frames):

    def grad_folding(state_in, pieces, offset):
        key_rows, value_rows = pieces
        count = key_rows.shape[1]
        allowed = key_allowed(frame_tokens, clip_frames, count)

        def grad_one_head(operands):
            query_head, grad_head, total_head, inner_head, key_head, value_head = operands
            scores = jnp.einsum(
                "crd,cpd->crp", query_head, key_head, preferred_element_type=jnp.float32
            )
            scores = jnp.where(allowed[:, None, :], scores, masked_score)
            probs = jnp.where(allowed[:, None, :], jnp.exp(scores - total_head[:, :, None]), 0.0)
            grad_prob = jnp.einsum(
                "crd,cpd->crp", grad_head, value_head, preferred_element_type=jnp.float32
            )
            grad_score = (probs * (grad_prob - inner_head[:, :, None])).astype(jnp.bfloat16)
            query_grad = jnp.einsum(
                "crp,cpd->crd", grad_score, key_head, preferred_element_type=jnp.float32
            )
            key_grad = jnp.einsum(
                "crp,crd->cpd", grad_score, query_head, preferred_element_type=jnp.float32
            )
            value_grad = jnp.einsum(
                "crp,crd->cpd",
                probs.astype(jnp.bfloat16),
                grad_head,
                preferred_element_type=jnp.float32,
            )
            return (query_grad, key_grad, value_grad)

        query_grad, key_grad, value_grad = lax.map(
            grad_one_head,
            (
                query_heads,
                grad_heads,
                log_total,
                row_inner,
                split_heads(key_rows),
                split_heads(value_rows),
            ),
        )
        key_all = merge_heads(key_grad)
        value_all = merge_heads(value_grad)
        return (query_grad, key_all, value_all)

    return grad_folding


def shards(
    inputs,
    frame_tokens,
    clip_frames,
    norm1_gain,
    norm1_bias,
    qkv_weight,
    query_bias,
    value_bias,
    out_weight,
    out_bias,
    norm2_gain,
    norm2_bias,
    fc1_weight,
    fc1_bias,
    fc2_weight,
    fc2_bias,
    learn_gain,
    learn_bias,
    map1_weight,
    map1_bias,
    map2_weight,
    map2_bias,
    cot_pooled,
):
    clip_count, row_count, model_width = inputs.shape
    seq_size = lax.axis_size("seq")
    position = lax.axis_index("seq")
    full_length = row_count * seq_size
    frames_here = row_count // PATCH
    scaling = HEAD ** (-0.5)
    slots_all = float(clip_count * lax.axis_size("clip") * (full_length // PATCH))
    state = inputs.astype(jnp.float32)
    act1 = normed(state, norm1_gain, norm1_bias).astype(jnp.bfloat16)
    mixed = project(act1, qkv_weight)
    queries = ((mixed[..., :model_width] + query_bias) * scaling).astype(jnp.bfloat16)
    key_rows = mixed[..., model_width : 2 * model_width].astype(jnp.bfloat16)
    value_rows = (mixed[..., 2 * model_width :] + value_bias).astype(jnp.bfloat16)
    query_heads = split_heads(queries)
    start_state = (
        jnp.full((HEADS, clip_count, row_count), masked_score, jnp.float32),
        jnp.zeros((HEADS, clip_count, row_count), jnp.float32),
        jnp.zeros((HEADS, clip_count, row_count, HEAD), jnp.float32),
    )
    forward_fold = attend_fold(query_heads, frame_tokens, clip_frames)
    running, totals, summed = forward_fold(
        start_state,
        (
            lax.all_gather(key_rows, "seq", axis=1, tiled=True),
            lax.all_gather(value_rows, "seq", axis=1, tiled=True),
        ),
        jnp.int32(0),
    )
    attended = merge_heads(summed / totals[..., None])
    log_total = running + jnp.log(totals)
    att_low = attended.astype(jnp.bfloat16)
    resid1 = state + project(att_low, out_weight) + out_bias
    act2 = normed(resid1, norm2_gain, norm2_bias).astype(jnp.bfloat16)
    hidden_pre = project(act2, fc1_weight) + fc1_bias
    hidden = gelu_exact(hidden_pre).astype(jnp.bfloat16)
    resid2 = resid1 + project(hidden, fc2_weight) + fc2_bias
    act3 = normed(resid2, learn_gain, learn_bias).astype(jnp.bfloat16)
    map_pre = project(act3, map1_weight) + map1_bias
    map_hidden = gelu_exact(map_pre).astype(jnp.bfloat16)
    logits = project(map_hidden, map2_weight) + map2_bias
    row_ids = position * row_count + jnp.arange(row_count, dtype=jnp.int32)
    frame_ids = row_ids // PATCH
    slot_ids = row_ids - frame_ids * PATCH
    valid = (
        (frame_ids[None, :] < clip_frames[:, None]) & (slot_ids[None, :] < frame_tokens[:, None])
    ).astype(jnp.float32)
    sigmoid_raw = jax.nn.sigmoid(logits)
    gates = sigmoid_raw * valid[..., None]
    inverse = lax.rsqrt(frame_tokens.astype(jnp.float32))
    gates_low = gates.astype(jnp.bfloat16).reshape(clip_count, frames_here, PATCH, NTOK)
    output_low = resid2.astype(jnp.bfloat16).reshape(clip_count, frames_here, PATCH, model_width)
    pooled = jnp.einsum(
        "cfpk,cfpd->cfkd", gates_low, output_low, preferred_element_type=jnp.float32
    )
    pooled = (pooled * inverse[:, None, None, None]).astype(jnp.bfloat16)
    gate_sum = jnp.sum(gates, axis=-1)
    gate_square = jnp.sum(gates * gates, axis=-1)
    pair_count = NTOK * (NTOK - 1)
    intersection = (
        jnp.sum(jnp.sum(gate_sum * gate_sum - gate_square, axis=1) * inverse * inverse) / pair_count
    )
    grad_out = jnp.einsum(
        "cfpk,cfkd->cfpd", gates_low, cot_pooled, preferred_element_type=jnp.float32
    )
    grad_out = (grad_out * inverse[:, None, None, None]).reshape(clip_count, row_count, model_width)
    grad_gate = jnp.einsum(
        "cfpd,cfkd->cfpk", output_low, cot_pooled, preferred_element_type=jnp.float32
    )
    grad_gate = (grad_gate * inverse[:, None, None, None]).reshape(clip_count, row_count, NTOK)
    penalty_factor = 2.0 / pair_count * (inverse * inverse)[:, None, None] / slots_all
    grad_gate = (grad_gate + penalty_factor * (gate_sum[..., None] - gates)) * valid[..., None]
    grad_logit = (grad_gate * sigmoid_raw * (1.0 - sigmoid_raw)).astype(jnp.bfloat16)
    map2_grad = weight_grad(map_hidden, grad_logit)
    map2_bias_grad = column_sums(grad_logit)
    grad_mpre = gelu_back(map_pre, back_project(grad_logit, map2_weight)).astype(jnp.bfloat16)
    map1_grad = weight_grad(act3, grad_mpre)
    map1_bias_grad = column_sums(grad_mpre)
    grad_res2, learn_gain_grad, learn_bias_grad = norm_back(
        resid2, learn_gain, learn_bias, back_project(grad_mpre, map1_weight)
    )
    grad_res2 = grad_res2 + grad_out
    branch_two = grad_res2.astype(jnp.bfloat16)
    fc2_grad = weight_grad(hidden, branch_two)
    fc2_bias_grad = column_sums(branch_two)
    grad_pre = gelu_back(hidden_pre, back_project(branch_two, fc2_weight)).astype(jnp.bfloat16)
    fc1_grad = weight_grad(act2, grad_pre)
    fc1_bias_grad = column_sums(grad_pre)
    grad_res1, norm2_gain_grad, norm2_bias_grad = norm_back(
        resid1, norm2_gain, norm2_bias, back_project(grad_pre, fc1_weight)
    )
    grad_res1 = grad_res1 + grad_res2
    branch_one = grad_res1.astype(jnp.bfloat16)
    out_grad = weight_grad(att_low, branch_one)
    out_bias_grad = column_sums(branch_one)
    grad_att = back_project(branch_one, out_weight).astype(jnp.bfloat16)
    product_rows = (grad_att.astype(jnp.float32) * attended).reshape(
        clip_count, row_count, HEADS, HEAD
    )
    row_inner = jnp.sum(product_rows, axis=-1).transpose(2, 0, 1)
    backward_fold = grad_fold(
        query_heads, split_heads(grad_att), log_total, row_inner, frame_tokens, clip_frames
    )
    back_start = (
        jnp.zeros((HEADS, clip_count, row_count, HEAD), jnp.float32),
        jnp.zeros((clip_count, full_length, model_width), jnp.float32),
        jnp.zeros((clip_count, full_length, model_width), jnp.float32),
    )
    query_sum, key_all, value_all = backward_fold(
        back_start,
        (
            lax.all_gather(key_rows, "seq", axis=1, tiled=True),
            lax.all_gather(value_rows, "seq", axis=1, tiled=True),
        ),
        jnp.int32(0),
    )
    key_home, value_home = (
        lax.psum_scatter(
            key_all.astype(jnp.bfloat16), "seq", scatter_dimension=1, tiled=True
        ).astype(jnp.float32),
        lax.psum_scatter(
            value_all.astype(jnp.bfloat16), "seq", scatter_dimension=1, tiled=True
        ).astype(jnp.float32),
    )
    grad_query = (merge_heads(query_sum) * scaling).astype(jnp.bfloat16)
    grad_value = value_home.astype(jnp.bfloat16)
    grad_mixed = jnp.concatenate([grad_query, key_home.astype(jnp.bfloat16), grad_value], axis=-1)
    qkv_grad = weight_grad(act1, grad_mixed)
    query_bias_grad = column_sums(grad_query)
    value_bias_grad = column_sums(grad_value)
    grad_in, norm1_gain_grad, norm1_bias_grad = norm_back(
        state, norm1_gain, norm1_bias, back_project(grad_mixed, qkv_weight)
    )
    input_grad = grad_in + grad_res1
    matrices = (qkv_grad, out_grad, fc1_grad, fc2_grad)
    matrices = (
        lax.psum_scatter(
            matrices[0].astype(jnp.bfloat16), "clip", scatter_dimension=0, tiled=True
        ).astype(jnp.float32),
        lax.psum_scatter(
            matrices[1].astype(jnp.bfloat16), "clip", scatter_dimension=0, tiled=True
        ).astype(jnp.float32),
        lax.psum_scatter(
            matrices[2].astype(jnp.bfloat16), "clip", scatter_dimension=0, tiled=True
        ).astype(jnp.float32),
        lax.psum_scatter(
            matrices[3].astype(jnp.bfloat16), "clip", scatter_dimension=0, tiled=True
        ).astype(jnp.float32),
    )
    matrices = (
        lax.psum_scatter(
            matrices[0].astype(jnp.bfloat16), "seq", scatter_dimension=1, tiled=True
        ).astype(jnp.float32),
        lax.psum_scatter(
            matrices[1].astype(jnp.bfloat16), "seq", scatter_dimension=1, tiled=True
        ).astype(jnp.float32),
        lax.psum_scatter(
            matrices[2].astype(jnp.bfloat16), "seq", scatter_dimension=1, tiled=True
        ).astype(jnp.float32),
        lax.psum_scatter(
            matrices[3].astype(jnp.bfloat16), "seq", scatter_dimension=1, tiled=True
        ).astype(jnp.float32),
    )
    small_sums = lax.psum(
        (
            norm1_gain_grad,
            norm1_bias_grad,
            query_bias_grad,
            value_bias_grad,
            out_bias_grad,
            norm2_gain_grad,
            norm2_bias_grad,
            fc1_bias_grad,
            fc2_bias_grad,
            learn_gain_grad,
            learn_bias_grad,
            map1_grad,
            map1_bias_grad,
            map2_grad,
            map2_bias_grad,
            intersection,
        ),
        ("clip", "seq"),
    )
    penalty = small_sums[15] / slots_all
    return (
        pooled,
        penalty,
        input_grad,
        small_sums[0],
        small_sums[1],
        matrices[0],
        small_sums[2],
        small_sums[3],
        matrices[1],
        small_sums[4],
        small_sums[5],
        small_sums[6],
        matrices[2],
        small_sums[7],
        matrices[3],
        small_sums[8],
        small_sums[9],
        small_sums[10],
        small_sums[11],
        small_sums[12],
        small_sums[13],
        small_sums[14],
    )


def solution(mesh):
    in_specs = (
        P("clip", "seq", None),
        P("clip"),
        P("clip"),
        P(),
        P(),
        P(),
        P(),
        P(),
        P(),
        P(),
        P(),
        P(),
        P(),
        P(),
        P(),
        P(),
        P(),
        P(),
        P(),
        P(),
        P(),
        P(),
        P("clip", "seq", None, None),
    )
    out_specs = (
        P("clip", "seq", None, None),
        P(),
        P("clip", "seq", None),
        P(),
        P(),
        P("clip", "seq"),
        P(),
        P(),
        P("clip", "seq"),
        P(),
        P(),
        P(),
        P("clip", "seq"),
        P(),
        P("clip", "seq"),
        P(),
        P(),
        P(),
        P(),
        P(),
        P(),
        P(),
    )
    return jax.shard_map(shards, mesh=mesh, in_specs=in_specs, out_specs=out_specs, check_vma=False)
```

profile of v0, /device:TPU:0, one launch (start us, length us, event | category | flops | bytes accessed | tf_op | source)
XLA Modules:
  0.0 3146.7 jit_solution(5510250585292236608)
XLA Ops:
  65.2 99.1 %all-gather.5.cloned.1.call-done = bf16[2,3136,768]{2,1,0:T(8,128)(2,1)} async-done(((bf16[2,1568,768]{2,1,0:T(8,128)(2,1)}), bf16[2,3136,768]{2,1,0:T(8,128)(2,1)}) %all-gather.5.cloned.1.call-update) | async-done | bytes 9633808 | tf_op jit(solution)/shard_map/all_gather | solution.py:212
  187.0 97.1 %all-gather.3.cloned.1.call-done = bf16[2,3136,768]{2,1,0:T(8,128)(2,1)} async-done(((bf16[2,1568,768]{2,1,0:T(8,128)(2,1)}), bf16[2,3136,768]{2,1,0:T(8,128)(2,1)}) %all-gather.3.cloned.1.call-update) | async-done | bytes 9633808 | tf_op jit(solution)/shard_map/all_gather | solution.py:211
  310.3 678.8 %while.30 = (s32[]{:T(128)}, f32[12,2,1568]{2,1,0:T(2,128)}, f32[12,2,1568]{2,1,0:T(2,128)}, f32[12,2,1568,64]{2,3,1,0:T(8,128)}, bf16[12,2,1568,64]{2,3,1,0:T(8...) while((s32[]{:T(128)}, f32[12,2,1568]{2,1,0:T(2,128)}, ...), condition=%wide.region_5.6_spmd.clone, body=%wide.region_2.5_spmd.clone.sunk | while | flops 2616211200 | bytes 121938056 | solution.py:105
  311.3 20.4 select_reduce_fusion.2
  348.4 18.0 fusion.192
  367.9 20.4 select_reduce_fusion.2
  405.0 18.0 fusion.192
  424.4 20.4 select_reduce_fusion.2
  461.5 18.0 fusion.192
  481.0 20.4 select_reduce_fusion.2
  518.1 18.0 fusion.192
  537.5 20.4 select_reduce_fusion.2
  574.6 18.0 fusion.192
  594.1 20.4 select_reduce_fusion.2
  631.2 18.0 fusion.192
  650.6 20.4 select_reduce_fusion.2
  687.7 18.0 fusion.192
  707.1 20.4 select_reduce_fusion.2
  763.7 20.4 select_reduce_fusion.2
  820.3 20.4 select_reduce_fusion.2
  857.4 18.0 fusion.192
  876.8 20.4 select_reduce_fusion.2
  933.3 20.4 select_reduce_fusion.2
  1026.1 43.2 %fusion.88 = (u8[1568,3072]{1,0:T(8,128)(4,1)}, u8[1568,3072]{1,0:T(8,128)(4,1)}, f32[2,1568,3072]{2,1,0:T(8,128)}) fusion(f32[3072]{0:T(1024)} %param.40, bf16[768,3072]{1,0:T(8,128)(2,1)} %param.39, f32[2,1568,768]{2,1,0:T(8,128)} %copy-done.3, f32[768]{0:T(1024)} %param.38, f32[768]{0:T(1024)} %param.37, f32[2,1568]{1,0:T(2,128)} %fusion.136, ...), kind=kOutput, calls=%fused_computation.137 | convolution fusion | flops 14934786048 | bytes 62564864 | tf_op jit(solution)/shard_map/dot_general | solution.py:39
  1069.4 95.0 %multiply_convert_fusion.1 = (bf16[2,1568,3072]{2,1,0:T(8,128)(2,1)}, f32[2,1568,3072]{2,1,0:T(8,128)}) fusion(f32[2,1568,3072]{2,1,0:T(8,128)} %get-tuple-element.382, f32[3072]{0:T(1024)} %param.40, u8[1568,3072]{1,0:T(8,128)(4,1)} %get-tuple-element.269, u8[1568,3072]{1,0:T(8,128)(4,1)} %get-tuple-element.268), kind=kLoop, calls=%fused_computation.77 | loop fusion | flops 683999232 | bytes 105984000 | tf_op jit(solution)/shard_map/convert_element_type | solution.py:222
  1164.4 24.7 fusion.152
  1267.5 43.9 %convert_reduce_fusion = (f32[3072]{0:T(1024)}, bf16[2,1568,3072]{2,1,0:T(8,128)(2,1)}) fusion(f32[2,1568,3072]{2,1,0:T(8,128)} %get-tuple-element.361, bf16[2,1568,768]{2,1,0:T(8,128)(2,1)} %get-tuple-element.353, bf16[3072,768]{1,0:T(8,128)(2,1)} %param.41, f32[2,1568,3072]{2,1,0:T(8,128)} %get-tuple-element.382, f32[3072]{0:T(1024)S(1)} %copy-done.46), kind=kOutput, calls=%fused_computation.75 | convolution fusion | flops 14961275904 | bytes 105897984 | tf_op jit(solution)/shard_map/dot_general | solution.py:45
  1311.4 25.6 fusion.145
  1401.5 1007.2 %while.31 = (s32[]{:T(128)}, f32[12,2,1568,64]{2,3,1,0:T(8,128)}, bf16[12,2,3136,64]{2,3,1,0:T(8,128)(2,1)}, bf16[12,2,3136,64]{2,3,1,0:T(8,128)(2,1)}, bf16[12,...) while((s32[]{:T(128)}, f32[12,2,1568,64]{2,3,1,0:T(8,128)}, ...), condition=%wide.region_21.22_spmd.clone, body=%wide.region_20.21_spmd.clone.sunk | while | flops 6392441344 | bytes 188014736 | solution.py:145
  1403.5 19.9 fusion.205
  1423.6 23.1 multiply_convert_fusion.8
  1487.4 19.9 fusion.205
  1507.5 23.1 multiply_convert_fusion.8
  1571.3 19.9 fusion.205
  1591.4 23.1 multiply_convert_fusion.8
  1655.2 19.9 fusion.205
  1675.3 23.1 multiply_convert_fusion.8
  1739.1 19.9 fusion.205
  1759.1 23.1 multiply_convert_fusion.8
  1822.9 19.9 fusion.205
  1843.0 23.1 multiply_convert_fusion.8
  1906.8 19.9 fusion.205
  1926.8 23.1 multiply_convert_fusion.8
  1990.7 19.9 fusion.205
  2010.7 23.1 multiply_convert_fusion.8
  2074.6 19.9 fusion.205
  2094.6 23.1 multiply_convert_fusion.8
  2158.5 19.9 fusion.205
  2178.5 23.1 multiply_convert_fusion.8
  2242.4 19.9 fusion.205
  2262.5 23.1 multiply_convert_fusion.8
  2326.3 19.9 fusion.205
  2346.3 23.1 multiply_convert_fusion.8
  2465.1 22.6 bitcast_convert_fusion
  2487.8 27.2 bitcast_convert_fusion.1
  2543.5 114.9 %reduce-scatter.19.cloned.1.call-done = bf16[2,1568,768]{2,1,0:T(8,128)(2,1)} async-done(((bf16[2,3136,768]{2,1,0:T(8,128)(2,1)}), bf16[2,1568,768]{2,1,0:T(8,128)(2,1)}) %reduce-scatter.19.cloned.1.call-update) | async-done | bytes 4816912 | tf_op jit(solution)/shard_map/reduce_scatter | solution.py:307
  2658.3 21.1 bitcast_convert_fusion.2
  2679.5 40.3 %reduce-scatter.23.cloned.1.call-done = bf16[48,768]{1,0:T(8,128)(2,1)} async-done(((bf16[768,768]{1,0:T(8,128)(2,1)}), bf16[48,768]{1,0:T(8,128)(2,1)}) %reduce-scatter.23.cloned.1.call-update) | async-done | bytes 73744 | tf_op jit(solution)/shard_map/reduce_scatter | solution.py:326
  2721.8 76.4 %reduce-scatter.29.cloned.1.call-done = bf16[192,768]{1,0:T(8,128)(2,1)} async-done(((bf16[3072,768]{1,0:T(8,128)(2,1)}), bf16[192,768]{1,0:T(8,128)(2,1)}) %reduce-scatter.29.cloned.1.call-update) | async-done | bytes 294928 | tf_op jit(solution)/shard_map/reduce_scatter | solution.py:332
  2801.5 75.7 %reduce-scatter.25.cloned.1.call-done = bf16[48,3072]{1,0:T(8,128)(2,1)} async-done(((bf16[768,3072]{1,0:T(8,128)(2,1)}), bf16[48,3072]{1,0:T(8,128)(2,1)}) %reduce-scatter.25.cloned.1.call-update) | async-done | bytes 294928 | tf_op jit(solution)/shard_map/reduce_scatter | solution.py:329
  2883.7 65.1 %reduce-scatter.21.cloned.1.call-done = bf16[48,2304]{1,0:T(8,128)(2,1)} async-done(((bf16[768,2304]{1,0:T(8,128)(2,1)}), bf16[48,2304]{1,0:T(8,128)(2,1)}) %reduce-scatter.21.cloned.1.call-update) | async-done | bytes 221200 | tf_op jit(solution)/shard_map/reduce_scatter | solution.py:323
  2992.7 20.1 fusion.146
  3033.3 41.5 %all-reduce = (f32[]{:T(128)}, f32[768]{0:T(1024)}, f32[768]{0:T(1024)}, f32[768]{0:T(1024)}, f32[768]{0:T(1024)}, /*index=5*/f32[768]{0:T(1024)}, f32[768]{0:T(...) all-reduce(f32[]{:T(128)S(6)} %div.123, ...), channel_id=1, replica_groups=mesh['clip'=16,'seq'=2] {'clip','seq'}, use_global_device_ids=true, to_apply=%region_14.15 | all-reduce | flops 11337 | bytes 90696 | tf_op jit(solution)/shard_map/psum | solution.py:350
  3078.8 58.4 %all-reduce.3.cloned.1.call-done = f32[768,64]{0,1:T(8,128)} async-done(((f32[768,64]{0,1:T(8,128)}), f32[768,64]{0,1:T(8,128)}) %all-reduce.3.cloned.1.call-update) | async-done | bytes 196624 | tf_op jit(solution)/shard_map/psum | solution.py:350
  (482 shorter events, 1230.5 us)
Async XLA Ops:
  7.2 157.1 %all-gather.5.cloned.1.call-start = ((), (), s32[]{:S(2)}) async-start(), calls=%async_computation.11 | async-start | bytes 14450688 | tf_op jit(solution)/shard_map/all_gather | solution.py:212
  10.5 21.2 copy-start.18
  43.2 240.9 %all-gather.3.cloned.1.call-start = ((), (), s32[]{:S(2)}) async-start(), calls=%async_computation.10 | async-start | bytes 14450688 | tf_op jit(solution)/shard_map/all_gather | solution.py:211
  49.7 2493.8 %reduce-scatter.17.cloned.1.call-start = ((), (), s32[]{:S(2)}) async-start(), calls=%async_computation.12 | async-start | bytes 14450688 | tf_op jit(solution)/shard_map/reduce_scatter | solution.py:304
  1020.1 49.3 %copy-start.22 = (f32[2,1568]{1,0:T(2,128)}, f32[2,1568]{1,0:T(2,128)S(1)}, u32[]{:S(2)}) copy-start(f32[2,1568]{1,0:T(2,128)S(1)} %broadcast_multiply_fusion.2) | copy-start | bytes 37636
  1069.4 95.0 %copy-start.50 = (f32[768]{0:T(1024)S(1)}, f32[768]{0:T(1024)}, u32[]{:S(2)}) copy-start(f32[768]{0:T(1024)} %param.42) | copy-start | bytes 9220
  1189.1 44.9 %copy-start.14 = (f32[2,1568]{1,0:T(2,128)}, f32[2,1568]{1,0:T(2,128)S(1)}, u32[]{:S(2)}) copy-start(f32[2,1568]{1,0:T(2,128)S(1)} %broadcast_multiply_fusion.1) | copy-start | bytes 37636
  1267.5 43.9 %copy-start.23 = (f32[2,1568]{1,0:T(2,128)S(1)}, f32[2,1568]{1,0:T(2,128)}, u32[]{:S(2)}) copy-start(f32[2,1568]{1,0:T(2,128)} %copy-done.22) | copy-start | bytes 37636
  1403.5 20.1 copy-start.16
  1403.5 19.9 copy-start.9
  1403.5 19.9 copy-start.37
  1423.5 23.2 copy-start.17
  1487.4 20.1 copy-start.16
  1487.4 19.9 copy-start.9
  1487.4 19.9 copy-start.37
  1507.5 23.2 copy-start.17
  1571.3 20.1 copy-start.16
  1571.3 19.9 copy-start.9
  1591.4 23.2 copy-start.17
  1655.2 20.1 copy-start.16
  1655.2 19.9 copy-start.9
  1655.2 19.9 copy-start.37
  1675.3 23.2 copy-start.17
  1739.0 20.1 copy-start.16
  1739.0 19.9 copy-start.9
  1739.0 19.9 copy-start.37
  1759.1 23.2 copy-start.17
  1822.9 20.1 copy-start.16
  1822.9 19.9 copy-start.9
  1843.0 23.2 copy-start.17
  1906.8 20.1 copy-start.16
  1906.8 19.9 copy-start.9
  1906.8 19.9 copy-start.37
  1926.8 23.2 copy-start.17
  1990.6 20.1 copy-start.16
  1990.6 19.9 copy-start.9
  2010.7 23.2 copy-start.17
  2074.5 20.1 copy-start.16
  2074.5 19.9 copy-start.9
  2094.6 23.2 copy-start.17
  2158.4 20.1 copy-start.16
  2158.5 19.9 copy-start.9
  2178.5 23.2 copy-start.17
  2242.4 20.1 copy-start.16
  2242.4 19.9 copy-start.9
  2242.4 19.9 copy-start.37
  2262.4 23.2 copy-start.17
  2326.2 20.1 copy-start.16
  2326.2 19.9 copy-start.9
  2326.2 19.9 copy-start.37
  2346.3 23.2 copy-start.17
  2430.6 227.7 %reduce-scatter.19.cloned.1.call-start = ((), (), s32[]{:S(2)}) async-start(), calls=%async_computation.13 | async-start | bytes 14450688 | tf_op jit(solution)/shard_map/reduce_scatter | solution.py:307
  2453.1 266.7 %reduce-scatter.23.cloned.1.call-start = ((), (), s32[]{:S(2)}) async-start(), calls=%async_computation.15 | async-start | bytes 1253376 | tf_op jit(solution)/shard_map/reduce_scatter | solution.py:326
  2465.1 22.7 copy-start.24
  2465.1 333.1 %reduce-scatter.29.cloned.1.call-start = ((), (), s32[]{:S(2)}) async-start(), calls=%async_computation.18 | async-start | bytes 5013504 | tf_op jit(solution)/shard_map/reduce_scatter | solution.py:332
  2487.7 389.5 %reduce-scatter.25.cloned.1.call-start = ((), (), s32[]{:S(2)}) async-start(), calls=%async_computation.16 | async-start | bytes 5013504 | tf_op jit(solution)/shard_map/reduce_scatter | solution.py:329
  2515.0 433.7 %reduce-scatter.21.cloned.1.call-start = ((), (), s32[]{:S(2)}) async-start(), calls=%async_computation.14 | async-start | bytes 3760128 | tf_op jit(solution)/shard_map/reduce_scatter | solution.py:323
  2531.3 345.9 %copy-start.15 = (f32[2,1568]{1,0:T(2,128)S(1)}, f32[2,1568]{1,0:T(2,128)}, u32[]{:S(2)}) copy-start(f32[2,1568]{1,0:T(2,128)} %copy-done.14) | copy-start | bytes 37636
  2679.4 282.0 %reduce-scatter.33.cloned.1.call-start = ((), (), s32[]{:S(2)}) async-start(), calls=%async_computation.21 | async-start | bytes 294912
  2721.6 255.1 %reduce-scatter.35.cloned.1.call-start = ((), (), s32[]{:S(2)}) async-start(), calls=%async_computation.22 | async-start | bytes 589824
  2800.1 190.9 %reduce-scatter.27.cloned.1.call-start = ((), (), s32[]{:S(2)}) async-start(), calls=%async_computation.17 | async-start | bytes 442368 | tf_op jit(solution)/shard_map/reduce_scatter | solution.py:343
  2877.2 198.3 %reduce-scatter.31.cloned.1.call-start = ((), (), s32[]{:S(2)}) async-start(), calls=%async_computation.20 | async-start | bytes 884736
  2950.8 186.5 %all-reduce.3.cloned.1.call-start = ((), (), s32[]{:S(2)}) async-start(), calls=%async_computation.19 | async-start | bytes 393216 | tf_op jit(solution)/shard_map/psum | solution.py:350
  2992.7 21.0 copy-start.19
  (67 other events, 791.9 us)
Sparse Core Ops, SparseCore 0:
  43.3 120.9 all-gather.4
  165.9 118.2 all-gather.2
  2430.7 112.6 reduce-scatter.16
  2545.6 112.6 reduce-scatter.18
  2661.8 58.0 reduce-scatter.22
  2723.5 74.6 reduce-scatter.28
  2802.5 74.5 reduce-scatter.24
  2881.6 67.0 reduce-scatter.20
  2951.5 9.8 reduce-scatter.32
  2963.5 13.1 reduce-scatter.34
  2979.0 12.0 reduce-scatter.26
  2993.3 15.2 reduce-scatter.30
  3014.1 123.0 all-reduce.2
where the time goes:
time: 3160 us; the launch traced here: 3150 us
  matrix products  1740 us (55%)
  waiting for transfers between devices  667 us (21%)
  other arithmetic  450 us (14%)
  local copies, waits for them, and re-layouts  224 us (7%)
  blocking collectives  41.5 us (1%)
    dot_general x12, matrix products, grad_one_head(): jnp.einsum('crd,cpd->crp', grad_head, value_head, preferred_element_type=...  278 us
    dot_general x12, matrix products, attend_one_head(): jnp.einsum('crd,cpd->crp', query_head, key_head, preferred_element_type=j...  245 us
    dot_general x12, matrix products, grad_one_head(): jnp.einsum('crd,cpd->crp', query_head, key_head, preferred_element_type=j...  239 us
    reduce_sum x12, other arithmetic, attend_one_head(): totals = totals * shrink + jnp.sum(weights, axis=2)  216 us
    dot_general x12, matrix products, grad_one_head(): jnp.einsum('crp,crd->cpd', probs.astype(jnp.bfloat16), grad_head, preferr...  204 us
    dot_general x12, matrix products, attend_one_head(): jnp.einsum('crp,cpd->crd', weights.astype(jnp.bfloat16), value_head, pref...  200 us
    dot_general x12, matrix products, grad_one_head(): jnp.einsum('crp,cpd->crd', grad_score, key_head, preferred_element_type=j...  135 us
    dot_general x12, matrix products, grad_one_head(): jnp.einsum('crp,crd->cpd', grad_score, query_head, preferred_element_type...  130 us
  transfers between devices with their start and end apart: 13, of which 12 were waited for; matrix products, arithmetic and copies ran while one was open for 8% of the time, Pallas kernels for 0%

commit v1 on v0

v1 whole, which is shorter than its diff:
```python
import jax
import jax.numpy as jnp
from jax import lax
from jax.experimental import pallas as pl
from jax.experimental.pallas import tpu as pltpu
from jax.sharding import PartitionSpec as P

HEADS = 12
HEAD = 64
NTOK = 8
PATCH = 196
TILE = 256
LOG2E = 1.4426950408889634
LN2 = 0.6931471805599453
VMEM = 60 * 1024 * 1024

epsilon = 1e-06
masked_score = -1e30
bf16 = jnp.bfloat16
f32 = jnp.float32

NN = (((1,), (0,)), ((), ()))
NT = (((1,), (1,)), ((), ()))
TN = (((0,), (0,)), ((), ()))


def dot(left, right, dims=NN):
    return lax.dot_general(left, right, dims, preferred_element_type=f32)


def split3(value):
    hi = value.astype(bf16).astype(f32)
    mid = (value - hi).astype(bf16).astype(f32)
    return hi, mid, value - hi - mid


def attend_kernel(q, k, v, kaug, att, aq, qp, vt, acc):
    rows = q.shape[0]
    keys = k.shape[0]
    chunks = keys // TILE
    qt = q[...].T
    zero = jnp.zeros((HEAD, rows), bf16)
    ids = lax.broadcasted_iota(jnp.int32, (128, rows), 0)
    for j in range(2):
        part = qt[j * HEAD : (j + 1) * HEAD]
        qp[j, 0:HEAD] = part if j == 0 else zero
        qp[j, HEAD:128] = zero if j == 0 else part
        qp[j, 128:256] = jnp.where(ids == 3, 1.0, 0.0).astype(bf16)
    vt[...] = v[...].T
    ones = jnp.ones((16, TILE), bf16)

    def left(base):
        return jnp.concatenate([k[pl.ds(base, TILE), :], kaug[pl.ds(base, TILE), :]], axis=1)

    def values(j, base):
        return jnp.concatenate([vt[j * HEAD : (j + 1) * HEAD, pl.ds(base, TILE)], ones], axis=0)

    def fold(t, first):
        base = t * TILE if first else pl.multiple_of(t * TILE, TILE)
        for j in range(2):
            p = jnp.exp2(dot(left(base), qp[j])).astype(bf16)
            part = dot(values(j, base), p)
            if first:
                acc[j] = part
            else:
                acc[j] += part

    fold(0, True)

    @pl.loop(1, chunks)
    def _(t):
        fold(t, False)

    for j in range(2):
        total = acc[j, HEAD : HEAD + 1]
        fine = (total > 2.0**-60) & (total < 2.0**60)
        bad = jnp.max(jnp.where(fine, 0.0, 1.0)) > 0.5
        acc[j, HEAD + 8 : HEAD + 9] = jnp.zeros((1, rows), f32)

        @pl.when(bad)
        def _():
            def largest(t, best):
                s = dot(left(pl.multiple_of(t * TILE, TILE)), qp[j])
                return jnp.maximum(best, jnp.max(s, axis=0, keepdims=True))

            best = lax.fori_loop(0, chunks, largest, jnp.full((1, rows), -1e38, f32))
            acc[j] = jnp.zeros((HEAD + 16, rows), f32)

            @pl.loop(0, chunks)
            def _(t):
                base = pl.multiple_of(t * TILE, TILE)
                p = jnp.exp2(dot(left(base), qp[j]) - best).astype(bf16)
                acc[j] += dot(values(j, base), p)

            acc[j, HEAD + 8 : HEAD + 9] = best

    ids = lax.broadcasted_iota(jnp.int32, (HEAD, rows), 0)
    outs = []
    augs = []
    for j in range(2):
        total = acc[j, HEAD : HEAD + 1]
        outs.append(acc[j, 0:HEAD] * (1.0 / total))
        lse = jnp.log2(total) + acc[j, HEAD + 8 : HEAD + 9]
        hi, mid, low = split3(-lse)
        aug = jnp.where(ids == 0, hi, jnp.where(ids == 1, mid, jnp.where(ids == 2, low, 0.0)))
        augs.append(jnp.where(ids == 3, 1.0, aug))
    att[...] = jnp.concatenate(outs, axis=0).T.astype(bf16)
    aq[...] = jnp.concatenate(augs, axis=0).T.astype(bf16)


def attend(mixed, keys_values, kaug):
    rows = mixed.shape[0]
    keys = keys_values.shape[0]
    pairs = HEADS // 2
    first = keys_values.shape[1] // 128 - 2 * pairs
    return pl.pallas_call(
        attend_kernel,
        grid=(pairs,),
        in_specs=[
            pl.BlockSpec((rows, 128), lambda h: (0, h)),
            pl.BlockSpec((keys, 128), lambda h: (0, first + h)),
            pl.BlockSpec((keys, 128), lambda h: (0, first + pairs + h)),
            pl.BlockSpec((keys, 128), lambda h: (0, 0)),
        ],
        out_specs=[
            pl.BlockSpec((rows, 128), lambda h: (0, h)),
            pl.BlockSpec((rows, 128), lambda h: (0, h)),
        ],
        out_shape=[
            jax.ShapeDtypeStruct((rows, HEADS * HEAD), bf16),
            jax.ShapeDtypeStruct((rows, HEADS * HEAD), bf16),
        ],
        scratch_shapes=[
            pltpu.VMEM((2, 256, rows), bf16),
            pltpu.VMEM((128, keys), bf16),
            pltpu.VMEM((2, HEAD + 16, rows), f32),
        ],
        compiler_params=pltpu.CompilerParams(vmem_limit_bytes=VMEM),
        cost_estimate=pl.CostEstimate(
            flops=4 * HEADS * rows * keys * 256, transcendentals=HEADS * rows * keys, bytes_accessed=rows * 768 * 10
        ),
        name="attend",
    )(mixed, keys_values, keys_values, kaug)


def attend_back_kernel(q, do, att, aq, k, v, kaug_t, dq, dk, dv, kp, vp, dkt, dvt):
    step = pl.program_id(1)
    rows = q.shape[0]
    keys = k.shape[0]
    tiles = keys // TILE
    pad = HEAD - 16

    @pl.when(step == 0)
    def _():
        for source, held in ((k, kp), (v, vp)):
            flat = source[...].T
            zero = jnp.zeros((HEAD, keys), bf16)
            rest = jnp.zeros((pad, keys), bf16)
            for j in range(2):
                part = flat[j * HEAD : (j + 1) * HEAD]
                held[j, 0:HEAD] = part if j == 0 else zero
                held[j, HEAD:128] = zero if j == 0 else part
                aug = jnp.concatenate([kaug_t[...], rest], axis=0)
                held[j, 128 : 128 + HEAD] = aug if j == 0 else zero
                held[j, 128 + HEAD : 256] = zero if j == 0 else aug
        dkt[...] = jnp.zeros_like(dkt)
        dvt[...] = jnp.zeros_like(dvt)

    lane = lax.broadcasted_iota(jnp.int32, (rows, 128), 1)
    product = do[...].astype(f32) * att[...].astype(f32)
    inner0 = jnp.sum(jnp.where(lane < HEAD, product, 0.0), axis=1, keepdims=True)
    inner1 = jnp.sum(jnp.where(lane < HEAD, 0.0, product), axis=1, keepdims=True)
    hi, mid, low = split3(-jnp.where(lane < HEAD, inner0, inner1))
    within = lane % HEAD
    ado = jnp.where(within == 0, hi, jnp.where(within == 1, mid, jnp.where(within == 2, low, 0.0))).astype(bf16)
    qa = jnp.concatenate([q[...], aq[...]], axis=1)
    da = jnp.concatenate([do[...], ado], axis=1)
    qt = q[...].T
    dot_ = do[...].T
    units = [(j, t) for j in range(2) for t in range(tiles)]
    totals = [None, None]

    def scores(j, t):
        cols = slice(t * TILE, (t + 1) * TILE)
        return dot(qa, kp[j, :, cols]), dot(da, vp[j, :, cols])

    def weigh(s, dp):
        p = jnp.exp2(s)
        return p.astype(bf16), (p * dp).astype(bf16)

    def collect(j, t, p, ds):
        cols = slice(t * TILE, (t + 1) * TILE)
        part = slice(j * HEAD, (j + 1) * HEAD)
        dvt[part, cols] += dot(dot_[part], p)
        dkt[part, cols] += dot(qt[part], ds)
        more = dot(ds, k[cols, :])
        totals[j] = more if totals[j] is None else totals[j] + more

    raw = {}
    ready = {}
    count = len(units)
    for i in range(count + 2):
        if i < count:
            raw[i] = scores(*units[i])
        if 0 <= i - 1 < count:
            ready[i - 1] = weigh(*raw.pop(i - 1))
        if 0 <= i - 2 < count:
            collect(*units[i - 2], *ready.pop(i - 2))
    dq[...] = (jnp.where(lane < HEAD, totals[0], totals[1]) * HEAD ** (-0.5)).astype(bf16)

    @pl.when(step == pl.num_programs(1) - 1)
    def _():
        dk[...] = (dkt[...] * LN2).T.astype(bf16)
        dv[...] = dvt[...].T.astype(bf16)


def attend_back(mixed, keys_values, grad_att, att, aq, kaug_t):
    rows = mixed.shape[0]
    keys = keys_values.shape[0]
    pairs = HEADS // 2
    first = keys_values.shape[1] // 128 - 2 * pairs
    here = pl.BlockSpec((TILE, 128), lambda h, r: (r, h))
    whole = pl.BlockSpec((keys, 128), lambda h, r: (0, h))
    return pl.pallas_call(
        attend_back_kernel,
        grid=(pairs, rows // TILE),
        in_specs=[
            here,
            here,
            here,
            here,
            pl.BlockSpec((keys, 128), lambda h, r: (0, first + h)),
            pl.BlockSpec((keys, 128), lambda h, r: (0, first + pairs + h)),
            pl.BlockSpec((16, keys), lambda h, r: (0, 0)),
        ],
        out_specs=[here, whole, whole],
        out_shape=[
            jax.ShapeDtypeStruct((rows, HEADS * HEAD), bf16),
            jax.ShapeDtypeStruct((keys, HEADS * HEAD), bf16),
            jax.ShapeDtypeStruct((keys, HEADS * HEAD), bf16),
        ],
        scratch_shapes=[
            pltpu.VMEM((2, 256, keys), bf16),
            pltpu.VMEM((2, 256, keys), bf16),
            pltpu.VMEM((128, keys), f32),
            pltpu.VMEM((128, keys), f32),
        ],
        compiler_params=pltpu.CompilerParams(vmem_limit_bytes=VMEM),
        cost_estimate=pl.CostEstimate(
            flops=10 * HEADS * rows * keys * 200, transcendentals=HEADS * rows * keys, bytes_accessed=rows * 768 * 20
        ),
        name="attend_back",
    )(mixed, grad_att, att, aq, keys_values, keys_values, kaug_t)


def normed(value, gain, bias):
    average = jnp.mean(value, axis=-1, keepdims=True)
    centered = value - average
    variance = jnp.mean(centered * centered, axis=-1, keepdims=True)
    return centered * lax.rsqrt(variance + epsilon) * gain + bias


def norm_back(value, gain, bias, grad):
    result, pullback = jax.vjp(normed, value, gain, bias)
    return pullback(grad)


def gelu_exact(value):
    return jax.nn.gelu(value, approximate=False)


def gelu_back(value, grad):
    result, pullback = jax.vjp(gelu_exact, value)
    return pullback(grad)[0]


def column_sums(grad):
    return jnp.sum(grad.astype(f32), axis=0)


def shards(
    inputs,
    frame_tokens,
    clip_frames,
    norm1_gain,
    norm1_bias,
    qkv_weight,
    query_bias,
    value_bias,
    out_weight,
    out_bias,
    norm2_gain,
    norm2_bias,
    fc1_weight,
    fc1_bias,
    fc2_weight,
    fc2_bias,
    learn_gain,
    learn_bias,
    map1_weight,
    map1_bias,
    map2_weight,
    map2_bias,
    cot_pooled,
):
    clip_count, piece, width = inputs.shape
    seq_size = lax.axis_size("seq")
    position = lax.axis_index("seq")
    clip_size = lax.axis_size("clip")
    frames_here = piece // PATCH
    scaling = HEAD ** (-0.5)
    slots_all = float(clip_count * clip_size * seq_size * frames_here)
    group = seq_size // clip_count
    mine = position // group
    seat = position % group

    def route(turn):
        return [
            (s, ((s % clip_count + turn) % clip_count) * group + s // clip_count) for s in range(seq_size)
        ]

    def send(value, turn, back=False):
        pairs = route(turn)
        if back:
            pairs = [(b, a) for a, b in pairs]
        if all(a == b for a, b in pairs):
            return value
        return lax.ppermute(value, "seq", pairs)

    def scatter(whole):
        return [
            send(lax.dynamic_index_in_dim(whole, (position + turn) % clip_count, 0, False), turn)
            for turn in range(clip_count)
        ]

    def gather_back(pieces):
        home = [send(part, turn, True) for turn, part in enumerate(pieces)]
        stacked = jnp.stack(home)
        order = (jnp.arange(clip_count) - position) % clip_count
        return stacked[order]

    tokens = lax.dynamic_index_in_dim(frame_tokens, mine, 0, False)
    frames = lax.dynamic_index_in_dim(clip_frames, mine, 0, False)
    rows = clip_count * piece
    padded = -(-rows // TILE) * TILE
    gap = padded - rows

    x_low = jnp.concatenate(scatter(inputs) + [jnp.zeros((gap, width), bf16)], axis=0)
    cot = jnp.concatenate(scatter(cot_pooled), axis=0).reshape(clip_count * frames_here * NTOK, width)

    def placed(ids, at_seat):
        turn = ids // piece
        source = clip_count * at_seat + (mine - turn) % clip_count
        local = ids - turn * piece
        frame = local // PATCH
        slot = local - frame * PATCH
        inside = (source * frames_here + frame < frames) & (slot < tokens) & (ids < rows)
        return inside, jnp.where(ids < rows, turn * frames_here + frame, -1)

    row_ids = jnp.arange(padded, dtype=jnp.int32)
    inside, frame_ids = placed(row_ids, seat)
    valid = inside.astype(f32)[:, None]
    key_ids = jnp.arange(group * padded, dtype=jnp.int32)
    key_inside, _ = placed(key_ids % padded, key_ids // padded)
    lane16 = jnp.arange(HEAD)
    key_mask = jnp.where(key_inside, 0.0, masked_score)
    kaug = jnp.where(lane16[None, :] < 3, 1.0, jnp.where(lane16[None, :] == 3, key_mask[:, None], 0.0)).astype(bf16)
    kaug = jnp.concatenate([kaug, jnp.zeros_like(kaug)], axis=1)
    sub16 = jnp.arange(16)[:, None]
    kaug_t = jnp.where(sub16 < 3, 1.0, jnp.where(sub16 == 3, key_mask[None, :], 0.0)).astype(bf16)

    state = x_low.astype(f32)
    act1 = normed(state, norm1_gain, norm1_bias).astype(bf16)
    zeros = jnp.zeros((width,), f32)
    ones = jnp.ones((width,), f32)
    col_scale = jnp.concatenate([ones * (scaling * LOG2E), ones, ones])
    col_bias = jnp.concatenate([query_bias * (scaling * LOG2E), zeros, value_bias])
    mixed = (dot(act1, qkv_weight) * col_scale + col_bias).astype(bf16)
    if group == 1:
        keys_values = mixed
    else:
        both = lax.all_gather(mixed[:, width:], "seq", axis=0, tiled=True)
        keys_values = lax.dynamic_slice_in_dim(both, mine * (group * padded), group * padded, 0)
    att, aq = attend(mixed, keys_values, kaug)

    resid1 = state + dot(att, out_weight) + out_bias
    act2 = normed(resid1, norm2_gain, norm2_bias).astype(bf16)
    hidden_pre = dot(act2, fc1_weight) + fc1_bias
    hidden = gelu_exact(hidden_pre).astype(bf16)
    resid2 = resid1 + dot(hidden, fc2_weight) + fc2_bias
    act3 = normed(resid2, learn_gain, learn_bias).astype(bf16)
    map_pre = dot(act3, map1_weight) + map1_bias
    map_hidden = gelu_exact(map_pre).astype(bf16)
    logits = dot(map_hidden, map2_weight) + map2_bias
    sigmoid_raw = jax.nn.sigmoid(logits)
    gates = sigmoid_raw * valid
    inverse = lax.rsqrt(tokens.astype(f32))
    slots = clip_count * frames_here * NTOK
    spread = (frame_ids[:, None] == jnp.arange(slots, dtype=jnp.int32)[None, :] // NTOK).astype(f32)
    gates_low = gates.astype(bf16)
    gates_wide = (jnp.tile(gates_low.astype(f32), (1, slots // NTOK)) * spread).astype(bf16)
    output_low = resid2.astype(bf16)
    pooled = (dot(gates_wide, output_low, TN) * inverse).astype(bf16)
    pooled = pooled.reshape(clip_count, frames_here, NTOK, width)
    pooled = gather_back([pooled[t] for t in range(clip_count)])
    gate_sum = jnp.sum(gates, axis=-1, keepdims=True)
    gate_square = jnp.sum(gates * gates, axis=-1)
    pair_count = NTOK * (NTOK - 1)
    intersection = jnp.sum(gate_sum[:, 0] * gate_sum[:, 0] - gate_square) * inverse * inverse / pair_count
    grad_out = dot(gates_wide, cot) * inverse
    grad_wide = dot(output_low, cot, NT) * spread
    grad_gate = jnp.sum(grad_wide.reshape(padded, slots // NTOK, NTOK), axis=1) * inverse
    penalty_factor = 2.0 / pair_count * (inverse * inverse) / slots_all
    grad_gate = (grad_gate + penalty_factor * (gate_sum - gates)) * valid
    grad_logit = (grad_gate * sigmoid_raw * (1.0 - sigmoid_raw)).astype(bf16)
    map2_grad = dot(map_hidden, grad_logit, TN)
    map2_bias_grad = column_sums(grad_logit)
    grad_mpre = gelu_back(map_pre, dot(grad_logit, map2_weight, NT)).astype(bf16)
    map1_grad = dot(act3, grad_mpre, TN)
    map1_bias_grad = column_sums(grad_mpre)
    grad_res2, learn_gain_grad, learn_bias_grad = norm_back(
        resid2, learn_gain, learn_bias, dot(grad_mpre, map1_weight, NT)
    )
    grad_res2 = grad_res2 + grad_out
    branch_two = grad_res2.astype(bf16)

    def reduce_matrix(matrix):
        matrix = lax.psum_scatter(matrix.astype(bf16), "clip", scatter_dimension=0, tiled=True)
        return lax.psum_scatter(matrix, "seq", scatter_dimension=1, tiled=True).astype(f32)

    fc2_grad = reduce_matrix(dot(hidden, branch_two, TN))
    fc2_bias_grad = column_sums(branch_two)
    grad_pre = gelu_back(hidden_pre, dot(branch_two, fc2_weight, NT)).astype(bf16)
    fc1_grad = reduce_matrix(dot(act2, grad_pre, TN))
    fc1_bias_grad = column_sums(grad_pre)
    grad_res1, norm2_gain_grad, norm2_bias_grad = norm_back(
        resid1, norm2_gain, norm2_bias, dot(grad_pre, fc1_weight, NT)
    )
    grad_res1 = grad_res1 + grad_res2
    branch_one = grad_res1.astype(bf16)
    out_grad = reduce_matrix(dot(att, branch_one, TN))
    out_bias_grad = column_sums(branch_one)
    grad_att = dot(branch_one, out_weight, NT).astype(bf16)

    def flat_sum(parts):
        sizes = [part.size for part in parts]
        flat = jnp.concatenate([part.reshape(-1) for part in parts])
        total = lax.psum(flat, ("clip", "seq"))
        outs = []
        at = 0
        for part, size in zip(parts, sizes):
            outs.append(total[at : at + size].reshape(part.shape))
            at += size
        return outs

    early = flat_sum(
        [
            out_bias_grad,
            norm2_gain_grad,
            norm2_bias_grad,
            fc1_bias_grad,
            fc2_bias_grad,
            learn_gain_grad,
            learn_bias_grad,
            map1_grad,
            map1_bias_grad,
            map2_grad,
            map2_bias_grad,
            intersection.reshape(1),
        ]
    )

    grad_q, grad_k, grad_v = attend_back(mixed, keys_values, grad_att, att, aq, kaug_t)
    if group > 1:
        both = jnp.zeros((seq_size * padded, 2 * width), bf16)
        both = lax.dynamic_update_slice_in_dim(
            both, jnp.concatenate([grad_k, grad_v], axis=1), mine * (group * padded), 0
        )
        both = lax.psum_scatter(both, "seq", scatter_dimension=0, tiled=True)
        grad_k, grad_v = both[:, :width], both[:, width:]
    grad_mixed = jnp.concatenate([grad_q, grad_k, grad_v], axis=1)
    qkv_grad = reduce_matrix(dot(act1, grad_mixed, TN))
    query_bias_grad = column_sums(grad_q)
    value_bias_grad = column_sums(grad_v)
    grad_in, norm1_gain_grad, norm1_bias_grad = norm_back(
        state, norm1_gain, norm1_bias, dot(grad_mixed, qkv_weight, NT)
    )
    input_grad = (grad_in + grad_res1)[:rows].reshape(clip_count, piece, width).astype(bf16)
    input_grad = gather_back([input_grad[t] for t in range(clip_count)]).astype(f32)
    late = flat_sum([norm1_gain_grad, norm1_bias_grad, query_bias_grad, value_bias_grad])
    penalty = early[11].reshape(()) / slots_all
    return (
        pooled,
        penalty,
        input_grad,
        late[0],
        late[1],
        qkv_grad,
        late[2],
        late[3],
        out_grad,
        early[0],
        early[1],
        early[2],
        fc1_grad,
        early[3],
        fc2_grad,
        early[4],
        early[5],
        early[6],
        early[7],
        early[8],
        early[9],
        early[10],
    )


def solution(mesh):
    row_spec = P("clip", "seq", None)
    pool_spec = P("clip", "seq", None, None)
    matrix_spec = P("clip", "seq")
    in_specs = (row_spec, P("clip"), P("clip")) + (P(),) * 19 + (pool_spec,)
    out_specs = (
        (pool_spec, P(), row_spec, P(), P(), matrix_spec, P(), P(), matrix_spec, P(), P(), P(), matrix_spec, P())
        + (matrix_spec,)
        + (P(),) * 7
    )
    return jax.shard_map(shards, mesh=mesh, in_specs=in_specs, out_specs=out_specs, check_vma=False)
```

time: 3160 us -> 1200 us (0.38)
  matrix products: 1740 us -> 388 us
  waiting for transfers between devices: 667 us -> 48.2 us
  Pallas kernels: 0 us -> 455 us
  other arithmetic: 450 us -> 113 us
  local copies, waits for them, and re-layouts: 224 us -> 89.4 us
  blocking collectives: 41.5 us -> 79.1 us
    dot_general x105 -> x21, matrix products: 1740 us -> 388 us  [dot(): return lax.dot_general(left, right, dims, preferred_element_type=f32)]
    pallas_call x0 -> x2, Pallas kernels: none -> 455 us  [the longest x1 318 us: attend_back(): pl.pallas_call(attend_back_kernel, grid=(pairs, rows // TILE), in_specs=[...]
    reduce_scatter x7 -> x5, waiting for transfers between devices: 396 us -> 0.04 us  [the longest x4 0.04 us: reduce_matrix(): lax.psum_scatter(matrix.astype(bf16), 'clip', scatter_dimension=0, tiled=...]
    reduce_sum x19 -> x5, other arithmetic: 251 us -> 15.1 us  [the longest x4 13.8 us: column_sums(): return jnp.sum(grad.astype(f32), axis=0)]
    all_gather x2 -> x0, waiting for transfers between devices: 196 us -> none  [the longest x1 99.1 us: shards(): lax.all_gather(value_rows, 'seq', axis=1, tiled=True)]
    convert_element_type x8 -> x9, other arithmetic: 117 us -> 19.8 us  [the longest x1 6.96 us: shards(): gather_back([input_grad[t] for t in range(clip_count)]).astype(f32)]
    convert_element_type x8 -> x0, local copies, waits for them, and re-layouts: 70.1 us -> none  [the longest x2 22.4 us: shards(): value_all.astype(jnp.bfloat16)]
    psum x1, waiting for transfers between devices: 58.4 us -> 8.48 us  [flat_sum(): total = lax.psum(flat, ('clip', 'seq'))]
  transfers between devices with their start and end apart: 13 -> 13, of which waited for: 12 -> 2; matrix products, arithmetic and copies ran while one was open for 8% -> 22% of each run, Pallas kernels for 0% -> 27%
where the time goes in v1:
time: 1200 us
  Pallas kernels  455 us (38%)
  matrix products  388 us (32%)
  other arithmetic  113 us (9%)
  local copies, waits for them, and re-layouts  89.4 us (7%)
  blocking collectives  79.1 us (7%)
  waiting for transfers between devices  48.2 us (4%)
  between operations  19.9 us (2%)
    dot_general x21, matrix products, dot(): return lax.dot_general(left, right, dims, preferred_element_type=f32)  388 us
    pallas_call x1, Pallas kernels, attend_back(): pl.pallas_call(attend_back_kernel, grid=(pairs, rows // TILE), in_specs=[...  318 us
    pallas_call x1, Pallas kernels, attend(): pl.pallas_call(attend_kernel, grid=(pairs,), in_specs=[pl.BlockSpec((rows...  136 us
    psum x1, blocking collectives, flat_sum(): total = lax.psum(flat, ('clip', 'seq'))  79.1 us
    ppermute x4, waiting for transfers between devices, send(): return lax.ppermute(value, 'seq', pairs)  39.5 us
    unnamed x148, local copies, waits for them, and re-layouts  27.7 us
  transfers between devices with their start and end apart: 13, of which 2 were waited for; matrix products, arithmetic and copies ran while one was open for 22% of the time, Pallas kernels for 27%

profile of v1, /device:TPU:0, one launch (start us, length us, event | category | flops | bytes accessed | tf_op | source)
XLA Modules:
  0.0 1198.1 jit_solution(17815371473087643288)
XLA Ops:
  8.1 1.7 constant_dynamic-slice_fusion.1
  10.6 3.0 collective-permute-start.2
  13.5 4.9 dynamic-slice_bitcast_fusion.1
  27.6 1.9 fusion.72
  31.4 1.6 pad_maximum_fusion.2
  33.0 39.5 %collective-permute-done = bf16[1568,768]{1,0:T(8,128)(2,1)} collective-permute-done((bf16[1568,768]{1,0:T(8,128)(2,1)}, bf16[1568,768]{1,0:T(8,128)(2,1)}, u32[]{:S(2)}, u32[]{:S(2)}) %collective-permute-start) | collective-permute-done | bytes 2408480 | tf_op jit(solution)/shard_map/ppermute | solution.py:328
  72.5 3.6 convert_reduce_fusion.1
  76.1 7.1 fusion.15
  84.5 19.7 %add_convert_fusion.1.q.k.v = bf16[3328,2304]{1,0:T(8,128)(2,1)} fusion(bf16[768,2304]{1,0:T(8,128)(2,1)S(1)} %copy-done, f32[2304]{0:T(1024)S(1)} %pad_maximum_fusion.3, f32[2304]{0:T(1024)S(1)} %copy-done.64, f32[768]{0:T(1024)S(1)} %copy-done.56, f32[768]{0:T(1024)S(1)} %copy-done.41, f32[3328]{0:T(1024)S(1)} %fusion.73, ...), kind=kOutput, calls=%fused_computation.21 | convolution fusion | flops 11828723712 | bytes 23749120 | tf_op jit(solution)/shard_map/dot_general | solution.py:28
  104.2 136.4 %attend.1 = (bf16[3328,768]{1,0:T(8,128)(2,1)}, bf16[3328,768]{1,0:T(8,128)(2,1)}) custom-call(bf16[3328,2304]{1,0:T(8,128)(2,1)} %add_convert_fusion.1.q.k.v, bf16[3328,2304]{1,0:T(8,128)(2,1)} %add_convert_fusion.1.q.k.v, bf16[3328,2304]{1,0:T(8,128)(2,1)} %add_convert_fusion.1.q.k.v, bf16[3328,128]{1,0:T(8,128)(2,1)} %concatenate.23.kaug), custom_call_target="tpu_custom_call" | custom-call | flops 136096776192 | bytes 25559040 | tf_op jit(solution)/shard_map/attend/pallas_call | solution.py:116
  240.6 9.6 fusion.94
  252.2 109.9 %multiply_convert_fusion = (bf16[3328,3072]{1,0:T(8,128)(2,1)}, f32[3328,3072]{1,0:T(8,128)}, f32[3328,3072]{1,0:T(8,128)}) fusion(f32[3072]{0:T(1024)S(1)} %copy-done.53, bf16[768,3072]{1,0:T(8,128)(2,1)} %param.35, f32[3328,768]{1,0:T(8,128)S(1)} %get-tuple-element.121, f32[768]{0:T(1024)S(1)} %copy-done.58, f32[768]{0:T(1024)S(1)} %copy-done.48, ...), kind=kOutput, calls=%fused_computation.7 | convolution fusion | flops 16391012352 | bytes 117223424 | tf_op jit(solution)/shard_map/dot_general | solution.py:28
  362.2 22.4 %fusion.95 = (f32[3328]{0:T(1024)S(1)}, f32[3328,768]{1,0:T(8,128)S(1)}) fusion(f32[768]{0:T(1024)S(1)} %copy-done.55, f32[3328,768]{1,0:T(8,128)} %copy-done.7, bf16[3328,3072]{1,0:T(8,128)(2,1)} %get-tuple-element.97, bf16[3072,768]{1,0:T(8,128)(2,1)S(1)} %copy-done.52), kind=kOutput, calls=%fused_computation.219 | convolution fusion | flops 15711138816 | bytes 45629440 | tf_op jit(solution)/shard_map/dot_general | solution.py:28
  386.0 1.8 fusion.36
  387.9 2.6 add_convert_fusion.3
  390.5 4.4 multiply_convert_fusion.1
  399.1 7.2 multiply_reduce_fusion
  406.4 9.2 fusion.89
  415.6 7.6 fusion.18
  423.2 45.8 %convert_reduce_fusion = (f32[3072]{0:T(1024)}, bf16[3328,3072]{1,0:T(8,128)(2,1)}) fusion(f32[3328,3072]{1,0:T(8,128)} %get-tuple-element.98, bf16[3072,768]{1,0:T(8,128)(2,1)} %param.37, f32[3328,768]{1,0:T(8,128)} %fusion.18, f32[3328,3072]{1,0:T(8,128)} %get-tuple-element.122, f32[3072]{0:T(1024)} %param.36), kind=kOutput, calls=%fused_computation.5 | convolution fusion | flops 15879828480 | bytes 117202944 | tf_op jit(solution)/shard_map/dot_general | solution.py:28
  468.9 30.4 %multiply_reduce_fusion.1 = (f32[768]{0:T(1024)}, f32[3328]{0:T(1024)S(1)}, f32[768]{0:T(1024)}, f32[3328,768]{1,0:T(8,128)}) fusion(f32[3328,768]{1,0:T(8,128)} %copy-done.7, f32[3328]{0:T(1024)} %copy-done.36, f32[3328]{0:T(1024)S(1)} %copy-done.30, f32[768]{0:T(1024)} %param.33, bf16[3328,3072]{1,0:T(8,128)(2,1)} %get-tuple-element.130, ...), kind=kOutput, calls=%fused_computation.47 | convolution fusion | flops 15723916288 | bytes 45662208 | tf_op jit(solution)/shard_map/dot_general | solution.py:28
  499.4 9.5 fusion.88
  508.9 9.1 convert_reduce_fusion.5
  518.0 2.3 copy-done.9
  520.3 7.8 convolution_convert_fusion.4
  528.1 9.2 convolution_convert_fusion.do
  537.4 318.4 %attend_back.1 = (bf16[3328,768]{1,0:T(8,128)(2,1)}, bf16[3328,768]{1,0:T(8,128)(2,1)}, bf16[3328,768]{1,0:T(8,128)(2,1)}) custom-call(bf16[3328,2304]{1,0:T(8,128)(2,1)} %add_convert_fusion.1.q.k.v, bf16[3328,768]{1,0:T(8,128)(2,1)} %convolution_convert_fusion.do, bf16[3328,768]{1,0:T(8,128)(2,1)} %get-tuple-element.27.att, ...), custom_call_target="tpu_custom_call" | custom-call | flops 265814016000 | bytes 51118080 | tf_op jit(solution)/shard_map/attend_back/pallas_call | solution.py:224
  855.9 5.5 constant_dynamic-update-slice_fusion.2
  861.5 2.9 constant_dynamic-update-slice_fusion.1
  864.4 2.7 constant_dynamic-update-slice_fusion
  867.1 21.5 %convolution_convert_fusion.3 = bf16[768,2304]{1,0:T(8,128)(2,1)} fusion(bf16[3328,2304]{1,0:T(8,128)(2,1)} %constant_dynamic-update-slice_fusion, f32[768]{0:T(1024)S(1)} %copy-done.57, f32[768]{0:T(1024)S(1)} %copy-done.42, f32[3328]{0:T(1024)S(1)} %copy-done.25, f32[3328]{0:T(1024)S(1)} %copy-done.16, bf16[1568,768]{1,0:T(8,128)(2,1)} %collective-permute-done, ...), kind=kOutput, calls=%fused_computation.61 | convolution fusion | flops 11807490048 | bytes 23730688 | tf_op jit(solution)/shard_map/dot_general | solution.py:28
  890.7 2.2 fusion.97
  894.3 24.6 %convolution_convert_fusion.1 = bf16[3072,768]{1,0:T(8,128)(2,1)} fusion(bf16[3328,3072]{1,0:T(8,128)(2,1)} %get-tuple-element.97, f32[3328,768]{1,0:T(8,128)} %fusion.18), kind=kOutput, calls=%fused_computation.59 | convolution fusion | flops 15708389376 | bytes 35389440 | tf_op jit(solution)/shard_map/dot_general | solution.py:28
  919.0 4.9 fusion.96
  924.0 1.8 reshape.496
  925.8 24.7 %fusion.16 = (f32[3328]{0:T(1024)S(1)}, f32[3328,768]{1,0:T(8,128)}) fusion(f32[768]{0:T(1024)} %param.26, f32[3328]{0:T(1024)S(1)} %copy-done.16, bf16[3328]{0:T(1024)(128)(2,1)} %copy-done.21, bf16[1568,768]{1,0:T(8,128)(2,1)} %collective-permute-done, bf16[1568,768]{1,0:T(8,128)(2,1)} %get-tuple-element.103, ...), kind=kOutput, calls=%fused_computation.38 | convolution fusion | flops 11803161600 | bytes 33951232 | tf_op jit(solution)/shard_map/dot_general | solution.py:28
  950.5 12.3 %fusion.14 = (f32[768]{0:T(1024)}, f32[3328]{0:T(1024)S(1)}, f32[768]{0:T(1024)}) fusion(f32[3328,768]{1,0:T(8,128)} %get-tuple-element.132, f32[3328]{0:T(1024)S(1)} %copy-done.26, f32[3328]{0:T(1024)S(1)} %copy-done.16, bf16[3328]{0:T(1024)(128)(2,1)S(1)} %copy-done.23, bf16[1568,768]{1,0:T(8,128)(2,1)} %collective-permute-done, ...), kind=kLoop, calls=%fused_computation.36 | loop fusion | flops 43445504 | bytes 15109632 | tf_op jit(solution)/shard_map/transpose(jvp())/reduce_sum | solution.py:260
  962.9 18.3 %add_convert_fusion.2 = (bf16[3328,768]{1,0:T(8,128)(2,1)}, f32[768]{0:T(1024)}) fusion(f32[3328]{0:T(1024)S(1)} %negate_multiply_fusion.2, f32[3328,768]{1,0:T(8,128)} %fusion.18, f32[3328,768]{1,0:T(8,128)} %copy-done.2, f32[3328]{0:T(1024)S(1)} %copy-done.28, f32[3328]{0:T(1024)S(1)} %multiply_multiply_fusion.10, f32[3328]{0:T(1024)S(1)} %copy-done.16, ...), kind=kLoop, calls=%fused_computation.44 | loop fusion | flops 51117312 | bytes 40678912 | tf_op jit(solution)/shard_map/convert
  981.2 16.7 %concatenate.25 = f32[57417]{0:T(1024)} concatenate(f32[768]{0:T(1024)} %get-tuple-element.89, f32[768]{0:T(1024)} %get-tuple-element.78, f32[768]{0:T(1024)} %get-tuple-element.84, f32[3072]{0:T(1024)} %get-tuple-element.129, f32[768]{0:T(1024)} %get-tuple-element.100, f32[768]{0:T(1024)} %get-tuple-element.76, f32[768]{0:T(1024)} %get-tuple-element.83, f32[49152]{0:T(1024)} %reshape.496, ...), dimensions={0} | concatenate | bytes 459336 | tf_op jit(solution)/shard_map/concatenate | solution.py:447
  998.0 1.7 copy.79
  999.8 27.1 %convolution_convert_fusion.2 = bf16[768,3072]{1,0:T(8,128)(2,1)} fusion(bf16[3328,3072]{1,0:T(8,128)(2,1)} %get-tuple-element.130, f32[3328,768]{1,0:T(8,128)} %copy-done.7, f32[768]{0:T(1024)} %param.34, f32[768]{0:T(1024)} %param.33, f32[3328]{0:T(1024)} %copy-done.36, f32[3328]{0:T(1024)} %copy-done.29), kind=kOutput, calls=%fused_computation.60 | convolution fusion | flops 15718612992 | bytes 35422208 | tf_op jit(solution)/shard_map/dot_general | solution.py:28
  1027.0 5.1 slice_bitcast_fusion
  1033.0 5.0 fusion.42
  1038.8 1.6 collective-permute-start.1
  1041.2 2.0 copy.77
  1043.3 3.2 convert_reduce_fusion.2
  1047.2 79.1 %psum.15 = f32[3072]{0:T(1024)S(1)} all-reduce(f32[3072]{0:T(1024)} %pad_maximum_fusion.4), channel_id=1, replica_groups=mesh['clip'=16,'seq'=2] {'clip','seq'}, use_global_device_ids=true, to_apply=%region_30.31 | all-reduce | flops 3072 | bytes 24576 | tf_op jit(solution)/shard_map/psum | solution.py:448
  1126.3 1.9 copy.81
  1128.9 1.6 pad_maximum_fusion.1
  1130.5 2.3 gather_fusion
  1132.8 8.5 all-reduce.3.cloned.1.call-done
  1144.2 1.6 slice.116
  1145.8 1.8 reshape.499
  1147.6 1.8 copy.71
  1159.6 3.6 fusion.24
  1163.1 3.0 pad_maximum_fusion
  1166.2 4.2 gather_fusion.1
  1170.3 3.7 gather_fusion.2
  1174.0 7.0 maximum_convert_fusion
  1181.0 1.8 copy.78
  1182.7 1.6 convert_element_type.160
  1184.3 1.7 copy.82
  1186.1 1.6 convert_element_type.166
  1187.7 1.6 convert_element_type.164
  (223 shorter events, 39.2 us)
Async XLA Ops:
  8.0 76.4 %copy-start = (bf16[768,2304]{1,0:T(8,128)(2,1)S(1)}, bf16[768,2304]{1,0:T(8,128)(2,1)}, u32[]{:S(2)}) copy-start(bf16[768,2304]{1,0:T(8,128)(2,1)} %param.28) | copy-start | bytes 10616836
  8.0 10.9 copy-start.60
  8.1 11.5 copy-start.61
  8.1 18.8 %copy-start.50 = (f32[768]{0:T(1024)S(1)}, f32[768]{0:T(1024)}, u32[]{:S(2)}) copy-start(f32[768]{0:T(1024)} %param.29) | copy-start | bytes 9220
  8.1 990.0 %reduce-scatter.17.cloned.1.call-start = ((), (), s32[]{:S(2)}) async-start(), calls=%async_computation.10 | async-start | bytes 1253376 | tf_op jit(solution)/shard_map/reduce_scatter | solution.py:428
  10.6 73.9 %copy-start.41 = (f32[768]{0:T(1024)S(1)}, f32[768]{0:T(1024)}, u32[]{:S(2)}) copy-start(f32[768]{0:T(1024)} %param.26) | copy-start | bytes 9220
  10.6 20.8 %collective-permute-start.2 = (bf16[8,8,768]{2,0,1:T(8,128)(2,1)}, bf16[8,8,768]{2,0,1:T(8,128)(2,1)}, u32[]{:S(2)}, u32[]{:S(2)}) collective-permute-start(bf16[8,8,768]{2,0,1:T(8,128)(2,1)} %bitcast.74), channel_id=1, source_target_pairs={{0,1},{1,0},{2,3},{3,2},{4,5},{5,4},{6,7},{7,6},{8,9},{9,8},{10,11... | collective-permute-start | bytes 294920 | tf_op jit(solution)/shard_map/ppermute | solution.py:328
  18.5 54.1 %collective-permute-start = (bf16[1568,768]{1,0:T(8,128)(2,1)}, bf16[1568,768]{1,0:T(8,128)(2,1)}, u32[]{:S(2)}, u32[]{:S(2)}) collective-permute-start(bf16[1568,768]{1,0:T(8,128)(2,1)} %get-tuple-element.104), channel_id=1, source_target_pairs={{0,1},{1,0},{2,3},{3,2},{4,5},{5,4},{6,7},{7,6},{8,9},{9,8},{10,11... | collective-permute-start | bytes 7225352 | tf_op jit(solution)/shard_map/ppermute | solution.py:328
  23.7 60.7 %copy-start.3 = (bf16[1568,768]{1,0:T(8,128)(2,1)S(1)}, bf16[1568,768]{1,0:T(8,128)(2,1)}, u32[]{:S(2)}) copy-start(bf16[1568,768]{1,0:T(8,128)(2,1)} %get-tuple-element.103) | copy-start | bytes 7225348
  23.7 60.7 %copy-start.56 = (f32[768]{0:T(1024)S(1)}, f32[768]{0:T(1024)}, u32[]{:S(2)}) copy-start(f32[768]{0:T(1024)} %param.27) | copy-start | bytes 9220
  23.7 60.7 %copy-start.64 = (f32[2304]{0:T(1024)S(1)}, f32[2304]{0:T(1024)}, u32[]{:S(2)}) copy-start(f32[2304]{0:T(1024)} %constant.253.clone.1) | copy-start | bytes 27652
  26.3 214.4 %copy-start.21 = (bf16[3328]{0:T(1024)(128)(2,1)}, bf16[3328]{0:T(1024)(128)(2,1)S(1)}, u32[]{:S(2)}) copy-start(bf16[3328]{0:T(1024)(128)(2,1)S(1)} %pad.18.clone) | copy-start | bytes 19972
  76.1 7.7 copy-start.15
  104.2 136.4 %copy-start.54 = (f32[768]{0:T(1024)S(1)}, f32[768]{0:T(1024)}, u32[]{:S(2)}) copy-start(f32[768]{0:T(1024)} %param.32) | copy-start | bytes 9220
  250.2 112.0 %copy-start.7 = (f32[3328,768]{1,0:T(8,128)}, f32[3328,768]{1,0:T(8,128)S(1)}, u32[]{:S(2)}) copy-start(f32[3328,768]{1,0:T(8,128)S(1)} %get-tuple-element.121) | copy-start | bytes 30670852
  250.3 111.9 %copy-start.29 = (f32[3328]{0:T(1024)}, f32[3328]{0:T(1024)S(1)}, u32[]{:S(2)}) copy-start(f32[3328]{0:T(1024)S(1)} %broadcast_multiply_fusion.1) | copy-start | bytes 39940
  252.2 110.0 %copy-start.36 = (f32[3328]{0:T(1024)}, f32[3328]{0:T(1024)S(1)}, u32[]{:S(2)}) copy-start(f32[3328]{0:T(1024)S(1)} %fusion.74) | copy-start | bytes 39940
  252.2 110.0 %copy-start.52 = (bf16[3072,768]{1,0:T(8,128)(2,1)S(1)}, bf16[3072,768]{1,0:T(8,128)(2,1)}, u32[]{:S(2)}) copy-start(bf16[3072,768]{1,0:T(8,128)(2,1)} %param.37) | copy-start | bytes 14155780
  252.2 110.0 %copy-start.55 = (f32[768]{0:T(1024)S(1)}, f32[768]{0:T(1024)}, u32[]{:S(2)}) copy-start(f32[768]{0:T(1024)} %param.38) | copy-start | bytes 9220
  384.6 21.8 %copy-start.1 = (f32[3328,768]{1,0:T(8,128)}, f32[3328,768]{1,0:T(8,128)S(1)}, u32[]{:S(2)}) copy-start(f32[3328,768]{1,0:T(8,128)S(1)} %get-tuple-element.124) | copy-start | bytes 30670852
  390.5 5.4 copy-start.39
  390.5 5.3 copy-start.59
  396.9 9.5 copy-start.38
  397.5 8.8 copy-start.20
  397.5 18.0 %copy-start.19 = (bf16[3328,8]{0,1:T(8,128)(2,1)}, bf16[3328,8]{0,1:T(8,128)(2,1)S(1)}, u32[]{:S(2)}) copy-start(bf16[3328,8]{0,1:T(8,128)(2,1)S(1)} %get-tuple-element.115) | copy-start | bytes 159748
  399.1 7.2 copy-start.12
  406.4 9.2 copy-start.14
  406.4 9.2 copy-start.51
  423.2 45.8 %copy-start.30 = (f32[3328]{0:T(1024)S(1)}, f32[3328]{0:T(1024)}, u32[]{:S(2)}) copy-start(f32[3328]{0:T(1024)} %copy-done.29) | copy-start | bytes 39940
  468.9 30.4 %copy-start.34 = (f32[3328]{0:T(1024)S(1)}, f32[3328]{0:T(1024)}, u32[]{:S(2)}) copy-start(f32[3328]{0:T(1024)} %copy-done.33) | copy-start | bytes 39940
  468.9 30.4 %copy-start.37 = (f32[3328]{0:T(1024)S(1)}, f32[3328]{0:T(1024)}, u32[]{:S(2)}) copy-start(f32[3328]{0:T(1024)} %copy-done.36) | copy-start | bytes 39940
  468.9 30.4 %copy-start.49 = (f32[768]{0:T(1024)S(1)}, f32[768]{0:T(1024)}, u32[]{:S(2)}) copy-start(f32[768]{0:T(1024)} %param.33) | copy-start | bytes 9220
  508.9 9.1 copy-start.2
  508.9 9.1 copy-start.27
  537.4 503.8 %reduce-scatter.15.cloned.1.call-start = ((), (), s32[]{:S(2)}) async-start(), calls=%async_computation.9 | async-start | bytes 3760128 | tf_op jit(solution)/shard_map/reduce_scatter | solution.py:428
  855.9 5.5 copy-start.10
  855.9 8.5 slice-start
  861.4 5.7 copy-start.4
  861.4 5.7 copy-start.16
  861.4 5.7 copy-start.22
  861.4 5.7 copy-start.25
  861.4 5.7 copy-start.42
  861.5 5.7 copy-start.57
  888.7 237.6 %reduce-scatter.23.cloned.1.call-start = ((), (), s32[]{:S(2)}) async-start(), calls=%async_computation.13 | async-start | bytes 5013504 | tf_op jit(solution)/shard_map/reduce_scatter | solution.py:428
  919.0 222.4 %all-reduce.3.cloned.1.call-start = ((), (), s32[]{:S(2)}) async-start(), calls=%async_computation.8 | async-start | bytes 466944 | tf_op jit(solution)/shard_map/psum | solution.py:448
  925.7 24.7 %copy-start.32 = (f32[3328]{0:T(1024)S(1)}, f32[3328]{0:T(1024)}, u32[]{:S(2)}) copy-start(f32[3328]{0:T(1024)} %copy-done.31) | copy-start | bytes 39940
  925.7 24.8 %copy-start.5 = (bf16[1568,768]{1,0:T(8,128)(2,1)S(1)}, bf16[1568,768]{1,0:T(8,128)(2,1)}, u32[]{:S(2)}) copy-start(bf16[1568,768]{1,0:T(8,128)(2,1)} %get-tuple-element.103) | copy-start | bytes 7225348
  925.7 24.8 %copy-start.23 = (bf16[3328]{0:T(1024)(128)(2,1)S(1)}, bf16[3328]{0:T(1024)(128)(2,1)}, u32[]{:S(2)}) copy-start(bf16[3328]{0:T(1024)(128)(2,1)} %copy-done.21) | copy-start | bytes 19972
  925.7 24.8 %copy-start.26 = (f32[3328]{0:T(1024)S(1)}, f32[3328]{0:T(1024)}, u32[]{:S(2)}) copy-start(f32[3328]{0:T(1024)} %copy-done.24) | copy-start | bytes 39940
  925.8 24.8 %copy-start.43 = (f32[768]{0:T(1024)S(1)}, f32[768]{0:T(1024)}, u32[]{:S(2)}) copy-start(f32[768]{0:T(1024)} %param.26) | copy-start | bytes 9220
  950.5 12.4 %copy-start.6 = (f32[3328,768]{1,0:T(8,128)S(1)}, f32[3328,768]{1,0:T(8,128)}, u32[]{:S(2)}) copy-start(f32[3328,768]{1,0:T(8,128)} %get-tuple-element.132) | copy-start | bytes 30670852
  950.5 12.4 %copy-start.28 = (f32[3328]{0:T(1024)S(1)}, f32[3328]{0:T(1024)}, u32[]{:S(2)}) copy-start(f32[3328]{0:T(1024)} %copy-done.27) | copy-start | bytes 39940
  998.0 158.6 %reduce-scatter.27.cloned.1.call-start = ((), (), s32[]{:S(2)}) async-start(), calls=%async_computation.15 | async-start | bytes 294912
  999.8 163.3 %reduce-scatter.19.cloned.1.call-start = ((), (), s32[]{:S(2)}) async-start(), calls=%async_computation.11 | async-start | bytes 5013504 | tf_op jit(solution)/shard_map/reduce_scatter | solution.py:428
  1026.9 6.2 copy-start.18
  1026.9 154.1 %reduce-scatter.25.cloned.1.call-start = ((), (), s32[]{:S(2)}) async-start(), calls=%async_computation.14 | async-start | bytes 884736
  1027.0 13.5 %slice-start.2 = ((s8[5111808]{0:T(1024)(128)(4,1)}), s8[917504]{0:T(1024)(128)(4,1)S(1)}, s32[]{:S(2)}) async-start(s8[5111808]{0:T(1024)(128)(4,1)} %bitcast.78), calls=%async_computation.19 | async-start | bytes 1835008
  1032.0 127.5 %collective-permute-start.3 = (bf16[1568,768]{1,0:T(8,128)(2,1)}, bf16[1568,768]{1,0:T(8,128)(2,1)}, u32[]{:S(2)}, u32[]{:S(2)}) collective-permute-start(bf16[1568,768]{1,0:T(8,128)(2,1)} %get-tuple-element.102), channel_id=1, source_target_pairs={{1,0},{0,1},{3,2},{2,3},{5,4},{4,5},{7,6},{6,7},{9,8},{8,9},{11,10... | collective-permute-start | bytes 7225352 | tf_op jit(solution)/shard_map/ppermute | solution.py:328
  1033.0 7.4 slice-start.3
  1038.1 8.5 copy-start.44
  1038.1 8.4 copy-start.45
  1038.8 90.1 %collective-permute-start.1 = (bf16[8,8,768]{2,1,0:T(8,128)(2,1)}, bf16[8,8,768]{2,1,0:T(8,128)(2,1)}, u32[]{:S(2)}, u32[]{:S(2)}) collective-permute-start(bf16[8,8,768]{2,1,0:T(8,128)(2,1)} %get-tuple-element.114), channel_id=1, source_target_pairs={{1,0},{0,1},{3,2},{2,3},{5,4},{4,5},{7,6},{6,7},{9,8},{8,9},{11,10... | collective-permute-start | bytes 294920 | tf_op jit(solution)/shard_map/ppermute | solution.py:328
  1043.3 141.1 %reduce-scatter.29.cloned.1.call-start = ((), (), s32[]{:S(2)}) async-start(), calls=%async_computation.16 | async-start | bytes 589824
  1128.2 59.5 %reduce-scatter.21.cloned.1.call-start = ((), (), s32[]{:S(2)}) async-start(), calls=%async_computation.12 | async-start | bytes 442368 | tf_op jit(solution)/shard_map/reduce_scatter | solution.py:429
  (18 other events, 36.8 us)
Sparse Core Ops, SparseCore 0:
  537.5 58.3 reduce-scatter.16
  888.8 68.2 reduce-scatter.14
  961.0 74.8 reduce-scatter.22
  1038.7 12.1 reduce-scatter.26
  1055.1 76.8 reduce-scatter.18
  1134.1 14.1 reduce-scatter.24
  1150.6 13.1 reduce-scatter.28
  1166.0 12.0 reduce-scatter.20
Sparse Core Ops, SparseCore 1:
  998.0 143.2 all-reduce.2

commit v2 on v1

v2 whole, which is shorter than its diff:
```python
import jax
import jax.numpy as jnp
from jax import lax
from jax.experimental import pallas as pl
from jax.experimental.pallas import tpu as pltpu
from jax.sharding import PartitionSpec as P

HEADS = 12
HEAD = 64
NTOK = 8
PATCH = 196
TILE = 256
MIDDLE = 448
LOG2E = 1.4426950408889634
LN2 = 0.6931471805599453
VMEM = 60 * 1024 * 1024

epsilon = 1e-06
masked_score = -1e30
bf16 = jnp.bfloat16
f32 = jnp.float32

NN = (((1,), (0,)), ((), ()))
NT = (((1,), (1,)), ((), ()))


def dot(left, right, dims=NN):
    return lax.dot_general(left, right, dims, preferred_element_type=f32)


def split3(value):
    hi = value.astype(bf16).astype(f32)
    mid = (value - hi).astype(bf16).astype(f32)
    return hi, mid, value - hi - mid


def up(count, unit):
    return -(-count // unit) * unit


def tile_of(count, most):
    return max(size for size in range(16, most + 1, 16) if count % size == 0)


def blocks_of(count, unit):
    return [(base, min(unit, count - base)) for base in range(0, count, unit)]


def flip(value):
    return jnp.concatenate([value[base : base + size].T for base, size in blocks_of(value.shape[0], 128)], axis=1)


def spread_heads(source, held, aug):
    count = source.shape[0]
    zero = jnp.zeros((HEAD, held.shape[2]), bf16)
    for j in range(2):
        other = (1 - j) * HEAD
        held[j, other : other + HEAD] = zero
        if held.shape[2] > count:
            edge = count // 128 * 128
            held[j, j * HEAD : (j + 1) * HEAD, edge:] = jnp.zeros((HEAD, held.shape[2] - edge), bf16)
        held[j, 128:256] = aug(j)
    for base, size in blocks_of(count, 256):
        flat = flip(source[base : base + size])
        for j in range(2):
            held[j, j * HEAD : (j + 1) * HEAD, base : base + size] = flat[j * HEAD : (j + 1) * HEAD]


def spread_queries(q, qp):
    ids = lax.broadcasted_iota(jnp.int32, (128, qp.shape[2]), 0)
    spread_heads(q, qp, lambda j: jnp.where(ids == 3, 1.0, 0.0).astype(bf16))


def flip_into(source, target):
    for base, size in blocks_of(source.shape[0], 256):
        target[:, base : base + size] = flip(source[base : base + size])


def key_block(k, kaug, base, size):
    return jnp.concatenate([k[pl.ds(base, size), :], kaug[pl.ds(base, size), :]], axis=1)


def value_block(vt, j, base, size):
    ones = jnp.ones((16, size), bf16)
    return jnp.concatenate([vt[j * HEAD : (j + 1) * HEAD, pl.ds(base, size)], ones], axis=0)


def over_tiles(step, begin, count):
    @pl.loop(begin // TILE, count // TILE, unroll=3)
    def _(t):
        step(pl.multiple_of(t * TILE, TILE), TILE)

    if count % TILE:
        step(count // TILE * TILE, count % TILE)


def fold_tile(k, kaug, qp, vt, acc, low, fresh, base, size):
    for j in range(2):
        p = jnp.exp2(dot(key_block(k, kaug, base, size), qp[j, :, low:])).astype(bf16)
        part = dot(value_block(vt, j, base, size), p)
        if fresh:
            acc[j, :, low:] = part
        else:
            acc[j, :, low:] += part


def attend_near_kernel(q, k, v, kaug, acc, qp, vt):
    spread_queries(q, qp)
    flip_into(v, vt)
    fold_tile(k, kaug, qp, vt, acc, 0, True, 0, TILE)
    over_tiles(lambda base, size: fold_tile(k, kaug, qp, vt, acc, 0, False, base, size), TILE, k.shape[0])


def attend_near(near, mixed, kaug):
    pairs = HEADS // 2
    return pl.pallas_call(
        attend_near_kernel,
        grid=(pairs,),
        in_specs=[
            pl.BlockSpec((near, 128), lambda h: (0, h)),
            pl.BlockSpec((near, 128), lambda h: (0, pairs + h)),
            pl.BlockSpec((near, 128), lambda h: (0, 2 * pairs + h)),
            pl.BlockSpec((near, 128), lambda h: (0, 0)),
        ],
        out_specs=pl.BlockSpec((2, HEAD + 16, near), lambda h: (h, 0, 0)),
        out_shape=jax.ShapeDtypeStruct((HEADS, HEAD + 16, near), f32),
        scratch_shapes=[pltpu.VMEM((2, 256, near), bf16), pltpu.VMEM((128, near), bf16)],
        compiler_params=pltpu.CompilerParams(vmem_limit_bytes=VMEM),
        cost_estimate=pl.CostEstimate(
            flops=4 * HEADS * near * near * 256, transcendentals=HEADS * near * near, bytes_accessed=near * 768 * 10
        ),
        name="attend_near",
    )(mixed, mixed, mixed, kaug)


def attend_kernel(q, k, v, kaug, *refs):
    att, aq, qp, vt, acc = refs[-5:]
    rows = q.shape[0]
    keys = k.shape[0]
    wide = qp.shape[2]
    spread_queries(q, qp)
    flip_into(v, vt)

    def fold(low, fresh):
        return lambda base, size: fold_tile(k, kaug, qp, vt, acc, low, fresh, base, size)

    begun = 0
    if len(refs) > 5:
        begun = refs[0].shape[2]
        acc[:, :, :begun] = refs[0][...]
    fold(begun, True)(0, TILE)
    if begun:
        over_tiles(fold(begun, False), TILE, begun)
    over_tiles(fold(0, False), max(begun, TILE), keys)

    for j in range(2):
        total = acc[j, HEAD : HEAD + 1]
        fine = (total > 2.0**-60) & (total < 2.0**60)
        bad = jnp.max(jnp.where(fine, 0.0, 1.0)) > 0.5
        acc[j, HEAD + 8 : HEAD + 9] = jnp.zeros((1, wide), f32)

        @pl.when(bad)
        def _():
            acc[j, 0:1] = jnp.full((1, wide), -1e38, f32)

            def largest(base, size):
                s = dot(key_block(k, kaug, base, size), qp[j])
                acc[j, 0:1] = jnp.maximum(acc[j, 0:1], jnp.max(s, axis=0, keepdims=True))

            over_tiles(largest, 0, keys)
            best = acc[j, 0:1]
            acc[j] = jnp.zeros((HEAD + 16, wide), f32)

            def again(base, size):
                p = jnp.exp2(dot(key_block(k, kaug, base, size), qp[j]) - best).astype(bf16)
                acc[j] += dot(value_block(vt, j, base, size), p)

            over_tiles(again, 0, keys)
            acc[j, HEAD + 8 : HEAD + 9] = best

    ids = lax.broadcasted_iota(jnp.int32, (HEAD, 128), 0)
    for base, size in blocks_of(rows, 128):
        here = slice(base, base + 128)
        outs = []
        augs = []
        for j in range(2):
            total = acc[j, HEAD : HEAD + 1, here]
            outs.append(acc[j, 0:HEAD, here] * (1.0 / total))
            lse = jnp.log2(total) + acc[j, HEAD + 8 : HEAD + 9, here]
            hi, mid, low = split3(-lse)
            aug = jnp.where(ids == 0, hi, jnp.where(ids == 1, mid, jnp.where(ids == 2, low, 0.0)))
            augs.append(jnp.where(ids == 3, 1.0, aug))
        att[base : base + size, :] = jnp.concatenate(outs, axis=0).T[:size].astype(bf16)
        aq[base : base + size, :] = jnp.concatenate(augs, axis=0).T[:size].astype(bf16)


def attend(mixed, keys_values, kaug, *begun):
    rows = mixed.shape[0]
    keys = keys_values.shape[0]
    pairs = HEADS // 2
    wide = up(rows, 128)
    first = keys_values.shape[1] // 128 - 2 * pairs
    return pl.pallas_call(
        attend_kernel,
        grid=(pairs,),
        in_specs=[
            pl.BlockSpec((rows, 128), lambda h: (0, h)),
            pl.BlockSpec((keys, 128), lambda h: (0, first + h)),
            pl.BlockSpec((keys, 128), lambda h: (0, first + pairs + h)),
            pl.BlockSpec((keys, 128), lambda h: (0, 0)),
        ]
        + [pl.BlockSpec((2,) + one.shape[1:], lambda h: (h, 0, 0)) for one in begun],
        out_specs=[
            pl.BlockSpec((rows, 128), lambda h: (0, h)),
            pl.BlockSpec((rows, 128), lambda h: (0, h)),
        ],
        out_shape=[
            jax.ShapeDtypeStruct((rows, HEADS * HEAD), bf16),
            jax.ShapeDtypeStruct((rows, HEADS * HEAD), bf16),
        ],
        scratch_shapes=[
            pltpu.VMEM((2, 256, wide), bf16),
            pltpu.VMEM((128, up(keys, 128)), bf16),
            pltpu.VMEM((2, HEAD + 16, wide), f32),
        ],
        compiler_params=pltpu.CompilerParams(vmem_limit_bytes=VMEM),
        cost_estimate=pl.CostEstimate(
            flops=4 * HEADS * rows * keys * 256, transcendentals=HEADS * rows * keys, bytes_accessed=rows * 768 * 10
        ),
        name="attend",
    )(mixed, keys_values, keys_values, kaug, *begun)


def attend_back_kernel(q, do, att, aq, k, v, act_rows, act_keys, kaug_t, dq, dk, dv, weight_grad, kp, vp, dkt, dvt, dqs):
    step = pl.program_id(1)
    rows = q.shape[0]
    keys = k.shape[0]
    tiles = up(keys, TILE) // TILE

    @pl.when(step == 0)
    def _():
        rest = jnp.zeros((HEAD - 16, kp.shape[2]), bf16)
        zero = jnp.zeros((HEAD, kp.shape[2]), bf16)
        halves = (jnp.concatenate([kaug_t[...], rest, zero], axis=0), jnp.concatenate([zero, kaug_t[...], rest], axis=0))
        for source, held in ((k, kp), (v, vp)):
            spread_heads(source, held, lambda j: halves[j])
        dkt[...] = jnp.zeros_like(dkt)
        dvt[...] = jnp.zeros_like(dvt)

    lane = lax.broadcasted_iota(jnp.int32, (rows, 128), 1)
    product = do[...].astype(f32) * att[...].astype(f32)
    inner0 = jnp.sum(jnp.where(lane < HEAD, product, 0.0), axis=1, keepdims=True)
    inner1 = jnp.sum(jnp.where(lane < HEAD, 0.0, product), axis=1, keepdims=True)
    hi, mid, low = split3(-jnp.where(lane < HEAD, inner0, inner1))
    within = lane % HEAD
    ado = jnp.where(within == 0, hi, jnp.where(within == 1, mid, jnp.where(within == 2, low, 0.0))).astype(bf16)
    qa = jnp.concatenate([q[...], aq[...]], axis=1)
    da = jnp.concatenate([do[...], ado], axis=1)
    qt = flip(q[...])
    dot_ = flip(do[...])
    units = [(j, t) for j in range(2) for t in range(tiles)]
    totals = [None, None]

    def scores(j, t):
        cols = slice(t * TILE, (t + 1) * TILE)
        return dot(qa, kp[j, :, cols]), dot(da, vp[j, :, cols])

    def weigh(s, dp):
        p = jnp.exp2(s)
        return p.astype(bf16), (p * dp).astype(bf16)

    def collect(j, t, p, ds):
        cols = slice(t * TILE, (t + 1) * TILE)
        part = slice(j * HEAD, (j + 1) * HEAD)
        dvt[part, cols] += dot(dot_[part], p)
        dkt[part, cols] += dot(qt[part], ds)
        more = dot(ds[:, : min(TILE, keys - t * TILE)], k[t * TILE : min(keys, (t + 1) * TILE), :])
        totals[j] = more if totals[j] is None else totals[j] + more

    raw = {}
    ready = {}
    count = len(units)
    for i in range(count + 2):
        if i < count:
            raw[i] = scores(*units[i])
        if 0 <= i - 1 < count:
            ready[i - 1] = weigh(*raw.pop(i - 1))
        if 0 <= i - 2 < count:
            collect(*units[i - 2], *ready.pop(i - 2))
    grad_q = (jnp.where(lane < HEAD, totals[0], totals[1]) * HEAD ** (-0.5)).astype(bf16)
    dq[...] = grad_q
    dqs[pl.ds(pl.multiple_of(step * rows, 16), rows), :] = grad_q

    @pl.when(step == pl.num_programs(1) - 1)
    def _():
        total = jnp.zeros((128, act_rows.shape[1]), f32)
        for base, size in blocks_of(dqs.shape[0], TILE):
            total += dot(flip(dqs[base : base + size]), act_rows[base : base + size])
        weight_grad[:, 0:128] = total.T.astype(bf16)
        total = jnp.zeros((256, act_rows.shape[1]), f32)
        for base, size in blocks_of(keys, TILE):
            grad_k = (dkt[:, base : base + size] * LN2).astype(bf16)
            grad_v = dvt[:, base : base + size].astype(bf16)
            dk[base : base + size] = grad_k.T
            dv[base : base + size] = grad_v.T
            total += dot(jnp.concatenate([grad_k, grad_v], axis=0), act_keys[base : base + size])
        weight_grad[:, 128:384] = total.T.astype(bf16)


def attend_back(start, pairs, mixed, keys_values, grad_att, att, aq, act, act_keys, kaug_t):
    rows, width = act.shape
    keys = keys_values.shape[0]
    wide = up(keys, TILE)
    size = tile_of(rows, 512)
    first = keys_values.shape[1] // 128 - HEADS
    here = pl.BlockSpec((size, 128), lambda h, r: (r, start + h))
    whole = pl.BlockSpec((keys, 128), lambda h, r: (0, h))
    return pl.pallas_call(
        attend_back_kernel,
        grid=(pairs, rows // size),
        in_specs=[
            here,
            here,
            here,
            here,
            pl.BlockSpec((keys, 128), lambda h, r: (0, first + start + h)),
            pl.BlockSpec((keys, 128), lambda h, r: (0, first + HEADS // 2 + start + h)),
            pl.BlockSpec((rows, width), lambda h, r: (0, 0), pipeline_mode=pl.Buffered(1)),
            pl.BlockSpec((keys, width), lambda h, r: (0, 0), pipeline_mode=pl.Buffered(1)),
            pl.BlockSpec((16, wide), lambda h, r: (0, 0), pipeline_mode=pl.Buffered(1)),
        ],
        out_specs=[
            pl.BlockSpec((size, 128), lambda h, r: (r, h)),
            whole,
            whole,
            pl.BlockSpec((width, 384), lambda h, r: (0, h)),
        ],
        out_shape=[
            jax.ShapeDtypeStruct((rows, pairs * 128), bf16),
            jax.ShapeDtypeStruct((keys, pairs * 128), bf16),
            jax.ShapeDtypeStruct((keys, pairs * 128), bf16),
            jax.ShapeDtypeStruct((width, pairs * 384), bf16),
        ],
        scratch_shapes=[
            pltpu.VMEM((2, 256, wide), bf16),
            pltpu.VMEM((2, 256, wide), bf16),
            pltpu.VMEM((128, wide), f32),
            pltpu.VMEM((128, wide), f32),
            pltpu.VMEM((rows, 128), bf16),
        ],
        compiler_params=pltpu.CompilerParams(vmem_limit_bytes=VMEM),
        cost_estimate=pl.CostEstimate(
            flops=20 * pairs * rows * keys * 200, transcendentals=2 * pairs * rows * keys, bytes_accessed=rows * 768 * 20
        ),
        name="attend_back",
    )(mixed, grad_att, att, aq, keys_values, keys_values, act, act_keys, kaug_t)


def norm_stats(value):
    average = jnp.mean(value, axis=-1, keepdims=True)
    centered = value - average
    variance = jnp.mean(centered * centered, axis=-1, keepdims=True)
    scale = lax.rsqrt(variance + epsilon)
    return centered * scale, scale


def norm_back(unit, scale, gain, grad):
    inner = grad * gain
    along = jnp.mean(inner * unit, axis=-1, keepdims=True)
    return scale * (inner - jnp.mean(inner, axis=-1, keepdims=True) - unit * along)


def gelu_pair(value):
    size = jnp.abs(value)
    bell = jnp.exp2(value * value * (-0.5 * LOG2E))
    base = 1.0 + 0.231641888 * size
    t = pl.reciprocal(base, approx=True)
    t = t * (2.0 - base * t)
    fit = t * (0.127414796 + t * (-0.142248368 + t * (0.7107068705 + t * (-0.7265760135 + t * 0.5307027145))))
    tail = fit * bell
    share = jnp.where(value >= 0.0, 1.0 - tail, tail)
    return value * share, share + value * (bell * 0.3989422804014327)


def column_sums(grad):
    return jnp.sum(grad, axis=0, keepdims=True)


def project_kernel(x, gain, bias, weight, col_scale, col_bias, *refs):
    mixed, act_out, x_out = refs[-3:]
    x_out[...] = x[...]
    unit, _ = norm_stats(x[...].astype(f32))
    act = (unit * gain[...] + bias[...]).astype(bf16)
    act_out[...] = act
    mixed[...] = (dot(act, weight[...]) * col_scale[...] + col_bias[...]).astype(bf16)


def fixed(array):
    return pl.BlockSpec(array.shape, lambda i: (0,) * array.ndim, pipeline_mode=pl.Buffered(1))


def project(start, total, x, others, held=()):
    count, width = x.shape
    cols = others[2].shape[1]
    sizes = (cols, width, width)
    tile = tile_of(count, 256)
    return pl.pallas_call(
        project_kernel,
        grid=(count // tile,),
        in_specs=[pl.BlockSpec((tile, width), lambda i: (i, 0))]
        + [fixed(o) for o in others]
        + [pl.BlockSpec(memory_space=pl.ANY) for _ in held],
        out_specs=[pl.BlockSpec((tile, size), lambda i: (start // tile + i, 0)) for size in sizes],
        out_shape=[jax.ShapeDtypeStruct((total, size), bf16) for size in sizes],
        input_output_aliases={6 + i: i for i in range(len(held))},
        compiler_params=pltpu.CompilerParams(vmem_limit_bytes=VMEM),
        name="project",
    )(x, *others, *held)


def middle_kernel(
    x, att, aux, bias_o, gain2, bias2, bias_1, bias_2, gain3, bias3, wo, w1, w2, m1, m2, cot,
    grad_att, grad_low, weight_grads, sums, sums_wide, small, map1g, map2g, pooled,
    hidden, slope, acc1, acc2, acco, stage, sem,
):
    step = pl.program_id(0)
    rows, width = x.shape
    wide = w1.shape[1]
    part = wide // 4

    @pl.when(step == 0)
    def _():
        for ref in (sums, sums_wide, small, map1g, map2g, pooled, acc1, acc2, acco):
            ref[...] = jnp.zeros_like(ref)

    att_low = att[...]
    resid1 = x[...].astype(f32) + dot(att_low, wo[...]) + bias_o[...]
    unit2, scale2 = norm_stats(resid1)
    act2 = (unit2 * gain2[...] + bias2[...]).astype(bf16)
    total = None
    for c in range(4):
        cols = slice(c * part, (c + 1) * part)
        value, rate = gelu_pair(dot(act2, w1[:, cols]) + bias_1[:, cols])
        value = value.astype(bf16)
        hidden[:, cols] = value
        slope[:, cols] = rate.astype(bf16)
        more = dot(value, w2[cols, :])
        total = more if total is None else total + more
    resid2 = resid1 + total + bias_2[...]
    unit3, scale3 = norm_stats(resid2)
    act3 = (unit3 * gain3[...] + bias3[...]).astype(bf16)
    map_hidden, map_slope = gelu_pair(dot(act3, m1[...]) + aux[4:5])
    map_hidden = map_hidden.astype(bf16)
    logits = dot(map_hidden, m2[...]) + aux[3:4]
    lanes = logits.shape[1]
    lane = lax.broadcasted_iota(jnp.int32, (rows, lanes), 1)
    row = lax.broadcasted_iota(jnp.int32, (rows, lanes), 0) + step * rows
    slot = row - (lane >> 3) * PATCH
    mask = (slot >= 0) & (slot.astype(f32) < aux[0:1])
    inverse = aux[1:2]
    raw = 1.0 / (1.0 + jnp.exp2(logits * (-LOG2E)))
    gates = jnp.where(mask, raw, 0.0)
    gates_low = gates.astype(bf16)
    output_low = resid2.astype(bf16)
    pooled[...] += dot(gates_low.T, output_low)
    gate_sum = jnp.sum(gates, axis=1, keepdims=True)
    inverse_row = inverse[:, 0:1]
    small[2:3] += column_sums(gates * (gate_sum - gates))

    grad_out = dot(gates_low, cot[...]) * inverse_row
    grad_gate = dot(output_low, cot[...], NT) * inverse + aux[2:3] * (gate_sum - gates)
    grad_logit = jnp.where(mask, grad_gate * raw * (1.0 - raw), 0.0)
    small[1:2] += column_sums(grad_logit)
    grad_logit = grad_logit.astype(bf16)
    map2g[...] += dot(map_hidden.T, grad_logit)
    grad_mpre = dot(grad_logit, m2[...], NT) * map_slope
    small[0:1] += column_sums(grad_mpre)
    grad_mpre = grad_mpre.astype(bf16)
    map1g[...] += dot(grad_mpre.T, act3)
    grad_act = dot(grad_mpre, m1[...], NT)
    sums[4:5] += column_sums(grad_act * unit3)
    sums[5:6] += column_sums(grad_act)
    grad_res2 = norm_back(unit3, scale3, gain3[...], grad_act) + grad_out

    sums[3:4] += column_sums(grad_res2)
    g2 = grad_res2.astype(bf16)
    g2_t = g2.T
    act2_t = act2.T
    grad_act = None
    for c in range(4):
        cols = slice(c * part, (c + 1) * part)
        grad_pre = dot(g2, w2[cols, :], NT) * slope[:, cols].astype(f32)
        sums_wide[0:1, cols] += column_sums(grad_pre)
        grad_pre = grad_pre.astype(bf16)
        acc2[:, cols] += dot(g2_t, hidden[:, cols])
        acc1[:, cols] += dot(act2_t, grad_pre)
        more = dot(grad_pre, w1[:, cols], NT)
        grad_act = more if grad_act is None else grad_act + more
    sums[1:2] += column_sums(grad_act * unit2)
    sums[2:3] += column_sums(grad_act)
    grad_res1 = norm_back(unit2, scale2, gain2[...], grad_act) + grad_res2

    sums[0:1] += column_sums(grad_res1)
    g1 = grad_res1.astype(bf16)
    grad_low[...] = g1
    acco[...] += dot(att_low.T, g1)
    grad_att[...] = dot(g1, wo[...], NT).astype(bf16)

    @pl.when(step == pl.num_programs(0) - 1)
    def _():
        share = stage.shape[1]
        groups = stage.shape[0]

        def drain(value, *targets):
            stage[...] = value.astype(bf16).reshape(stage.shape)
            copies = [pltpu.make_async_copy(stage.at[lo:hi], target, sem) for lo, hi, target in targets]
            for copy in copies:
                copy.start()
            for copy in copies:
                copy.wait()

        for c in range(4):
            cols = slice(c * part, (c + 1) * part)
            value1 = acc1[:, cols]
            value2 = acc2[:, cols].T
            if groups == 1:
                drain(value1, (0, 1, weight_grads.at[c : c + 1]))
                drain(value2, (0, 1, weight_grads.at[4 + c : 5 + c]))
            else:
                drain(value1, (0, groups, weight_grads.at[:, c]))
                drain(value2, *[(4 * i, 4 * i + 4, weight_grads.at[c * groups // 4 + i, 4:8]) for i in range(groups // 4)])
        if groups == 1:
            drain(acco[...], (0, 1, weight_grads.at[8:9]))
        else:
            drain(acco[...], (0, groups, weight_grads.at[:, 8]))


def middle(groups, x, att, *others):
    rows, width = x.shape
    wide = others[8 + 1].shape[1]
    share = width // groups
    if share % 16 == 0 and groups % 4 == 0:
        stage, blocks = (groups, share, width), (groups, 9, share, width)
    else:
        stage, blocks = (1, width, width), (9, width, width)
    lanes = others[0].shape[1]
    size = tile_of(rows, MIDDLE)
    tile = pl.BlockSpec((size, width), lambda i: (i, 0))
    anywhere = pl.BlockSpec(memory_space=pl.ANY)
    summed = [
        jax.ShapeDtypeStruct((8, width), f32),
        jax.ShapeDtypeStruct((8, wide), f32),
        jax.ShapeDtypeStruct((8, lanes), f32),
        jax.ShapeDtypeStruct((lanes, width), f32),
        jax.ShapeDtypeStruct((lanes, lanes), f32),
        jax.ShapeDtypeStruct((lanes, width), f32),
    ]
    return pl.pallas_call(
        middle_kernel,
        grid=(rows // size,),
        in_specs=[tile, tile] + [fixed(o) for o in others],
        out_specs=[tile, tile, anywhere] + [pl.BlockSpec(s.shape, lambda i: (0, 0)) for s in summed],
        out_shape=[
            jax.ShapeDtypeStruct((rows, width), bf16),
            jax.ShapeDtypeStruct((rows, width), bf16),
            jax.ShapeDtypeStruct(blocks, bf16),
        ]
        + summed,
        scratch_shapes=[
            pltpu.VMEM((size, wide), bf16),
            pltpu.VMEM((size, wide), bf16),
            pltpu.VMEM((width, wide), f32),
            pltpu.VMEM((width, wide), f32),
            pltpu.VMEM((width, width), f32),
            pltpu.VMEM(stage, bf16),
            pltpu.SemaphoreType.DMA,
        ],
        compiler_params=pltpu.CompilerParams(vmem_limit_bytes=VMEM),
        cost_estimate=pl.CostEstimate(
            flops=2 * rows * width * (6 * wide + 3 * width), transcendentals=rows * wide, bytes_accessed=rows * width * 12
        ),
        name="middle",
    )(x, att, *others)


def finish_kernel(place, x, g1, gain, bias, weight, *refs):
    grads, (grad_in, sums) = refs[:-2], refs[-2:]
    parts = len(grads) // 3
    width = x.shape[1]

    @pl.when(pl.program_id(0) == 0)
    def _():
        sums[...] = jnp.zeros_like(sums)

    unit, scale = norm_stats(x[...].astype(f32))
    grad_act = None
    for i in range(3):
        at = 0
        for n in range(parts):
            part = grads[3 * n + i][...]
            share = part.shape[1]
            if i != 1:
                sums[2 + i // 2 : 3 + i // 2, at : at + share] += column_sums(part.astype(f32))
            more = dot(part, weight[:, i * width + at : i * width + at + share], NT)
            grad_act = more if grad_act is None else grad_act + more
            at += share
    sums[0:1] += column_sums(grad_act * unit)
    sums[1:2] += column_sums(grad_act)
    total = norm_back(unit, scale, gain[...], grad_act) + g1[...].astype(f32)
    grad_in[...] = total.astype(grad_in.dtype).reshape(grad_in.shape)


def finish(start, count, x, g1, gain, bias, weight, grads, place=None, places=0):
    width = x.shape[1]
    size = tile_of(count, 256)
    begin = start // size
    tile = pl.BlockSpec((size, width), lambda i, at: (begin + i, 0))
    thin = [pl.BlockSpec((size, grad.shape[1]), lambda i, at: (begin + i, 0)) for grad in grads]
    if place is None:
        place = jnp.int32(0)
        out = (pl.BlockSpec((size, width), lambda i, at: (i, 0)), jax.ShapeDtypeStruct((count, width), bf16))
    else:
        out = (
            pl.BlockSpec((1, size, width), lambda i, at: (at[0], i, 0)),
            jax.ShapeDtypeStruct((places, count, width), f32),
        )

    def one(array):
        return pl.BlockSpec(array.shape, lambda i, at: (0, 0), pipeline_mode=pl.Buffered(1))

    return pl.pallas_call(
        finish_kernel,
        grid_spec=pltpu.PrefetchScalarGridSpec(
            num_scalar_prefetch=1,
            grid=(count // size,),
            in_specs=[tile] * 2 + [one(o) for o in (gain, bias, weight)] + thin,
            out_specs=[out[0], pl.BlockSpec((8, width), lambda i, at: (0, 0))],
        ),
        out_shape=[out[1], jax.ShapeDtypeStruct((8, width), f32)],
        compiler_params=pltpu.CompilerParams(vmem_limit_bytes=VMEM),
        cost_estimate=pl.CostEstimate(flops=1, transcendentals=0, bytes_accessed=1),
        name="finish",
    )(place.reshape(1), x, g1, gain, bias, weight, *grads)


def shards(
    inputs,
    frame_tokens,
    clip_frames,
    norm1_gain,
    norm1_bias,
    qkv_weight,
    query_bias,
    value_bias,
    out_weight,
    out_bias,
    norm2_gain,
    norm2_bias,
    fc1_weight,
    fc1_bias,
    fc2_weight,
    fc2_bias,
    learn_gain,
    learn_bias,
    map1_weight,
    map1_bias,
    map2_weight,
    map2_bias,
    cot_pooled,
):
    clip_count, piece, width = inputs.shape
    seq_size = lax.axis_size("seq")
    position = lax.axis_index("seq")
    clip_size = lax.axis_size("clip")
    frames_here = piece // PATCH
    scaling = HEAD ** (-0.5)
    slots_all = float(clip_count * clip_size * seq_size * frames_here)
    group = seq_size // clip_count
    mine = position // group
    seat = position % group

    def route(turn):
        return [
            (s, ((s % clip_count + turn) % clip_count) * group + s // clip_count) for s in range(seq_size)
        ]

    def send(value, turn, back=False):
        pairs = route(turn)
        if back:
            pairs = [(b, a) for a, b in pairs]
        if all(a == b for a, b in pairs):
            return value
        return lax.ppermute(value, "seq", pairs)

    def scatter(whole):
        return [
            send(lax.dynamic_index_in_dim(whole, (position + turn) % clip_count, 0, False), turn)
            for turn in range(clip_count)
        ]

    def gather_back(parts, kind, whole=None):
        if whole is None:
            whole = jnp.zeros((clip_count,) + parts[0].shape, kind)
        for turn, part in enumerate(parts):
            if part is not None:
                home = send(part, turn, True).astype(kind)
                whole = lax.dynamic_update_index_in_dim(whole, home, (position + turn) % clip_count, 0)
        return whole

    tokens = lax.dynamic_index_in_dim(frame_tokens, mine, 0, False)
    frames = lax.dynamic_index_in_dim(clip_frames, mine, 0, False)
    rows = clip_count * piece
    keys = group * rows
    split = piece % 16 == 0 and group == 1
    near = piece // TILE * TILE
    x_parts = scatter(inputs)
    cot = jnp.concatenate(scatter(cot_pooled), axis=0).reshape(clip_count * frames_here * NTOK, width)

    def placed(ids, at_seat):
        turn = ids // piece
        source = clip_count * at_seat + (mine - turn) % clip_count
        local = ids - turn * piece
        frame = local // PATCH
        slot = local - frame * PATCH
        return (source * frames_here + frame < frames) & (slot < tokens)

    key_ids = jnp.arange(keys, dtype=jnp.int32)
    key_inside = placed(key_ids % rows, key_ids // rows)
    lane16 = jnp.arange(HEAD)
    key_mask = jnp.where(key_inside, 0.0, masked_score)
    kaug = jnp.where(lane16[None, :] < 3, 1.0, jnp.where(lane16[None, :] == 3, key_mask[:, None], 0.0)).astype(bf16)
    kaug = jnp.concatenate([kaug, jnp.zeros_like(kaug)], axis=1)
    sub16 = jnp.arange(16)[:, None]
    wide_mask = jnp.pad(key_mask, (0, up(keys, TILE) - keys), constant_values=masked_score)
    kaug_t = jnp.where(sub16 < 3, 1.0, jnp.where(sub16 == 3, wide_mask[None, :], 0.0)).astype(bf16)

    def line(vector):
        return vector.reshape(1, -1)

    zeros = jnp.zeros((width,), f32)
    ones = jnp.ones((width,), f32)
    col_scale = line(jnp.concatenate([ones * (scaling * LOG2E), ones, ones]))
    col_bias = line(jnp.concatenate([query_bias * (scaling * LOG2E), zeros, value_bias]))
    others = (line(norm1_gain), line(norm1_bias), qkv_weight, col_scale, col_bias)
    begun = ()
    if split:
        held = project(0, rows, x_parts[0], others)
        held, begun = lax.optimization_barrier((held, (attend_near(near, held[0], kaug),)))
        mixed, act1, x_low = project(piece, rows, jnp.concatenate(x_parts[1:], axis=0), others, held)
    else:
        mixed, act1, x_low = project(0, rows, jnp.concatenate(x_parts, axis=0), others)
    if group == 1:
        keys_values, act_keys = mixed, act1
    else:
        both = lax.all_gather(mixed[:, width:], "seq", axis=0, tiled=True)
        keys_values = lax.dynamic_slice_in_dim(both, mine * keys, keys, 0)
        act_keys = lax.all_gather(act1, "seq", axis=0, tiled=True)
        act_keys = lax.dynamic_slice_in_dim(act_keys, mine * keys, keys, 0)
    att, aq = attend(mixed, keys_values, kaug, *begun)

    slots = clip_count * frames_here * NTOK
    lanes = -(-slots // 128) * 128
    pair_count = NTOK * (NTOK - 1)
    lane_ids = jnp.arange(lanes)
    lane_turn = lane_ids // (frames_here * NTOK)
    lane_frame = lane_ids // NTOK - lane_turn * frames_here
    lane_source = clip_count * seat + (mine - lane_turn) % clip_count
    lane_open = (lane_source * frames_here + lane_frame < frames) & (lane_ids < slots)
    inverse = lax.rsqrt(tokens.astype(f32))
    factor = 2.0 / pair_count * inverse * inverse / slots_all
    map_size = map1_bias.shape[0]
    aux = jnp.stack(
        [
            jnp.where(lane_open, tokens, 0).astype(f32),
            jnp.full((lanes,), inverse),
            jnp.full((lanes,), factor),
            jnp.tile(map2_bias, lanes // NTOK),
            jnp.pad(map1_bias, (0, lanes - map_size)),
        ]
        + [jnp.zeros((lanes,), f32)] * 3
    )
    map1_wide = jnp.pad(map1_weight, ((0, 0), (0, lanes - map_size)))
    map2_wide = jnp.pad(jnp.tile(map2_weight, (1, lanes // NTOK)), ((0, lanes - map_size), (0, 0)))
    cot = jnp.pad(cot, ((0, lanes - slots), (0, 0)))
    grad_att, grad_low, weight_part, sums, sums_wide, small, map1_part, map2_part, pooled = middle(
        clip_size,
        x_low,
        att,
        aux,
        line(out_bias),
        line(norm2_gain),
        line(norm2_bias),
        line(fc1_bias),
        line(fc2_bias),
        line(learn_gain),
        line(learn_bias),
        out_weight,
        fc1_weight,
        fc2_weight,
        map1_wide,
        map2_wide,
        cot,
    )

    def over_clip(matrix):
        return lax.psum_scatter(matrix, "clip", scatter_dimension=0, tiled=True)

    def over_seq(*matrices):
        thin = width // seq_size
        blocks = [
            m.reshape(m.shape[0], seq_size, -1, thin).transpose(1, 0, 2, 3).reshape(seq_size, -1, thin)
            for m in matrices
        ]
        total = lax.psum_scatter(jnp.concatenate(blocks, axis=1), "seq", scatter_dimension=0, tiled=False)
        outs = []
        at = 0
        for m, block in zip(matrices, blocks):
            count = block.shape[1]
            outs.append(total[at : at + count].reshape(m.shape[0], -1).astype(f32))
            at += count
        return outs

    def bits(size):
        return [1 << n for n in range(size.bit_length() - 1)]

    clip_steps = [("clip", bit) for bit in bits(clip_size)]
    seq_steps = [("seq", bit) for bit in bits(seq_size)]
    early_steps = clip_steps[:1] + seq_steps + clip_steps[1:]

    def meet(value, step):
        axis, bit = step
        return lax.ppermute(value, axis, [(i, i ^ bit) for i in range(lax.axis_size(axis))])

    def part_ways(blocks, step):
        axis, bit = step
        halves = blocks.reshape((-1, 2) + blocks.shape[1:])
        side = (lax.axis_index(axis) // bit) % 2
        away = lax.dynamic_index_in_dim(halves, 1 - side, 1, False)
        return lax.dynamic_index_in_dim(halves, side, 1, False), meet(away, step)

    def add_low(kept, received):
        return (kept.astype(f32) + received.astype(f32)).astype(bf16)

    def back(start, pairs, source):
        return attend_back(
            start, pairs, source, keys_values if group > 1 else source, grad_att, att, aq, act1, act_keys, kaug_t
        )

    tie = lax.optimization_barrier
    pairs = (4, 2)
    early = jnp.concatenate(
        [
            sums.reshape(-1),
            sums_wide[0],
            small.reshape(-1) * jnp.repeat(jnp.stack([1.0, 1.0, inverse * inverse] + [1.0] * 5), lanes),
            map1_part[:map_size].reshape(-1),
            jnp.sum(map2_part[:map_size].reshape(map_size, lanes // NTOK, NTOK), axis=1).reshape(-1),
        ]
    )
    share = width // clip_size
    if weight_part.ndim == 3:
        fc1_part = weight_part[:4].reshape(4, clip_size, share, width).transpose(1, 0, 2, 3)
        fc2_part = weight_part[4:8].reshape(clip_size, 4, share, width)
        weight_part = jnp.concatenate([fc1_part, fc2_part, weight_part[8].reshape(clip_size, 1, share, width)], axis=1)
    slab = over_clip(weight_part)[0]
    near_early = meet(early, early_steps[0])
    back0 = back(0, pairs[0], mixed)
    mixed, slab, early, near_early, back0 = tie((mixed, slab, early, near_early, back0))
    early = early + near_early
    near_early = meet(early, early_steps[1])
    fc1_grad, fc2_grad, out_grad = over_seq(
        slab[:4].transpose(1, 0, 2).reshape(share, 4 * width), slab[4:8].reshape(4 * share, width), slab[8]
    )
    slab0 = over_clip(back0[3])
    back1 = back(pairs[0], pairs[1], mixed)
    fc1_grad, fc2_grad, out_grad, slab0, early, near_early, back1 = tie(
        (fc1_grad, fc2_grad, out_grad, slab0, early, near_early, back1)
    )
    early = early + near_early
    pooled = (pooled[:slots] * inverse).astype(bf16).reshape(clip_count, frames_here, NTOK, width)
    pooled = gather_back([pooled[t] for t in range(clip_count)], bf16)

    grads = [list(one[:3]) for one in (back0, back1)]
    if group > 1:
        both = jnp.zeros((seq_size * rows, 2 * width), bf16)
        both = lax.dynamic_update_slice_in_dim(
            both, jnp.concatenate([one[i] for i in (1, 2) for one in grads], axis=1), mine * keys, 0
        )
        both = lax.psum_scatter(both, "seq", scatter_dimension=0, tiled=True)
        at = 0
        for i in (1, 2):
            for n in range(2):
                grads[n][i] = both[:, at : at + pairs[n] * 128]
                at += pairs[n] * 128
    grads = [grad for one in grads for grad in one]
    rest = (grad_low, line(norm1_gain), line(norm1_bias), qkv_weight, grads)
    near_early = meet(early, early_steps[2])
    kept, received = part_ways(back1[3].reshape(clip_size, share, -1), clip_steps[0])
    if split:
        far, late = finish(piece, rows - piece, x_low, *rest)
        far = [far[t * piece : (t + 1) * piece] for t in range(clip_count - 1)]
        far, x_low, late, near_early, received = tie((far, x_low, late, near_early, received))
    early = early + near_early
    near_early = meet(early, early_steps[3])
    kept, received = part_ways(add_low(kept, received), clip_steps[1])
    if split:
        local, local_sums = finish(0, piece, x_low, *rest, place=position % clip_count, places=clip_count)
        local, local_sums, near_early, received = tie((local, local_sums, near_early, received))
        input_grad = gather_back([None] + far, f32, local)
        late = (local_sums + late)[:4]
    else:
        local, late = finish(0, rows, x_low, *rest)
        input_grad = gather_back([local[t * piece : (t + 1) * piece] for t in range(clip_count)], f32)
        late = late[:4]
    early = early + near_early
    for step in early_steps[4:]:
        early = early + meet(early, step)
    slab1 = add_low(kept, received)
    for step in clip_steps[2:]:
        slab1 = add_low(*part_ways(slab1, step))
    for step in clip_steps + seq_steps:
        late = late + meet(late, step)
    qkv = [
        part.reshape(share, count, 3, 128).transpose(0, 2, 1, 3) for part, count in zip((slab0, slab1), pairs)
    ]
    qkv = jnp.concatenate(qkv, axis=2).reshape(share, seq_size, -1).transpose(1, 0, 2)
    for step in seq_steps:
        qkv = add_low(*part_ways(qkv, step))
    qkv_grad = qkv[0].astype(f32)

    at = 0
    taken = []
    for size in (sums.size, sums_wide.shape[1], small.size, map_size * width, map_size * NTOK):
        taken.append(early[at : at + size])
        at += size
    sums, fc1_bias_grad, small, map1_grad, map2_grad = taken
    sums = sums.reshape(8, width)
    small = small.reshape(8, lanes)
    map1_grad = map1_grad.reshape(map_size, width).T
    map2_grad = map2_grad.reshape(map_size, NTOK)
    map2_bias_grad = jnp.sum(small[1].reshape(lanes // NTOK, NTOK), axis=0)
    penalty = jnp.sum(small[2]) / pair_count / slots_all
    return (
        pooled,
        penalty,
        input_grad,
        late[0],
        late[1],
        qkv_grad,
        late[2],
        late[3],
        out_grad,
        sums[0],
        sums[1],
        sums[2],
        fc1_grad,
        fc1_bias_grad,
        fc2_grad,
        sums[3],
        sums[4],
        sums[5],
        map1_grad,
        small[0, :map_size],
        map2_grad,
        map2_bias_grad,
    )


def solution(mesh):
    row_spec = P("clip", "seq", None)
    pool_spec = P("clip", "seq", None, None)
    matrix_spec = P("clip", "seq")
    in_specs = (row_spec, P("clip"), P("clip")) + (P(),) * 19 + (pool_spec,)
    out_specs = (
        (pool_spec, P(), row_spec, P(), P(), matrix_spec, P(), P(), matrix_spec, P(), P(), P(), matrix_spec, P())
        + (matrix_spec,)
        + (P(),) * 7
    )
    return jax.shard_map(shards, mesh=mesh, in_specs=in_specs, out_specs=out_specs, check_vma=False)
```

time: 1200 us -> 867 us (0.72)
  matrix products: 388 us -> 0 us
  Pallas kernels: 455 us -> 717 us
  other arithmetic: 113 us -> 21 us
  blocking collectives: 79.1 us -> 0 us
  local copies, waits for them, and re-layouts: 89.4 us -> 34.4 us
  starting transfers between devices: 5.37 us -> 23 us
    dot_general x21 -> x0, matrix products: 388 us -> none  [dot(): return lax.dot_general(left, right, dims, preferred_element_type=f32)]
    pallas_call x1 -> x8, Pallas kernels: 318 us -> 603 us  [the longest x2 319 us: attend_back(): pl.pallas_call(attend_back_kernel, grid=(pairs, rows // size), in_specs=[...]
    psum x1 -> x0, blocking collectives: 79.1 us -> none  [flat_sum(): total = lax.psum(flat, ('clip', 'seq'))]
    reduce_sum x12 -> x2, other arithmetic: 59.4 us -> 0.56 us  [the longest x1 0.54 us: shards(): map2_bias_grad = jnp.sum(small[1].reshape(lanes // NTOK, NTOK), axis=0)]
    ppermute x0 -> x15, waiting for transfers between devices: none -> 47.3 us  [meet(): lax.ppermute(value, axis, [(i, i ^ bit) for i in range(lax.axis_size(axis...]
    ppermute x4, waiting for transfers between devices: 39.5 us -> 0.01 us  [send(): return lax.ppermute(value, 'seq', pairs)]
    another operation x4 -> x1, other arithmetic: 26.5 us -> 0.59 us  [shards(): jnp.stack([1.0, 1.0, inverse * inverse] + [1.0] * 5)]
    unnamed x148 -> x62, local copies, waits for them, and re-layouts: 27.7 us -> 5.69 us
  transfers between devices with their start and end apart: 13 -> 22, of which waited for: 2 -> 5; matrix products, arithmetic and copies ran while one was open for 22% -> 5% of each run, Pallas kernels for 27% -> 46%
where the time goes in v2:
time: 867 us; the launch traced here: 860 us
  Pallas kernels  717 us (83%)
  waiting for transfers between devices  47.4 us (5%)
  local copies, waits for them, and re-layouts  34.4 us (4%)
  starting transfers between devices  23 us (3%)
  other arithmetic  21 us (2%)
  between operations  17.2 us (2%)
    pallas_call x2, Pallas kernels, attend_back(): pl.pallas_call(attend_back_kernel, grid=(pairs, rows // size), in_specs=[...  319 us
    pallas_call x1, Pallas kernels, middle(): pl.pallas_call(middle_kernel, grid=(rows // size,), in_specs=[tile, tile]...  197 us
    pallas_call x1, Pallas kernels, attend(): pl.pallas_call(attend_kernel, grid=(pairs,), in_specs=[pl.BlockSpec((rows...  114 us
    ppermute x15, waiting for transfers between devices, meet(): lax.ppermute(value, axis, [(i, i ^ bit) for i in range(lax.axis_size(axis...  47.3 us
    pallas_call x1, Pallas kernels, attend_near(): pl.pallas_call(attend_near_kernel, grid=(pairs,), in_specs=[pl.BlockSpec(...  33.3 us
    pallas_call x2, Pallas kernels, finish(): pl.pallas_call(finish_kernel, grid_spec=pltpu.PrefetchScalarGridSpec(num_...  30 us
    pallas_call x2, Pallas kernels, project(): pl.pallas_call(project_kernel, grid=(count // tile,), in_specs=[pl.BlockS...  23.5 us
    ppermute x15, starting transfers between devices, meet(): lax.ppermute(value, axis, [(i, i ^ bit) for i in range(lax.axis_size(axis...  17.8 us
  transfers between devices with their start and end apart: 22, of which 5 were waited for; matrix products, arithmetic and copies ran while one was open for 5% of the time, Pallas kernels for 46%

profile of v2, /device:TPU:0, one launch (start us, length us, event | category | flops | bytes accessed | tf_op | source)
XLA Modules:
  0.0 860.2 jit_solution(6125089745639454687)
XLA Ops:
  7.4 5.0 dynamic-slice_bitcast_fusion
  12.4 3.0 collective-permute-start
  18.4 1.3 fusion.20
  20.3 1.1 concatenate.19.kaug
  21.3 11.7 %project.2 = (bf16[3136,2304]{1,0:T(8,128)(2,1)}, bf16[3136,768]{1,0:T(8,128)(2,1)}, bf16[3136,768]{1,0:T(8,128)(2,1)}) custom-call(bf16[1568,768]{1,0:T(8,128)(2,1)} %get-tuple-element.234.x, f32[1,768]{1,0:T(1,128)} %reshape.425.gain, f32[1,768]{1,0:T(1,128)} %reshape.426.bias, bf16[768,2304]{1,0:T(8,128)(2,1)} %weight.7, ...), custom_call_target="tpu_custom_call" | custom-call | tf_op jit(solution)/shard_map/project/pallas_call | solution.py:407
  33.1 33.3 %attend_near.1.refs_0_ = f32[12,80,1536]{2,1,0:T(8,128)} custom-call(bf16[3136,2304]{1,0:T(8,128)(2,1)} %get-tuple-element.85.q.k.v.refs_0_, bf16[3136,2304]{1,0:T(8,128)(2,1)} %get-tuple-element.85.q.k.v.refs_0_, bf16[3136,2304]{1,0:T(8,128)(2,1)} %get-tuple-element.85.q.k.v.refs_0_, bf16[3136,128]{1,0:T(8,128)(2,1)} %concatenate.19.kaug), custom_call_target="tpu_custom_call" | custom-call | flops 28991029248 | bytes 11796480 | tf_op jit(solution)/shard_map/attend_near/pallas_call | solution.py:116
  70.9 0.7 pad.18.m1
  71.7 0.6 pad.19.m2
  72.4 1.3 fusion.26
  73.8 0.6 stack.18.aux
  74.4 0.7 select_convert_fusion.1.kaug_t
  75.7 0.7 maximum_bitcast_fusion.cot
  76.4 1.4 copy-done.2
  77.8 11.8 %project.3 = (bf16[3136,2304]{1,0:T(8,128)(2,1)}, bf16[3136,768]{1,0:T(8,128)(2,1)}, bf16[3136,768]{1,0:T(8,128)(2,1)}) custom-call(bf16[1568,768]{1,0:T(8,128)(2,1)} %copy-done.2, f32[1,768]{1,0:T(1,128)} %reshape.425.gain, f32[1,768]{1,0:T(1,128)} %reshape.426.bias, ...), custom_call_target="tpu_custom_call", output_to_operand_aliasing={{0}: (6, {}), {1}: (7, {}), {2}: (8, {})} | custom-call | tf_op jit(solution)/shard_map/project/pallas_call | solution.py:407
  89.6 114.5 %attend.1 = (bf16[3136,768]{1,0:T(8,128)(2,1)}, bf16[3136,768]{1,0:T(8,128)(2,1)}) custom-call(bf16[3136,2304]{1,0:T(8,128)(2,1)} %get-tuple-element.110.q.k.v, bf16[3136,2304]{1,0:T(8,128)(2,1)} %get-tuple-element.110.q.k.v, bf16[3136,2304]{1,0:T(8,128)(2,1)} %get-tuple-element.110.q.k.v, bf16[3136,128]{1,0:T(8,128)(2,1)} %concatenate.19.kaug, ...), custom_call_target="tpu_custom_call" | custom-call | flops 120846286848 | bytes 24084480 | tf_op jit(solution)/shard_map/attend/pallas_call | solution.py:203
  204.0 196.6 %middle.1 = (bf16[3136,768]{1,0:T(8,128)(2,1)}, bf16[3136,768]{1,0:T(8,128)(2,1)}, bf16[16,9,48,768]{3,2,1,0:T(8,128)(2,1)}, f32[8,768]{1,0:T(8,128)}, f32[8,307...) custom-call(bf16[3136,768]{1,0:T(8,128)(2,1)} %get-tuple-element.128.x, ...), custom_call_target="tpu_custom_call" | custom-call | flops 99883155456 | bytes 28901376 | tf_op jit(solution)/shard_map/middle/pallas_call | solution.py:558
  400.7 0.6 copy-done.9
  401.6 0.6 constant_dynamic-update-slice_fusion.4
  402.2 0.9 slice.146
  403.9 0.7 constant_dynamic-update-slice_fusion.2
  404.6 0.7 constant_dynamic-update-slice_fusion.1
  405.9 211.0 %attend_back.2 = (bf16[3136,512]{1,0:T(8,128)(2,1)}, bf16[3136,512]{1,0:T(8,128)(2,1)}, bf16[3136,512]{1,0:T(8,128)(2,1)}, bf16[768,1536]{1,0:T(8,128)(2,1)}) custom-call(bf16[3136,2304]{1,0:T(8,128)(2,1)} %get-tuple-element.110.q.k.v, bf16[3136,768]{1,0:T(8,128)(2,1)} %get-tuple-element.99.do, bf16[3136,768]{1,0:T(8,128)(2,1)} %get-tuple-element.91.att, ...), custom_call_target="tpu_custom_call" | custom-call | flops 157351936000 | bytes 48168960 | tf_op jit(solution)/shard_map/attend_back/pallas_call | solution.py:318
  616.9 0.9 slice.151
  617.8 1.1 slice_bitcast_fusion
  619.6 0.9 pad_maximum_fusion
  620.5 0.9 copy.82
  621.6 1.1 add.255
  622.6 2.2 collective-permute-start.4
  624.9 108.4 %attend_back.3 = (bf16[3136,256]{1,0:T(8,128)(2,1)}, bf16[3136,256]{1,0:T(8,128)(2,1)}, bf16[3136,256]{1,0:T(8,128)(2,1)}, bf16[768,768]{1,0:T(8,128)(2,1)}) custom-call(bf16[3136,2304]{1,0:T(8,128)(2,1)} %get-tuple-element.110.q.k.v, bf16[3136,768]{1,0:T(8,128)(2,1)} %get-tuple-element.99.do, bf16[3136,768]{1,0:T(8,128)(2,1)} %get-tuple-element.91.att, ...), custom_call_target="tpu_custom_call" | custom-call | flops 78675968000 | bytes 48168960 | tf_op jit(solution)/shard_map/attend_back/pallas_call | solution.py:318
  733.3 1.7 fusion.5
  735.1 0.8 reshape.450
  735.8 1.4 fusion.7
  737.2 1.1 dynamic-slice_bitcast_fusion.2
  738.8 1.5 collective-permute-start.5
  740.3 14.9 %finish.2 = (bf16[1568,768]{1,0:T(8,128)(2,1)}, f32[8,768]{1,0:T(8,128)}) custom-call(s32[1]{0:T(128)} %constant.288.clone.1.place, bf16[3136,768]{1,0:T(8,128)(2,1)} %get-tuple-element.128.x, bf16[3136,768]{1,0:T(8,128)(2,1)} %get-tuple-element.117.g1, f32[1,768]{1,0:T(1,128)} %reshape.425.gain, f32[1,768]{1,0:T(1,128)} %reshape.426.bias, ...), custom_call_target="tpu_custom_call" | custom-call | flops 1 | bytes 1 | tf_op jit(solution)/shard_map/finish/pallas_call | solution.py:631
  755.4 0.7 collective-permute-start.8
  756.1 1.6 collective-permute-start.7
  757.7 1.0 multiply_convert_fusion
  758.8 15.1 %finish.3 = (f32[2,1568,768]{2,1,0:T(8,128)}, f32[8,768]{1,0:T(8,128)}) custom-call(s32[1]{0:T(128)} %bitcast.29.place, bf16[3136,768]{1,0:T(8,128)(2,1)} %get-tuple-element.128.x, bf16[3136,768]{1,0:T(8,128)(2,1)} %get-tuple-element.117.g1, f32[1,768]{1,0:T(1,128)} %reshape.425.gain, f32[1,768]{1,0:T(1,128)} %reshape.426.bias, bf16[768,2304]{1,0:T(8,128)(2,1)} %weight.7, ...), custom_call_target="tpu_custom_call" | custom-call | flops 1 | bytes 1 | tf_op jit(solution)/shard_map/finish/pallas_call | solution.py:631
  773.9 0.8 slice_add_fusion
  774.7 1.2 collective-permute-done.11
  775.9 1.5 collective-permute-start.12
  777.4 0.7 broadcast_in_dim.105
  778.1 0.6 fusion.6
  779.2 1.6 collective-permute-start.10
  781.2 1.0 fusion.1
  782.3 2.3 collective-permute-done.13
  784.5 2.6 collective-permute-start.14
  787.6 1.7 collective-permute-done.14
  789.8 0.6 bitcast_dynamic-update-slice_fusion
  790.4 1.0 reshape.445
  791.4 1.7 add.264
  793.1 2.5 collective-permute-start.9
  795.6 39.6 %collective-permute-done.15 = f32[4,768]{1,0:T(4,128)S(1)} collective-permute-done((f32[4,768]{1,0:T(4,128)S(1)}, f32[4,768]{1,0:T(4,128)S(1)}, u32[]{:S(2)}, u32[]{:S(2)}) %collective-permute-start.15) | collective-permute-done | bytes 12320 | tf_op jit(solution)/shard_map/ppermute | solution.py:832
  835.3 2.7 collective-permute-start.17
  838.0 0.6 slice_reduce_fusion
  838.6 2.6 collective-permute-done.17
  842.0 0.6 collective-permute-start.18
  842.6 1.0 add.265
  844.2 0.6 fusion.28
  845.9 0.7 reshape.449
  846.7 0.7 copy.85
  849.0 0.7 copy.89
  849.7 2.6 convert_dynamic-update-slice_fusion
  (161 shorter events, 16.7 us)
Async XLA Ops:
  7.2 64.4 %copy-start = (bf16[64,8]{0,1:T(8,128)(2,1)S(1)}, bf16[64,8]{0,1:T(8,128)(2,1)}, u32[]{:S(2)}) copy-start(bf16[64,8]{0,1:T(8,128)(2,1)} %param.43) | copy-start | bytes 3076
  7.2 609.7 %reduce-scatter.4.cloned.1.call-start = ((), (), s32[]{:S(2)}) async-start(), calls=%async_computation.3 | async-start | bytes 11280384 | tf_op jit(solution)/shard_map/reduce_scatter | solution.py:806
  7.3 8.1 copy-start.6
  7.3 8.2 copy-start.12
  7.3 8.7 %copy-start.13 = (f32[768]{0:T(1024)S(1)}, f32[768]{0:T(1024)}, u32[]{:S(2)}) copy-start(f32[768]{0:T(1024)} %param.27) | copy-start | bytes 9220
  7.3 9.3 %copy-start.20 = (f32[768]{0:T(1024)S(1)}, f32[768]{0:T(1024)}, u32[]{:S(2)}) copy-start(f32[768]{0:T(1024)} %param.29) | copy-start | bytes 9220
  7.3 9.3 %copy-start.22 = (f32[768]{0:T(1024)S(1)}, f32[768]{0:T(1024)}, u32[]{:S(2)}) copy-start(f32[768]{0:T(1024)} %param.30) | copy-start | bytes 9220
  7.3 9.9 %copy-start.25 = (s32[2]{0:T(128)S(1)}, s32[2]{0:T(128)}, u32[]{:S(2)}) copy-start(s32[2]{0:T(128)} %param.24) | copy-start | bytes 28
  7.3 10.5 %copy-start.26 = (s32[2]{0:T(128)S(1)}, s32[2]{0:T(128)}, u32[]{:S(2)}) copy-start(s32[2]{0:T(128)} %param.25) | copy-start | bytes 28
  12.4 64.0 %collective-permute-start = (bf16[1568,768]{1,0:T(8,128)(2,1)}, bf16[1568,768]{1,0:T(8,128)(2,1)S(1)}, u32[]{:S(2)}, u32[]{:S(2)}) collective-permute-start(bf16[1568,768]{1,0:T(8,128)(2,1)} %get-tuple-element.235), channel_id=1, source_target_pairs={{0,1},{1,0},{2,3},{3,2},{4,5},{5,4},{6,7},{7,6},{8,9},{9,8},{10,11... | collective-permute-start | bytes 7225352 | tf_op jit(solution)/shard_map/ppermute | solution.py:693
  15.4 60.4 %collective-permute-start.1 = (bf16[8,8,768]{2,1,0:T(8,128)(2,1)S(1)}, bf16[8,8,768]{2,1,0:T(8,128)(2,1)S(1)}, u32[]{:S(2)}, u32[]{:S(2)}) collective-permute-start(bf16[8,8,768]{2,1,0:T(8,128)(2,1)S(1)} %get-tuple-element.249), channel_id=1, source_target_pairs={{0,1},{1,0},{2,3},{3,2},{4,5},{5,4},{6,7},{7,6},{8,9},{9,8},{10,11... | collective-permute-start | bytes 294920 | tf_op jit(solution)/shard_map/ppermute | solution.py:693
  33.0 34.1 %copy-start.24 = (f32[8]{0:T(128)S(1)}, f32[8]{0:T(128)}, u32[]{:S(2)}) copy-start(f32[8]{0:T(128)} %param.44) | copy-start | bytes 100
  33.0 34.2 %copy-start.14 = (f32[768]{0:T(1024)S(1)}, f32[768]{0:T(1024)}, u32[]{:S(2)}) copy-start(f32[768]{0:T(1024)} %param.32) | copy-start | bytes 9220
  33.0 34.8 %copy-start.15 = (f32[768]{0:T(1024)S(1)}, f32[768]{0:T(1024)}, u32[]{:S(2)}) copy-start(f32[768]{0:T(1024)} %param.33) | copy-start | bytes 9220
  33.1 35.4 %copy-start.16 = (f32[768]{0:T(1024)S(1)}, f32[768]{0:T(1024)}, u32[]{:S(2)}) copy-start(f32[768]{0:T(1024)} %param.34) | copy-start | bytes 9220
  33.1 35.9 %copy-start.17 = (f32[768]{0:T(1024)S(1)}, f32[768]{0:T(1024)}, u32[]{:S(2)}) copy-start(f32[768]{0:T(1024)} %param.38) | copy-start | bytes 9220
  33.1 36.5 %copy-start.18 = (f32[768]{0:T(1024)S(1)}, f32[768]{0:T(1024)}, u32[]{:S(2)}) copy-start(f32[768]{0:T(1024)} %param.39) | copy-start | bytes 9220
  33.1 37.1 %copy-start.19 = (f32[768]{0:T(1024)S(1)}, f32[768]{0:T(1024)}, u32[]{:S(2)}) copy-start(f32[768]{0:T(1024)} %param.40) | copy-start | bytes 9220
  33.1 37.6 %copy-start.8 = (bf16[768,64]{0,1:T(8,128)(2,1)S(1)}, bf16[768,64]{0,1:T(8,128)(2,1)}, u32[]{:S(2)}) copy-start(bf16[768,64]{0,1:T(8,128)(2,1)} %param.41) | copy-start | bytes 294916
  33.1 40.6 %copy-start.27 = (f32[64]{0:T(128)S(1)}, f32[64]{0:T(128)}, u32[]{:S(2)}) copy-start(f32[64]{0:T(128)} %param.42) | copy-start | bytes 772
  76.4 1.4 copy-start.2
  400.6 0.7 copy-start.9
  400.6 0.8 copy-start.10
  400.6 2.5 copy-start.7
  400.6 3.3 copy-start.21
  400.7 3.3 copy-start.23
  400.7 332.6 %reduce-scatter.6.cloned.1.call-start = ((), (), s32[]{:S(2)}) async-start(), calls=%async_computation.4 | async-start | bytes 995328 | tf_op jit(solution)/shard_map/reduce_scatter | solution.py:814
  405.9 211.0 %collective-permute-start.3 = (f32[59904]{0:T(1024)}, f32[59904]{0:T(1024)}, u32[]{:S(2)}, u32[]{:S(2)}) collective-permute-start(f32[59904]{0:T(1024)} %constant_dynamic-update-slice_fusion), channel_id=1, source_target_pairs={{0,2},{2,0},{4,6},{6,4},{8,10},{10,8},{12,14},{14,12},{16,18},{18,... | collective-permute-start | bytes 718856 | tf_op jit(solution)/shard_map/ppermute | solution.py:832
  621.5 115.7 %reduce-scatter.8.cloned.1.call-start = ((), (), s32[]{:S(2)}) async-start(), calls=%async_computation.5 | async-start | bytes 2506752 | tf_op jit(solution)/shard_map/reduce_scatter | solution.py:806
  622.6 114.6 %collective-permute-start.4 = (f32[59904]{0:T(1024)S(1)}, f32[59904]{0:T(1024)S(1)}, u32[]{:S(2)}, u32[]{:S(2)}) collective-permute-start(f32[59904]{0:T(1024)S(1)} %add.255), channel_id=1, source_target_pairs={{0,1},{1,0},{2,3},{3,2},{4,5},{5,4},{6,7},{7,6},{8,9},{9,8},{10,11... | collective-permute-start | bytes 718856 | tf_op jit(solution)/shard_map/ppermute | solution.py:832
  738.3 16.9 %collective-permute-start.6 = (bf16[8,48,768]{2,1,0:T(8,128)(2,1)S(1)}, bf16[8,48,768]{2,1,0:T(8,128)(2,1)S(1)}, u32[]{:S(2)}, u32[]{:S(2)}) collective-permute-start(bf16[8,48,768]{2,1,0:T(8,128)(2,1)S(1)} %dynamic-slice_bitcast_fusion.2), channel_id=1, source_target_pairs={{0,2},{2,0},{4,6},{6,4},{8,10},{10,8},{12,14},{14,12},{16,18},{18,... | collective-permute-start | bytes 1769480 | tf_op jit(solution)/shard_map/ppermute | solution.py:832
  738.8 16.4 %collective-permute-start.5 = (f32[59904]{0:T(1024)S(1)}, f32[59904]{0:T(1024)S(1)}, u32[]{:S(2)}, u32[]{:S(2)}) collective-permute-start(f32[59904]{0:T(1024)S(1)} %add.256), channel_id=1, source_target_pairs={{0,4},{2,6},{4,0},{6,2},{8,12},{10,14},{12,8},{14,10},{16,20},{18,... | collective-permute-start | bytes 718856 | tf_op jit(solution)/shard_map/ppermute | solution.py:832
  740.3 14.9 %copy-start.3 = (bf16[768,768]{1,0:T(8,128)(2,1)S(1)}, bf16[768,768]{1,0:T(8,128)(2,1)}, u32[]{:S(2)}) copy-start(bf16[768,768]{1,0:T(8,128)(2,1)} %get-tuple-element.126) | copy-start | bytes 3538948
  755.4 18.5 %collective-permute-start.8 = (bf16[4,48,768]{2,1,0:T(8,128)(2,1)S(1)}, bf16[4,48,768]{2,1,0:T(8,128)(2,1)S(1)}, u32[]{:S(2)}, u32[]{:S(2)}) collective-permute-start(bf16[4,48,768]{2,1,0:T(8,128)(2,1)S(1)} %dynamic-slice_bitcast_fusion.3), channel_id=1, source_target_pairs={{0,4},{2,6},{4,0},{6,2},{8,12},{10,14},{12,8},{14,10},{16,20},{18,... | collective-permute-start | bytes 884744 | tf_op jit(solution)/shard_map/ppermute | solution.py:832
  756.1 17.8 %collective-permute-start.7 = (f32[59904]{0:T(1024)S(1)}, f32[59904]{0:T(1024)S(1)}, u32[]{:S(2)}, u32[]{:S(2)}) collective-permute-start(f32[59904]{0:T(1024)S(1)} %add.259), channel_id=1, source_target_pairs={{0,8},{2,10},{4,12},{6,14},{8,0},{10,2},{12,4},{14,6},{16,24},{18,... | collective-permute-start | bytes 718856 | tf_op jit(solution)/shard_map/ppermute | solution.py:832
  758.8 15.2 %copy-start.11 = (f32[8,768]{1,0:T(8,128)S(1)}, f32[8,768]{1,0:T(8,128)}, u32[]{:S(2)}) copy-start(f32[8,768]{1,0:T(8,128)} %get-tuple-element.136) | copy-start | bytes 73732
  773.9 4.8 copy-start.5
  773.9 4.8 copy-start.4
  774.7 1.2 collective-permute-start.11
  775.9 4.9 collective-permute-start.12
  778.7 11.0 %collective-permute-start.2 = (bf16[8,8,768]{2,1,0:T(8,128)(2,1)S(1)}, bf16[8,8,768]{2,1,0:T(8,128)(2,1)S(1)}, u32[]{:S(2)}, u32[]{:S(2)}) collective-permute-start(bf16[8,8,768]{2,1,0:T(8,128)(2,1)S(1)} %slice_bitcast_fusion.2), channel_id=1, source_target_pairs={{1,0},{0,1},{3,2},{2,3},{5,4},{4,5},{7,6},{6,7},{9,8},{8,9},{11,10... | collective-permute-start | bytes 294920 | tf_op jit(solution)/shard_map/ppermute | solution.py:693
  779.2 70.5 %collective-permute-start.10 = (bf16[1568,768]{1,0:T(8,128)(2,1)}, bf16[1568,768]{1,0:T(8,128)(2,1)S(1)}, u32[]{:S(2)}, u32[]{:S(2)}) collective-permute-start(bf16[1568,768]{1,0:T(8,128)(2,1)} %get-tuple-element.134), channel_id=1, source_target_pairs={{1,0},{0,1},{3,2},{2,3},{5,4},{4,5},{7,6},{6,7},{9,8},{8,9},{11,10... | collective-permute-start | bytes 7225352 | tf_op jit(solution)/shard_map/ppermute | solution.py:693
  780.8 3.8 collective-permute-start.13
  784.5 4.7 collective-permute-start.14
  787.2 48.0 %collective-permute-start.16 = (bf16[2,48,768]{2,1,0:T(8,128)(2,1)S(1)}, bf16[2,48,768]{2,1,0:T(8,128)(2,1)S(1)}, u32[]{:S(2)}, u32[]{:S(2)}) collective-permute-start(bf16[2,48,768]{2,1,0:T(8,128)(2,1)S(1)} %dynamic-slice_bitcast_fusion.5), channel_id=1, source_target_pairs={{0,8},{2,10},{4,12},{6,14},{8,0},{10,2},{12,4},{14,6},{16,24},{18,... | collective-permute-start | bytes 442376 | tf_op jit(solution)/shard_map/ppermute | solution.py:832
  789.3 45.9 %collective-permute-start.15 = (f32[4,768]{1,0:T(4,128)S(1)}, f32[4,768]{1,0:T(4,128)S(1)}, u32[]{:S(2)}, u32[]{:S(2)}) collective-permute-start(f32[4,768]{1,0:T(4,128)S(1)} %add.270), channel_id=1, source_target_pairs={{0,1},{1,0},{2,3},{3,2},{4,5},{5,4},{6,7},{7,6},{8,9},{9,8},{10,11... | collective-permute-start | bytes 36872 | tf_op jit(solution)/shard_map/ppermute | solution.py:832
  793.1 49.5 %collective-permute-start.9 = (f32[59904]{0:T(1024)}, f32[59904]{0:T(1024)S(1)}, u32[]{:S(2)}, u32[]{:S(2)}) collective-permute-start(f32[59904]{0:T(1024)} %add.264), channel_id=1, source_target_pairs={{0,16},{2,18},{4,20},{6,22},{8,24},{10,26},{12,28},{14,30},{16,0},... | collective-permute-start | bytes 718856 | tf_op jit(solution)/shard_map/ppermute | solution.py:832
  835.3 5.9 collective-permute-start.17
  842.0 6.7 collective-permute-start.18
  849.0 3.3 copy-start.1
Sparse Core Ops, SparseCore 0:
  400.8 121.9 reduce-scatter.3
  621.6 18.3 reduce-scatter.5
  644.2 64.1 reduce-scatter.7

commit v3 on v2

--- a/solution.py
+++ b/solution.py
@@ -10,6 +10,7 @@
 NTOK = 8
 PATCH = 196
 TILE = 256
+AHEAD = 0
 MIDDLE = 448
 LOG2E = 1.4426950408889634
 LN2 = 0.6931471805599453
@@ -247,6 +248,31 @@
         dkt[...] = jnp.zeros_like(dkt)
         dvt[...] = jnp.zeros_like(dvt)
 
+    units = [(j, t) for j in range(2) for t in range(tiles)]
+    count = len(units)
+    totals = [None, None]
+    qa = jnp.concatenate([q[...], aq[...]], axis=1)
+
+    def cols(t):
+        return slice(t * TILE, (t + 1) * TILE)
+
+    def scores(i):
+        j, t = units[i]
+        return dot(qa, kp[j, :, cols(t)])
+
+    def weigh(s, dp):
+        p = jnp.exp2(s)
+        return p.astype(bf16), (p * dp).astype(bf16)
+
+    def collect(j, t, p, ds):
+        part = slice(j * HEAD, (j + 1) * HEAD)
+        dvt[part, cols(t)] += dot(dot_[part], p)
+        dkt[part, cols(t)] += dot(qt[part], ds)
+        more = dot(ds[:, : min(TILE, keys - t * TILE)], k[t * TILE : min(keys, (t + 1) * TILE), :])
+        totals[j] = more if totals[j] is None else totals[j] + more
+
+    ahead = AHEAD
+    raw = {i: scores(i) for i in range(min(ahead, count))}
     lane = lax.broadcasted_iota(jnp.int32, (rows, 128), 1)
     product = do[...].astype(f32) * att[...].astype(f32)
     inner0 = jnp.sum(jnp.where(lane < HEAD, product, 0.0), axis=1, keepdims=True)
@@ -254,35 +280,16 @@
     hi, mid, low = split3(-jnp.where(lane < HEAD, inner0, inner1))
     within = lane % HEAD
     ado = jnp.where(within == 0, hi, jnp.where(within == 1, mid, jnp.where(within == 2, low, 0.0))).astype(bf16)
-    qa = jnp.concatenate([q[...], aq[...]], axis=1)
     da = jnp.concatenate([do[...], ado], axis=1)
-    qt = flip(q[...])
-    dot_ = flip(do[...])
-    units = [(j, t) for j in range(2) for t in range(tiles)]
-    totals = [None, None]
-
-    def scores(j, t):
-        cols = slice(t * TILE, (t + 1) * TILE)
-        return dot(qa, kp[j, :, cols]), dot(da, vp[j, :, cols])
-
-    def weigh(s, dp):
-        p = jnp.exp2(s)
-        return p.astype(bf16), (p * dp).astype(bf16)
-
-    def collect(j, t, p, ds):
-        cols = slice(t * TILE, (t + 1) * TILE)
-        part = slice(j * HEAD, (j + 1) * HEAD)
-        dvt[part, cols] += dot(dot_[part], p)
-        dkt[part, cols] += dot(qt[part], ds)
-        more = dot(ds[:, : min(TILE, keys - t * TILE)], k[t * TILE : min(keys, (t + 1) * TILE), :])
-        totals[j] = more if totals[j] is None else totals[j] + more
-
-    raw = {}
     ready = {}
-    count = len(units)
     for i in range(count + 2):
         if i < count:
-            raw[i] = scores(*units[i])
+            j, t = units[i]
+            s = raw.pop(i) if i in raw else scores(i)
+            raw[i] = (s, dot(da, vp[j, :, cols(t)]))
+        if i == 1:
+            qt = flip(q[...])
+            dot_ = flip(do[...])
         if 0 <= i - 1 < count:
             ready[i - 1] = weigh(*raw.pop(i - 1))
         if 0 <= i - 2 < count:
@@ -386,69 +393,83 @@
     return jnp.sum(grad, axis=0, keepdims=True)
 
 
-def project_kernel(x, gain, bias, weight, col_scale, col_bias, *refs):
+def project_kernel(place, x, vec, weight, *refs):
     mixed, act_out, x_out = refs[-3:]
-    x_out[...] = x[...]
-    unit, _ = norm_stats(x[...].astype(f32))
-    act = (unit * gain[...] + bias[...]).astype(bf16)
+    width = vec.shape[1]
+    rows = x[0]
+    x_out[...] = rows
+    unit, _ = norm_stats(rows.astype(f32))
+    act = (unit * vec[0:1] + vec[1:2]).astype(bf16)
     act_out[...] = act
-    mixed[...] = (dot(act, weight[...]) * col_scale[...] + col_bias[...]).astype(bf16)
+    total = dot(act, weight[...])
+    mixed[:, :width] = ((total[:, :width] + vec[8:9]) * (HEAD ** (-0.5) * LOG2E)).astype(bf16)
+    mixed[:, width : 2 * width] = total[:, width : 2 * width].astype(bf16)
+    mixed[:, 2 * width :] = (total[:, 2 * width :] + vec[9:10]).astype(bf16)
 
 
 def fixed(array):
     return pl.BlockSpec(array.shape, lambda i: (0,) * array.ndim, pipeline_mode=pl.Buffered(1))
 
 
-def project(start, total, x, others, held=()):
-    count, width = x.shape
-    cols = others[2].shape[1]
+def project(start, total, x, place, vec, weight, held=()):
+    _, count, width = x.shape
+    cols = weight.shape[1]
     sizes = (cols, width, width)
     tile = tile_of(count, 256)
+
+    def one(array):
+        return pl.BlockSpec(array.shape, lambda i, at: (0, 0), pipeline_mode=pl.Buffered(1))
+
     return pl.pallas_call(
         project_kernel,
-        grid=(count // tile,),
-        in_specs=[pl.BlockSpec((tile, width), lambda i: (i, 0))]
-        + [fixed(o) for o in others]
-        + [pl.BlockSpec(memory_space=pl.ANY) for _ in held],
-        out_specs=[pl.BlockSpec((tile, size), lambda i: (start // tile + i, 0)) for size in sizes],
+        grid_spec=pltpu.PrefetchScalarGridSpec(
+            num_scalar_prefetch=1,
+            grid=(count // tile,),
+            in_specs=[pl.BlockSpec((1, tile, width), lambda i, at: (at[0], i, 0)), one(vec), one(weight)]
+            + [pl.BlockSpec(memory_space=pl.ANY) for _ in held],
+            out_specs=[pl.BlockSpec((tile, size), lambda i, at: (start // tile + i, 0)) for size in sizes],
+        ),
         out_shape=[jax.ShapeDtypeStruct((total, size), bf16) for size in sizes],
-        input_output_aliases={6 + i: i for i in range(len(held))},
+        input_output_aliases={4 + i: i for i in range(len(held))},
         compiler_params=pltpu.CompilerParams(vmem_limit_bytes=VMEM),
         name="project",
-    )(x, *others, *held)
+    )(place.reshape(1), x, vec, weight, *held)
 
 
 def middle_kernel(
-    x, att, aux, bias_o, gain2, bias2, bias_1, bias_2, gain3, bias3, wo, w1, w2, m1, m2, cot,
-    grad_att, grad_low, weight_grads, sums, sums_wide, small, map1g, map2g, pooled,
-    hidden, slope, acc1, acc2, acco, stage, sem,
+    x, att, aux, vec, wo, w1, w2, m1, m2, cot, grad_att, grad_low, weight_grads, sums, pooled_out,
+    hidden, slope, acc1, acc2, acco, pooled, map2g, stage, sems,
 ):
     step = pl.program_id(0)
     rows, width = x.shape
     wide = w1.shape[1]
     part = wide // 4
+    map_size = sums.shape[0] - 32
+    bias_o, gain2, bias2, bias_2, gain3, bias3 = [vec[n : n + 1] for n in range(2, 8)]
 
     @pl.when(step == 0)
     def _():
-        for ref in (sums, sums_wide, small, map1g, map2g, pooled, acc1, acc2, acco):
+        for ref in (sums, pooled, map2g, acc1, acc2, acco):
             ref[...] = jnp.zeros_like(ref)
 
     att_low = att[...]
-    resid1 = x[...].astype(f32) + dot(att_low, wo[...]) + bias_o[...]
+    resid1 = x[...].astype(f32) + dot(att_low, wo[...]) + bias_o
     unit2, scale2 = norm_stats(resid1)
-    act2 = (unit2 * gain2[...] + bias2[...]).astype(bf16)
+    act2 = (unit2 * gain2 + bias2).astype(bf16)
     total = None
     for c in range(4):
         cols = slice(c * part, (c + 1) * part)
-        value, rate = gelu_pair(dot(act2, w1[:, cols]) + bias_1[:, cols])
+        value, rate = gelu_pair(dot(act2, w1[:, cols]) + vec[10 + c : 11 + c])
         value = value.astype(bf16)
         hidden[:, cols] = value
         slope[:, cols] = rate.astype(bf16)
         more = dot(value, w2[cols, :])
         total = more if total is None else total + more
-    resid2 = resid1 + total + bias_2[...]
+    resid2 = resid1 + total + bias_2
+    output_low = resid2.astype(bf16)
+    grad_gate = dot(output_low, cot[...], NT)
     unit3, scale3 = norm_stats(resid2)
-    act3 = (unit3 * gain3[...] + bias3[...]).astype(bf16)
+    act3 = (unit3 * gain3 + bias3).astype(bf16)
     map_hidden, map_slope = gelu_pair(dot(act3, m1[...]) + aux[4:5])
     map_hidden = map_hidden.astype(bf16)
     logits = dot(map_hidden, m2[...]) + aux[3:4]
@@ -461,26 +482,25 @@
     raw = 1.0 / (1.0 + jnp.exp2(logits * (-LOG2E)))
     gates = jnp.where(mask, raw, 0.0)
     gates_low = gates.astype(bf16)
-    output_low = resid2.astype(bf16)
     pooled[...] += dot(gates_low.T, output_low)
     gate_sum = jnp.sum(gates, axis=1, keepdims=True)
     inverse_row = inverse[:, 0:1]
-    small[2:3] += column_sums(gates * (gate_sum - gates))
+    sums[6:7, 256:384] += column_sums(gates * (gate_sum - gates)) * (inverse * inverse)
 
     grad_out = dot(gates_low, cot[...]) * inverse_row
-    grad_gate = dot(output_low, cot[...], NT) * inverse + aux[2:3] * (gate_sum - gates)
+    grad_gate = grad_gate * inverse + aux[2:3] * (gate_sum - gates)
     grad_logit = jnp.where(mask, grad_gate * raw * (1.0 - raw), 0.0)
-    small[1:2] += column_sums(grad_logit)
+    sums[6:7, 128:256] += column_sums(grad_logit)
     grad_logit = grad_logit.astype(bf16)
     map2g[...] += dot(map_hidden.T, grad_logit)
     grad_mpre = dot(grad_logit, m2[...], NT) * map_slope
-    small[0:1] += column_sums(grad_mpre)
+    sums[6:7, 0:128] += column_sums(grad_mpre)
     grad_mpre = grad_mpre.astype(bf16)
-    map1g[...] += dot(grad_mpre.T, act3)
+    sums[16 : 16 + map_size] += dot(grad_mpre.T[:map_size], act3)
     grad_act = dot(grad_mpre, m1[...], NT)
     sums[4:5] += column_sums(grad_act * unit3)
     sums[5:6] += column_sums(grad_act)
-    grad_res2 = norm_back(unit3, scale3, gain3[...], grad_act) + grad_out
+    grad_res2 = norm_back(unit3, scale3, gain3, grad_act) + grad_out
 
     sums[3:4] += column_sums(grad_res2)
     g2 = grad_res2.astype(bf16)
@@ -490,15 +510,18 @@
     for c in range(4):
         cols = slice(c * part, (c + 1) * part)
         grad_pre = dot(g2, w2[cols, :], NT) * slope[:, cols].astype(f32)
-        sums_wide[0:1, cols] += column_sums(grad_pre)
+        sums[8 + c : 9 + c] += column_sums(grad_pre)
         grad_pre = grad_pre.astype(bf16)
-        acc2[:, cols] += dot(g2_t, hidden[:, cols])
-        acc1[:, cols] += dot(act2_t, grad_pre)
+        slope[:, cols] = grad_pre
         more = dot(grad_pre, w1[:, cols], NT)
         grad_act = more if grad_act is None else grad_act + more
+    for c in range(4):
+        cols = slice(c * part, (c + 1) * part)
+        acc1[:, cols] += dot(act2_t, slope[:, cols])
+        acc2[:, cols] += dot(g2_t, hidden[:, cols])
     sums[1:2] += column_sums(grad_act * unit2)
     sums[2:3] += column_sums(grad_act)
-    grad_res1 = norm_back(unit2, scale2, gain2[...], grad_act) + grad_res2
+    grad_res1 = norm_back(unit2, scale2, gain2, grad_act) + grad_res2
 
     sums[0:1] += column_sums(grad_res1)
     g1 = grad_res1.astype(bf16)
@@ -508,53 +531,55 @@
 
     @pl.when(step == pl.num_programs(0) - 1)
     def _():
-        share = stage.shape[1]
-        groups = stage.shape[0]
+        groups, seqs, _, share, thin = weight_grads.shape
+        pending = [[], []]
+        count = 0
 
         def drain(value, *targets):
-            stage[...] = value.astype(bf16).reshape(stage.shape)
-            copies = [pltpu.make_async_copy(stage.at[lo:hi], target, sem) for lo, hi, target in targets]
-            for copy in copies:
+            nonlocal count
+            slot = count % 2
+            count += 1
+            for copy in pending[slot]:
+                copy.wait()
+            stage[slot] = value.astype(bf16).reshape(stage.shape[1:])
+            pending[slot] = [
+                pltpu.make_async_copy(stage.at[slot, lo:hi], target, sems.at[slot, n])
+                for n, (lo, hi, target) in enumerate(targets)
+            ]
+            for copy in pending[slot]:
                 copy.start()
-            for copy in copies:
-                copy.wait()
-
+
+        for t in range(4 * seqs):
+            drain(acc1[:, t * thin : (t + 1) * thin], (0, groups, weight_grads.at[:, t // 4, t % 4]))
         for c in range(4):
             cols = slice(c * part, (c + 1) * part)
-            value1 = acc1[:, cols]
-            value2 = acc2[:, cols].T
-            if groups == 1:
-                drain(value1, (0, 1, weight_grads.at[c : c + 1]))
-                drain(value2, (0, 1, weight_grads.at[4 + c : 5 + c]))
-            else:
-                drain(value1, (0, groups, weight_grads.at[:, c]))
-                drain(value2, *[(4 * i, 4 * i + 4, weight_grads.at[c * groups // 4 + i, 4:8]) for i in range(groups // 4)])
-        if groups == 1:
-            drain(acco[...], (0, 1, weight_grads.at[8:9]))
-        else:
-            drain(acco[...], (0, groups, weight_grads.at[:, 8]))
-
-
-def middle(groups, x, att, *others):
+            for s in range(seqs):
+                value = acc2[s * thin : (s + 1) * thin, cols].T
+                if groups == 1:
+                    drain(value, (0, 1, weight_grads.at[:, s, 4 + c]))
+                else:
+                    few = groups // 4
+                    drain(value, *[(4 * i, 4 * i + 4, weight_grads.at[c * few + i, s, 4:8]) for i in range(few)])
+        for s in range(seqs):
+            drain(acco[:, s * thin : (s + 1) * thin], (0, groups, weight_grads.at[:, s, 8]))
+        pooled_out[...] = (pooled[...] * inverse_row).astype(bf16)
+        for g in range(map_size // 16):
+            sums[16 + map_size :, g * 128 : (g + 1) * 128] = map2g[g * 16 : (g + 1) * 16]
+        for copy in pending[0] + pending[1]:
+            copy.wait()
+
+
+def middle(groups, seqs, map_size, x, att, *others):
     rows, width = x.shape
-    wide = others[8 + 1].shape[1]
-    share = width // groups
-    if share % 16 == 0 and groups % 4 == 0:
-        stage, blocks = (groups, share, width), (groups, 9, share, width)
-    else:
-        stage, blocks = (1, width, width), (9, width, width)
+    wide = others[3].shape[1]
     lanes = others[0].shape[1]
+    if width // groups % 16 or groups % 4 or width // seqs % 128:
+        groups, seqs = 1, 1
+    stage = (2, groups, width // groups, width // seqs)
     size = tile_of(rows, MIDDLE)
     tile = pl.BlockSpec((size, width), lambda i: (i, 0))
     anywhere = pl.BlockSpec(memory_space=pl.ANY)
-    summed = [
-        jax.ShapeDtypeStruct((8, width), f32),
-        jax.ShapeDtypeStruct((8, wide), f32),
-        jax.ShapeDtypeStruct((8, lanes), f32),
-        jax.ShapeDtypeStruct((lanes, width), f32),
-        jax.ShapeDtypeStruct((lanes, lanes), f32),
-        jax.ShapeDtypeStruct((lanes, width), f32),
-    ]
+    summed = [jax.ShapeDtypeStruct((map_size + 32, width), f32), jax.ShapeDtypeStruct((lanes, width), bf16)]
     return pl.pallas_call(
         middle_kernel,
         grid=(rows // size,),
@@ -563,7 +588,7 @@
         out_shape=[
             jax.ShapeDtypeStruct((rows, width), bf16),
             jax.ShapeDtypeStruct((rows, width), bf16),
-            jax.ShapeDtypeStruct(blocks, bf16),
+            jax.ShapeDtypeStruct((groups, seqs, 9, width // groups, width // seqs), bf16),
         ]
         + summed,
         scratch_shapes=[
@@ -572,8 +597,10 @@
             pltpu.VMEM((width, wide), f32),
             pltpu.VMEM((width, wide), f32),
             pltpu.VMEM((width, width), f32),
+            pltpu.VMEM((lanes, width), f32),
+            pltpu.VMEM((lanes, lanes), f32),
             pltpu.VMEM(stage, bf16),
-            pltpu.SemaphoreType.DMA,
+            pltpu.SemaphoreType.DMA((2, max(1, groups // 4))),
         ],
         compiler_params=pltpu.CompilerParams(vmem_limit_bytes=VMEM),
         cost_estimate=pl.CostEstimate(
@@ -583,7 +610,7 @@
     )(x, att, *others)
 
 
-def finish_kernel(place, x, g1, gain, bias, weight, *refs):
+def finish_kernel(place, x, g1, vec, weight, *refs):
     grads, (grad_in, sums) = refs[:-2], refs[-2:]
     parts = len(grads) // 3
     width = x.shape[1]
@@ -606,11 +633,11 @@
             at += share
     sums[0:1] += column_sums(grad_act * unit)
     sums[1:2] += column_sums(grad_act)
-    total = norm_back(unit, scale, gain[...], grad_act) + g1[...].astype(f32)
+    total = norm_back(unit, scale, vec[0:1], grad_act) + g1[...].astype(f32)
     grad_in[...] = total.astype(grad_in.dtype).reshape(grad_in.shape)
 
 
-def finish(start, count, x, g1, gain, bias, weight, grads, place=None, places=0):
+def finish(start, count, x, g1, vec, weight, grads, place=None, places=0):
     width = x.shape[1]
     size = tile_of(count, 256)
     begin = start // size
@@ -633,14 +660,16 @@
         grid_spec=pltpu.PrefetchScalarGridSpec(
             num_scalar_prefetch=1,
             grid=(count // size,),
-            in_specs=[tile] * 2 + [one(o) for o in (gain, bias, weight)] + thin,
+            in_specs=[tile] * 2 + [one(o) for o in (vec, weight)] + thin,
             out_specs=[out[0], pl.BlockSpec((8, width), lambda i, at: (0, 0))],
         ),
         out_shape=[out[1], jax.ShapeDtypeStruct((8, width), f32)],
         compiler_params=pltpu.CompilerParams(vmem_limit_bytes=VMEM),
-        cost_estimate=pl.CostEstimate(flops=1, transcendentals=0, bytes_accessed=1),
+        cost_estimate=pl.CostEstimate(
+            flops=2 * count * width * weight.shape[1] * 2, transcendentals=0, bytes_accessed=count * width * 10
+        ),
         name="finish",
-    )(place.reshape(1), x, g1, gain, bias, weight, *grads)
+    )(place.reshape(1), x, g1, vec, weight, *grads)
 
 
 def shards(
@@ -692,10 +721,10 @@
             return value
         return lax.ppermute(value, "seq", pairs)
 
-    def scatter(whole):
+    def scatter(whole, first=0):
         return [
             send(lax.dynamic_index_in_dim(whole, (position + turn) % clip_count, 0, False), turn)
-            for turn in range(clip_count)
+            for turn in range(first, clip_count)
         ]
 
     def gather_back(parts, kind, whole=None):
@@ -711,9 +740,8 @@
     frames = lax.dynamic_index_in_dim(clip_frames, mine, 0, False)
     rows = clip_count * piece
     keys = group * rows
-    split = piece % 16 == 0 and group == 1
+    split = piece % 16 == 0 and group == 1 and clip_count == 2
     near = piece // TILE * TILE
-    x_parts = scatter(inputs)
     cot = jnp.concatenate(scatter(cot_pooled), axis=0).reshape(clip_count * frames_here * NTOK, width)
 
     def placed(ids, at_seat):
@@ -734,21 +762,30 @@
     wide_mask = jnp.pad(key_mask, (0, up(keys, TILE) - keys), constant_values=masked_score)
     kaug_t = jnp.where(sub16 < 3, 1.0, jnp.where(sub16 == 3, wide_mask[None, :], 0.0)).astype(bf16)
 
-    def line(vector):
-        return vector.reshape(1, -1)
-
-    zeros = jnp.zeros((width,), f32)
-    ones = jnp.ones((width,), f32)
-    col_scale = line(jnp.concatenate([ones * (scaling * LOG2E), ones, ones]))
-    col_bias = line(jnp.concatenate([query_bias * (scaling * LOG2E), zeros, value_bias]))
-    others = (line(norm1_gain), line(norm1_bias), qkv_weight, col_scale, col_bias)
+    vec = jnp.concatenate(
+        [
+            norm1_gain,
+            norm1_bias,
+            out_bias,
+            norm2_gain,
+            norm2_bias,
+            fc2_bias,
+            learn_gain,
+            learn_bias,
+            query_bias,
+            value_bias,
+            fc1_bias,
+        ]
+    ).reshape(-1, width)
     begun = ()
     if split:
-        held = project(0, rows, x_parts[0], others)
+        (x_far,) = scatter(inputs, 1)
+        held = project(0, rows, inputs, position % clip_count, vec, qkv_weight)
         held, begun = lax.optimization_barrier((held, (attend_near(near, held[0], kaug),)))
-        mixed, act1, x_low = project(piece, rows, jnp.concatenate(x_parts[1:], axis=0), others, held)
+        mixed, act1, x_low = project(piece, rows, x_far[None], jnp.int32(0), vec, qkv_weight, held)
     else:
-        mixed, act1, x_low = project(0, rows, jnp.concatenate(x_parts, axis=0), others)
+        x_all = jnp.concatenate(scatter(inputs), axis=0)[None]
+        mixed, act1, x_low = project(0, rows, x_all, jnp.int32(0), vec, qkv_weight)
     if group == 1:
         keys_values, act_keys = mixed, act1
     else:
@@ -782,18 +819,14 @@
     map1_wide = jnp.pad(map1_weight, ((0, 0), (0, lanes - map_size)))
     map2_wide = jnp.pad(jnp.tile(map2_weight, (1, lanes // NTOK)), ((0, lanes - map_size), (0, 0)))
     cot = jnp.pad(cot, ((0, lanes - slots), (0, 0)))
-    grad_att, grad_low, weight_part, sums, sums_wide, small, map1_part, map2_part, pooled = middle(
+    grad_att, grad_low, weight_part, early, pooled = middle(
         clip_size,
+        seq_size,
+        map_size,
         x_low,
         att,
         aux,
-        line(out_bias),
-        line(norm2_gain),
-        line(norm2_bias),
-        line(fc1_bias),
-        line(fc2_bias),
-        line(learn_gain),
-        line(learn_bias),
+        vec,
         out_weight,
         fc1_weight,
         fc2_weight,
@@ -805,21 +838,6 @@
     def over_clip(matrix):
         return lax.psum_scatter(matrix, "clip", scatter_dimension=0, tiled=True)
 
-    def over_seq(*matrices):
-        thin = width // seq_size
-        blocks = [
-            m.reshape(m.shape[0], seq_size, -1, thin).transpose(1, 0, 2, 3).reshape(seq_size, -1, thin)
-            for m in matrices
-        ]
-        total = lax.psum_scatter(jnp.concatenate(blocks, axis=1), "seq", scatter_dimension=0, tiled=False)
-        outs = []
-        at = 0
-        for m, block in zip(matrices, blocks):
-            count = block.shape[1]
-            outs.append(total[at : at + count].reshape(m.shape[0], -1).astype(f32))
-            at += count
-        return outs
-
     def bits(size):
         return [1 << n for n in range(size.bit_length() - 1)]
 
@@ -848,36 +866,25 @@
 
     tie = lax.optimization_barrier
     pairs = (4, 2)
-    early = jnp.concatenate(
-        [
-            sums.reshape(-1),
-            sums_wide[0],
-            small.reshape(-1) * jnp.repeat(jnp.stack([1.0, 1.0, inverse * inverse] + [1.0] * 5), lanes),
-            map1_part[:map_size].reshape(-1),
-            jnp.sum(map2_part[:map_size].reshape(map_size, lanes // NTOK, NTOK), axis=1).reshape(-1),
-        ]
-    )
     share = width // clip_size
-    if weight_part.ndim == 3:
-        fc1_part = weight_part[:4].reshape(4, clip_size, share, width).transpose(1, 0, 2, 3)
-        fc2_part = weight_part[4:8].reshape(clip_size, 4, share, width)
-        weight_part = jnp.concatenate([fc1_part, fc2_part, weight_part[8].reshape(clip_size, 1, share, width)], axis=1)
+    thin = width // seq_size
+    if weight_part.shape[0] == 1:
+        fc1_part = weight_part[0, 0, :4].transpose(1, 0, 2).reshape(clip_size, share, seq_size, 4, thin)
+        fc2_part = weight_part[0, 0, 4:8].reshape(clip_size, 4, share, seq_size, thin).transpose(0, 3, 1, 2, 4)
+        out_part = weight_part[0, 0, 8].reshape(clip_size, 1, share, seq_size, thin).transpose(0, 3, 1, 2, 4)
+        weight_part = jnp.concatenate([fc1_part.transpose(0, 2, 3, 1, 4), fc2_part, out_part], axis=2)
     slab = over_clip(weight_part)[0]
     near_early = meet(early, early_steps[0])
     back0 = back(0, pairs[0], mixed)
     mixed, slab, early, near_early, back0 = tie((mixed, slab, early, near_early, back0))
     early = early + near_early
     near_early = meet(early, early_steps[1])
-    fc1_grad, fc2_grad, out_grad = over_seq(
-        slab[:4].transpose(1, 0, 2).reshape(share, 4 * width), slab[4:8].reshape(4 * share, width), slab[8]
-    )
+    slab = lax.psum_scatter(slab, "seq", scatter_dimension=0, tiled=False)
     slab0 = over_clip(back0[3])
     back1 = back(pairs[0], pairs[1], mixed)
-    fc1_grad, fc2_grad, out_grad, slab0, early, near_early, back1 = tie(
-        (fc1_grad, fc2_grad, out_grad, slab0, early, near_early, back1)
-    )
+    slab, slab0, early, near_early, back1 = tie((slab, slab0, early, near_early, back1))
     early = early + near_early
-    pooled = (pooled[:slots] * inverse).astype(bf16).reshape(clip_count, frames_here, NTOK, width)
+    pooled = pooled[:slots].reshape(clip_count, frames_here, NTOK, width)
     pooled = gather_back([pooled[t] for t in range(clip_count)], bf16)
 
     grads = [list(one[:3]) for one in (back0, back1)]
@@ -893,32 +900,45 @@
                 grads[n][i] = both[:, at : at + pairs[n] * 128]
                 at += pairs[n] * 128
     grads = [grad for one in grads for grad in one]
-    rest = (grad_low, line(norm1_gain), line(norm1_bias), qkv_weight, grads)
+    rest = (grad_low, vec, qkv_weight, grads)
     near_early = meet(early, early_steps[2])
     kept, received = part_ways(back1[3].reshape(clip_size, share, -1), clip_steps[0])
     if split:
-        far, late = finish(piece, rows - piece, x_low, *rest)
-        far = [far[t * piece : (t + 1) * piece] for t in range(clip_count - 1)]
-        far, x_low, late, near_early, received = tie((far, x_low, late, near_early, received))
+        size = tile_of(piece, 256)
+        lead = -(-piece // size // 2) * size
+        far0, sums0 = finish(piece, lead, x_low, *rest)
+        far0, sums0, x_low, near_early, received = tie((far0, sums0, x_low, near_early, received))
+        home0 = send(far0, 1, True)
     early = early + near_early
     near_early = meet(early, early_steps[3])
     kept, received = part_ways(add_low(kept, received), clip_steps[1])
     if split:
-        local, local_sums = finish(0, piece, x_low, *rest, place=position % clip_count, places=clip_count)
-        local, local_sums, near_early, received = tie((local, local_sums, near_early, received))
-        input_grad = gather_back([None] + far, f32, local)
-        late = (local_sums + late)[:4]
+        far1, sums1 = finish(piece + lead, piece - lead, x_low, *rest)
+        far1, sums1, x_low, near_early, received = tie((far1, sums1, x_low, near_early, received))
+        home1 = send(far1, 1, True)
+    early = early + near_early
+    near_early = meet(early, early_steps[4])
+    kept, received = part_ways(add_low(kept, received), clip_steps[2])
+    if split:
+        input_grad, late = finish(0, piece, x_low, *rest, place=position % clip_count, places=clip_count)
+        input_grad, late, near_early, received, home0 = tie((input_grad, late, near_early, received, home0))
+        other = (position + 1) % clip_count
+        input_grad = lax.dynamic_update_slice(input_grad, home0.astype(f32)[None], (other, 0, 0))
+        late = late + sums0 + sums1
     else:
         local, late = finish(0, rows, x_low, *rest)
         input_grad = gather_back([local[t * piece : (t + 1) * piece] for t in range(clip_count)], f32)
-        late = late[:4]
     early = early + near_early
-    for step in early_steps[4:]:
+    for step in early_steps[5:]:
         early = early + meet(early, step)
     slab1 = add_low(kept, received)
-    for step in clip_steps[2:]:
+    for step in clip_steps[3:]:
         slab1 = add_low(*part_ways(slab1, step))
-    for step in clip_steps + seq_steps:
+    late = late[:4]
+    for step in clip_steps:
+        late = late + meet(late, step)
+    late, slab1, slab, early = tie((late, slab1, slab, early))
+    for step in seq_steps:
         late = late + meet(late, step)
     qkv = [
         part.reshape(share, count, 3, 128).transpose(0, 2, 1, 3) for part, count in zip((slab0, slab1), pairs)
@@ -927,19 +947,18 @@
     for step in seq_steps:
         qkv = add_low(*part_ways(qkv, step))
     qkv_grad = qkv[0].astype(f32)
-
-    at = 0
-    taken = []
-    for size in (sums.size, sums_wide.shape[1], small.size, map_size * width, map_size * NTOK):
-        taken.append(early[at : at + size])
-        at += size
-    sums, fc1_bias_grad, small, map1_grad, map2_grad = taken
-    sums = sums.reshape(8, width)
-    small = small.reshape(8, lanes)
-    map1_grad = map1_grad.reshape(map_size, width).T
-    map2_grad = map2_grad.reshape(map_size, NTOK)
-    map2_bias_grad = jnp.sum(small[1].reshape(lanes // NTOK, NTOK), axis=0)
-    penalty = jnp.sum(small[2]) / pair_count / slots_all
+    if split:
+        input_grad = lax.dynamic_update_slice(input_grad, home1.astype(f32)[None], (other, lead, 0))
+    fc1_grad = slab[:4].transpose(1, 0, 2).reshape(share, 4 * thin).astype(f32)
+    fc2_grad = slab[4:8].reshape(4 * share, thin).astype(f32)
+    out_grad = slab[8].astype(f32)
+
+    small = early[6]
+    map1_grad = early[16 : 16 + map_size].T
+    map2_grad = early[16 + map_size :, : map_size // 16 * lanes].reshape(16, map_size // 16, lanes // NTOK, NTOK)
+    map2_grad = jnp.sum(map2_grad, axis=2).transpose(1, 0, 2).reshape(map_size, NTOK)
+    map2_bias_grad = jnp.sum(small[128:256].reshape(-1, NTOK), axis=0)
+    penalty = jnp.sum(small[256:384]) / pair_count / slots_all
     return (
         pooled,
         penalty,
@@ -950,17 +969,17 @@
         late[2],
         late[3],
         out_grad,
-        sums[0],
-        sums[1],
-        sums[2],
+        early[0],
+        early[1],
+        early[2],
         fc1_grad,
-        fc1_bias_grad,
+        early[8:12].reshape(-1),
         fc2_grad,
-        sums[3],
-        sums[4],
-        sums[5],
+        early[3],
+        early[4],
+        early[5],
         map1_grad,
-        small[0, :map_size],
+        small[:map_size],
         map2_grad,
         map2_bias_grad,
     )

time: 867 us -> 811 us (0.935)
  waiting for transfers between devices: 47.4 us -> 18.1 us
  local copies, waits for them, and re-layouts: 34.4 us -> 19.8 us
  Pallas kernels: 717 us -> 707 us
    ppermute x15, waiting for transfers between devices: 47.3 us -> 3.34 us  [meet(): lax.ppermute(value, axis, [(i, i ^ bit) for i in range(lax.axis_size(axis...]
    ppermute x4 -> x5, waiting for transfers between devices: 0.01 us -> 14.7 us  [send(): return lax.ppermute(value, 'seq', pairs)]
    pallas_call x1, Pallas kernels: 197 us -> 184 us  [middle(): pl.pallas_call(middle_kernel, grid=(rows // size,), in_specs=[tile, tile]...]
    pallas_call x2 -> x3, Pallas kernels: 30 us -> 33.5 us  [finish(): pl.pallas_call(finish_kernel, grid_spec=pltpu.PrefetchScalarGridSpec(num_...]
  transfers between devices with their start and end apart: 22 -> 23, of which waited for: 5 -> 7; matrix products, arithmetic and copies ran while one was open for 5% -> 3% of each run, Pallas kernels for 46% -> 49%
where the time goes in v3:
time: 811 us; the launch traced here: 804 us
  Pallas kernels  707 us (87%)
  starting transfers between devices  24.6 us (3%)
  local copies, waits for them, and re-layouts  19.8 us (2%)
  waiting for transfers between devices  18.1 us (2%)
  between operations  17.4 us (2%)
  other arithmetic  16.2 us (2%)
    pallas_call x2, Pallas kernels, attend_back(): pl.pallas_call(attend_back_kernel, grid=(pairs, rows // size), in_specs=[...  318 us
    pallas_call x1, Pallas kernels, middle(): pl.pallas_call(middle_kernel, grid=(rows // size,), in_specs=[tile, tile]...  184 us
    pallas_call x1, Pallas kernels, attend(): pl.pallas_call(attend_kernel, grid=(pairs,), in_specs=[pl.BlockSpec((rows...  115 us
    pallas_call x3, Pallas kernels, finish(): pl.pallas_call(finish_kernel, grid_spec=pltpu.PrefetchScalarGridSpec(num_...  33.5 us
    pallas_call x1, Pallas kernels, attend_near(): pl.pallas_call(attend_near_kernel, grid=(pairs,), in_specs=[pl.BlockSpec(...  33.3 us
    pallas_call x2, Pallas kernels, project(): pl.pallas_call(project_kernel, grid_spec=pltpu.PrefetchScalarGridSpec(num...  23.3 us
    ppermute x15, starting transfers between devices, meet(): lax.ppermute(value, axis, [(i, i ^ bit) for i in range(lax.axis_size(axis...  17.5 us
  transfers between devices with their start and end apart: 23, of which 7 were waited for; matrix products, arithmetic and copies ran while one was open for 3% of the time, Pallas kernels for 49%

profile of v3, /device:TPU:0, one launch (start us, length us, event | category | flops | bytes accessed | tf_op | source)
XLA Modules:
  0.0 803.7 jit_solution(5271461816382007219)
XLA Ops:
  7.4 3.3 dynamic-slice_bitcast_fusion
  10.7 3.0 collective-permute-start
  14.0 0.6 reshape.338.vec
  14.7 0.6 dynamic_slice.47
  15.3 0.6 dynamic_slice.46
  16.5 1.3 fusion.17
  18.3 1.1 concatenate.13.kaug
  19.4 11.7 %project.2 = (bf16[3136,2304]{1,0:T(8,128)(2,1)}, bf16[3136,768]{1,0:T(8,128)(2,1)}, bf16[3136,768]{1,0:T(8,128)(2,1)}) custom-call(s32[1]{0:T(128)} %bitcast.2.place, bf16[2,1568,768]{2,1,0:T(8,128)(2,1)} %x.11, f32[14,768]{1,0:T(8,128)} %reshape.338.vec, bf16[768,2304]{1,0:T(8,128)(2,1)} %weight.9), custom_call_target="tpu_custom_call" | custom-call | tf_op jit(solution)/shard_map/project/pallas_call | solution.py:423
  31.1 33.3 %attend_near.1.refs_0_ = f32[12,80,1536]{2,1,0:T(8,128)} custom-call(bf16[3136,2304]{1,0:T(8,128)(2,1)} %get-tuple-element.91.q.k.v.refs_0_, bf16[3136,2304]{1,0:T(8,128)(2,1)} %get-tuple-element.91.q.k.v.refs_0_, bf16[3136,2304]{1,0:T(8,128)(2,1)} %get-tuple-element.91.q.k.v.refs_0_, bf16[3136,128]{1,0:T(8,128)(2,1)} %concatenate.13.kaug), custom_call_target="tpu_custom_call" | custom-call | flops 28991029248 | bytes 11796480 | tf_op jit(solution)/shard_map/attend_near/pallas_call | solution.py:117
  64.7 0.7 pad.18.m1
  65.6 0.6 pad.19.m2
  66.2 1.3 fusion.23
  67.6 0.6 stack.12.aux
  68.3 0.7 maximum_bitcast_fusion.cot
  69.0 1.4 copy-done.2
  70.4 11.7 %project.3 = (bf16[3136,2304]{1,0:T(8,128)(2,1)}, bf16[3136,768]{1,0:T(8,128)(2,1)}, bf16[3136,768]{1,0:T(8,128)(2,1)}) custom-call(s32[1]{0:T(128)} %constant.255.clone.1.place, bf16[1,1568,768]{2,1,0:T(8,128)(2,1)} %bitcast.78, f32[14,768]{1,0:T(8,128)} %reshape.338.vec, ...), custom_call_target="tpu_custom_call", output_to_operand_aliasing={{0}: (4, {}), {1}: (5, {}), {2}: (6, {})} | custom-call | tf_op jit(solution)/shard_map/project/pallas_call | solution.py:423
  82.1 114.5 %attend.1 = (bf16[3136,768]{1,0:T(8,128)(2,1)}, bf16[3136,768]{1,0:T(8,128)(2,1)}) custom-call(bf16[3136,2304]{1,0:T(8,128)(2,1)} %get-tuple-element.116.q.k.v, bf16[3136,2304]{1,0:T(8,128)(2,1)} %get-tuple-element.116.q.k.v, bf16[3136,2304]{1,0:T(8,128)(2,1)} %get-tuple-element.116.q.k.v, bf16[3136,128]{1,0:T(8,128)(2,1)} %concatenate.13.kaug, ...), custom_call_target="tpu_custom_call" | custom-call | flops 120846286848 | bytes 24084480 | tf_op jit(solution)/shard_map/attend/pallas_call | solution.py:204
  196.6 184.5 %middle.1 = (bf16[3136,768]{1,0:T(8,128)(2,1)}, bf16[3136,768]{1,0:T(8,128)(2,1)}, bf16[16,2,9,48,384]{4,3,2,1,0:T(8,128)(2,1)}, f32[96,768]{1,0:T(8,128)}, bf16[128,768]{1,0:T(8,128)(2,1)}) custom-call(bf16[3136,768]{1,0:T(8,128)(2,1)} %get-tuple-element.134.x, bf16[3136,768]{1,0:T(8,128)(2,1)} %get-tuple-element.97.att, f32[8,128]{1,0:T(8,128)} %stack.12.aux, ...), custom_call_target="tpu_custom_call" | custom-call | flops 99883155456 | bytes 28901376 | tf_op jit(solution)/shard_map/middle/pallas_call | solution.py:583
  381.2 0.6 copy-done.10
  381.8 0.7 select_convert_fusion.1.kaug_t
  382.5 210.1 %attend_back.2 = (bf16[3136,512]{1,0:T(8,128)(2,1)}, bf16[3136,512]{1,0:T(8,128)(2,1)}, bf16[3136,512]{1,0:T(8,128)(2,1)}, bf16[768,1536]{1,0:T(8,128)(2,1)}) custom-call(bf16[3136,2304]{1,0:T(8,128)(2,1)} %get-tuple-element.116.q.k.v, bf16[3136,768]{1,0:T(8,128)(2,1)} %get-tuple-element.102.do, bf16[3136,768]{1,0:T(8,128)(2,1)} %get-tuple-element.97.att, ...), custom_call_target="tpu_custom_call" | custom-call | flops 157351936000 | bytes 48168960 | tf_op jit(solution)/shard_map/attend_back/pallas_call | solution.py:325
  592.9 2.0 collective-permute-start.2
  594.9 0.7 broadcast_in_dim.107
  595.6 0.6 bitcast_dynamic-update-slice_fusion.1
  596.2 2.1 collective-permute-done.2
  598.3 0.6 bitcast_dynamic-update-slice_fusion
  599.0 1.1 add.257
  600.0 1.8 collective-permute-start.4
  601.9 108.2 %attend_back.3 = (bf16[3136,256]{1,0:T(8,128)(2,1)}, bf16[3136,256]{1,0:T(8,128)(2,1)}, bf16[3136,256]{1,0:T(8,128)(2,1)}, bf16[768,768]{1,0:T(8,128)(2,1)}) custom-call(bf16[3136,2304]{1,0:T(8,128)(2,1)} %get-tuple-element.116.q.k.v, bf16[3136,768]{1,0:T(8,128)(2,1)} %get-tuple-element.102.do, bf16[3136,768]{1,0:T(8,128)(2,1)} %get-tuple-element.97.att, ...), custom_call_target="tpu_custom_call" | custom-call | flops 78675968000 | bytes 48168960 | tf_op jit(solution)/shard_map/attend_back/pallas_call | solution.py:325
  710.2 1.6 collective-permute-start.5
  711.7 1.1 dynamic-slice_bitcast_fusion.1
  712.9 10.0 %finish.3 = (bf16[896,768]{1,0:T(8,128)(2,1)}, f32[8,768]{1,0:T(8,128)}) custom-call(s32[1]{0:T(128)} %constant.255.clone.1.place, bf16[3136,768]{1,0:T(8,128)(2,1)} %get-tuple-element.134.x, bf16[3136,768]{1,0:T(8,128)(2,1)} %get-tuple-element.99.g1, f32[14,768]{1,0:T(8,128)} %reshape.338.vec, bf16[768,2304]{1,0:T(8,128)(2,1)} %weight.9, ...), custom_call_target="tpu_custom_call" | custom-call | flops 6341787648 | bytes 6881280 | tf_op jit(solution)/shard_map/finish/pallas_call | solution.py:658
  723.2 1.6 collective-permute-start.7
  724.8 1.2 fusion
  726.1 0.6 collective-permute-start.8
  726.7 0.5 collective-permute-start.11
  727.2 8.6 %finish.4 = (bf16[672,768]{1,0:T(8,128)(2,1)}, f32[8,768]{1,0:T(8,128)}) custom-call(s32[1]{0:T(128)} %constant.255.clone.1.place, bf16[3136,768]{1,0:T(8,128)(2,1)} %get-tuple-element.134.x, bf16[3136,768]{1,0:T(8,128)(2,1)} %get-tuple-element.99.g1, f32[14,768]{1,0:T(8,128)} %reshape.338.vec, bf16[768,2304]{1,0:T(8,128)(2,1)} %weight.9, ...), custom_call_target="tpu_custom_call" | custom-call | flops 4756340736 | bytes 5160960 | tf_op jit(solution)/shard_map/finish/pallas_call | solution.py:658
  735.8 1.0 add.266
  736.8 2.7 collective-permute-start.9
  740.1 1.5 collective-permute-start.17
  741.6 14.9 %finish.5 = (f32[2,1568,768]{2,1,0:T(8,128)}, f32[8,768]{1,0:T(8,128)}) custom-call(s32[1]{0:T(128)} %bitcast.2.place, bf16[3136,768]{1,0:T(8,128)(2,1)} %get-tuple-element.134.x, bf16[3136,768]{1,0:T(8,128)(2,1)} %get-tuple-element.99.g1, f32[14,768]{1,0:T(8,128)} %reshape.338.vec, bf16[768,2304]{1,0:T(8,128)(2,1)} %weight.9, ...), custom_call_target="tpu_custom_call" | custom-call | flops 11098128384 | bytes 12042240 | tf_op jit(solution)/shard_map/finish/pallas_call | solution.py:658
  756.5 3.4 collective-permute-done.11
  759.9 0.7 slice_add_fusion
  760.7 1.1 collective-permute-done.12
  761.9 1.5 collective-permute-start.13
  763.4 2.6 collective-permute-start.16
  766.5 1.7 convert_dynamic-update-slice_fusion
  768.2 1.7 collective-permute-done.14
  769.9 2.0 collective-permute-start.15
  771.9 9.1 %collective-permute-done.17 = bf16[672,768]{1,0:T(8,128)(2,1)S(1)} collective-permute-done((bf16[672,768]{1,0:T(8,128)(2,1)}, bf16[672,768]{1,0:T(8,128)(2,1)S(1)}, u32[]{:S(2)}, u32[]{:S(2)}) %collective-permute-start.17) | collective-permute-done | bytes 1032224 | tf_op jit(solution)/shard_map/ppermute | solution.py:722
  781.0 1.5 convert_dynamic-update-slice_fusion.1
  782.5 1.0 add.283
  783.6 0.6 bitcast_convert_fusion.1
  784.2 0.6 slice_reduce_fusion.4
  784.9 0.7 slice_bitcast_fusion
  787.1 0.7 bitcast_convert_fusion
  788.1 0.6 slice_reduce_fusion.10
  788.7 1.5 collective-permute-start.19
  790.2 0.7 copy.82
  790.9 0.6 reshape.346
  791.7 0.7 reshape.348
  792.4 0.5 reduce_sum.29
  793.7 0.6 slice_reduce_fusion
  795.1 0.7 copy.84
  (141 shorter events, 5.8 us)
Async XLA Ops:
  7.2 58.3 %copy-start = (bf16[64,8]{0,1:T(8,128)(2,1)S(1)}, bf16[64,8]{0,1:T(8,128)(2,1)}, u32[]{:S(2)}) copy-start(bf16[64,8]{0,1:T(8,128)(2,1)} %param.43) | copy-start | bytes 3076
  7.2 6.5 copy-start.5
  7.2 6.6 copy-start.14
  7.2 6.6 copy-start.15
  7.2 6.6 copy-start.16
  7.3 6.6 copy-start.17
  7.3 6.6 copy-start.18
  7.3 6.6 copy-start.19
  7.3 6.6 copy-start.20
  7.3 6.7 copy-start.21
  7.3 6.7 copy-start.22
  7.3 6.7 copy-start.23
  7.3 6.7 copy-start.11
  7.3 7.3 copy-start.25
  7.3 7.9 copy-start.26
  7.4 585.3 %reduce-scatter.4.cloned.1.call-start = ((), (), s32[]{:S(2)}) async-start(), calls=%async_computation.3 | async-start | bytes 11280384 | tf_op jit(solution)/shard_map/reduce_scatter | solution.py:839
  10.7 58.3 %collective-permute-start = (bf16[1568,768]{1,0:T(8,128)(2,1)}, bf16[1568,768]{1,0:T(8,128)(2,1)S(1)}, u32[]{:S(2)}, u32[]{:S(2)}) collective-permute-start(bf16[1568,768]{1,0:T(8,128)(2,1)} %dynamic-slice_bitcast_fusion), channel_id=1, source_target_pairs={{0,1},{1,0},{2,3},{3,2},{4,5},{5,4},{6,7},{7,6},{8,9},{9,8},{10,11... | collective-permute-start | bytes 7225352 | tf_op jit(solution)/shard_map/ppermute | solution.py:722
  13.7 54.6 %collective-permute-start.1 = (bf16[8,8,768]{2,1,0:T(8,128)(2,1)S(1)}, bf16[8,8,768]{2,1,0:T(8,128)(2,1)S(1)}, u32[]{:S(2)}, u32[]{:S(2)}) collective-permute-start(bf16[8,8,768]{2,1,0:T(8,128)(2,1)S(1)} %get-tuple-element.169), channel_id=1, source_target_pairs={{0,1},{1,0},{2,3},{3,2},{4,5},{5,4},{6,7},{7,6},{8,9},{9,8},{10,11... | collective-permute-start | bytes 294920 | tf_op jit(solution)/shard_map/ppermute | solution.py:722
  17.8 13.2 %copy-start.9 = (bf16[3136]{0:T(1024)(128)(2,1)}, bf16[3136]{0:T(1024)(128)(2,1)S(1)}, u32[]{:S(2)}) copy-start(bf16[3136]{0:T(1024)(128)(2,1)S(1)} %fusion.17) | copy-start | bytes 18820
  31.1 33.4 %copy-start.24 = (f32[8]{0:T(128)S(1)}, f32[8]{0:T(128)}, u32[]{:S(2)}) copy-start(f32[8]{0:T(128)} %param.44) | copy-start | bytes 100
  31.1 33.5 %copy-start.8 = (bf16[768,64]{0,1:T(8,128)(2,1)S(1)}, bf16[768,64]{0,1:T(8,128)(2,1)}, u32[]{:S(2)}) copy-start(bf16[768,64]{0,1:T(8,128)(2,1)} %param.41) | copy-start | bytes 294916
  31.1 36.4 %copy-start.27 = (f32[64]{0:T(128)S(1)}, f32[64]{0:T(128)}, u32[]{:S(2)}) copy-start(f32[64]{0:T(128)} %param.42) | copy-start | bytes 772
  69.0 1.4 copy-start.2
  381.1 0.7 copy-start.10
  381.1 329.0 %reduce-scatter.6.cloned.1.call-start = ((), (), s32[]{:S(2)}) async-start(), calls=%async_computation.4 | async-start | bytes 995328 | tf_op jit(solution)/shard_map/reduce_scatter | solution.py:882
  382.5 210.1 %collective-permute-start.3 = (f32[96,768]{1,0:T(8,128)}, f32[96,768]{1,0:T(8,128)}, u32[]{:S(2)}, u32[]{:S(2)}) collective-permute-start(f32[96,768]{1,0:T(8,128)} %get-tuple-element.114), channel_id=1, source_target_pairs={{0,2},{2,0},{4,6},{6,4},{8,10},{10,8},{12,14},{14,12},{16,18},{18,... | collective-permute-start | bytes 884744 | tf_op jit(solution)/shard_map/ppermute | solution.py:850
  382.5 210.4 %copy-start.6 = (bf16[128,768]{1,0:T(8,128)(2,1)S(1)}, bf16[128,768]{1,0:T(8,128)(2,1)}, u32[]{:S(2)}) copy-start(bf16[128,768]{1,0:T(8,128)(2,1)} %get-tuple-element.98) | copy-start | bytes 589828
  592.7 117.4 %reduce-scatter.8.cloned.1.call-start = ((), (), s32[]{:S(2)}) async-start(), calls=%async_computation.5 | async-start | bytes 2506752 | tf_op jit(solution)/shard_map/reduce_scatter | solution.py:839
  592.9 5.4 collective-permute-start.2
  600.0 110.0 %collective-permute-start.4 = (f32[96,768]{1,0:T(8,128)S(1)}, f32[96,768]{1,0:T(8,128)S(1)}, u32[]{:S(2)}, u32[]{:S(2)}) collective-permute-start(f32[96,768]{1,0:T(8,128)S(1)} %add.257), channel_id=1, source_target_pairs={{0,1},{1,0},{2,3},{3,2},{4,5},{5,4},{6,7},{7,6},{8,9},{9,8},{10,11... | collective-permute-start | bytes 884744 | tf_op jit(solution)/shard_map/ppermute | solution.py:850
  710.2 12.9 %collective-permute-start.5 = (f32[96,768]{1,0:T(8,128)S(1)}, f32[96,768]{1,0:T(8,128)S(1)}, u32[]{:S(2)}, u32[]{:S(2)}) collective-permute-start(f32[96,768]{1,0:T(8,128)S(1)} %add.258), channel_id=1, source_target_pairs={{0,4},{2,6},{4,0},{6,2},{8,12},{10,14},{12,8},{14,10},{16,20},{18,... | collective-permute-start | bytes 884744 | tf_op jit(solution)/shard_map/ppermute | solution.py:850
  712.8 10.3 %collective-permute-start.6 = (bf16[8,48,768]{2,1,0:T(8,128)(2,1)S(1)}, bf16[8,48,768]{2,1,0:T(8,128)(2,1)}, u32[]{:S(2)}, u32[]{:S(2)}) collective-permute-start(bf16[8,48,768]{2,1,0:T(8,128)(2,1)S(1)} %dynamic-slice_bitcast_fusion.1), channel_id=1, source_target_pairs={{0,2},{2,0},{4,6},{6,4},{8,10},{10,8},{12,14},{14,12},{16,18},{18,... | collective-permute-start | bytes 1769480 | tf_op jit(solution)/shard_map/ppermute | solution.py:850
  712.9 10.1 %copy-start.7 = (bf16[48,1536]{1,0:T(8,128)(2,1)S(1)}, bf16[48,1536]{1,0:T(8,128)(2,1)}, u32[]{:S(2)}) copy-start(bf16[48,1536]{1,0:T(8,128)(2,1)} %reduce-scatter.8.cloned.1.call-done) | copy-start | bytes 442372
  712.9 11.9 %copy-start.3 = (bf16[768,768]{1,0:T(8,128)(2,1)S(1)}, bf16[768,768]{1,0:T(8,128)(2,1)}, u32[]{:S(2)}) copy-start(bf16[768,768]{1,0:T(8,128)(2,1)} %get-tuple-element.128) | copy-start | bytes 3538948
  723.2 12.6 %collective-permute-start.7 = (f32[96,768]{1,0:T(8,128)S(1)}, f32[96,768]{1,0:T(8,128)}, u32[]{:S(2)}, u32[]{:S(2)}) collective-permute-start(f32[96,768]{1,0:T(8,128)S(1)} %add.261), channel_id=1, source_target_pairs={{0,8},{2,10},{4,12},{6,14},{8,0},{10,2},{12,4},{14,6},{16,24},{18,... | collective-permute-start | bytes 884744 | tf_op jit(solution)/shard_map/ppermute | solution.py:850
  726.1 9.7 %collective-permute-start.8 = (bf16[4,48,768]{2,1,0:T(8,128)(2,1)S(1)}, bf16[4,48,768]{2,1,0:T(8,128)(2,1)S(1)}, u32[]{:S(2)}, u32[]{:S(2)}) collective-permute-start(bf16[4,48,768]{2,1,0:T(8,128)(2,1)S(1)} %dynamic-slice_bitcast_fusion.2), channel_id=1, source_target_pairs={{0,4},{2,6},{4,0},{6,2},{8,12},{10,14},{12,8},{14,10},{16,20},{18,... | collective-permute-start | bytes 884744 | tf_op jit(solution)/shard_map/ppermute | solution.py:850
  726.7 33.3 %collective-permute-start.11 = (bf16[896,768]{1,0:T(8,128)(2,1)}, bf16[896,768]{1,0:T(8,128)(2,1)S(1)}, u32[]{:S(2)}, u32[]{:S(2)}) collective-permute-start(bf16[896,768]{1,0:T(8,128)(2,1)} %get-tuple-element.139), channel_id=1, source_target_pairs={{1,0},{0,1},{3,2},{2,3},{5,4},{4,5},{7,6},{6,7},{9,8},{8,9},{11,10... | collective-permute-start | bytes 4128776 | tf_op jit(solution)/shard_map/ppermute | solution.py:722
  736.8 19.7 %collective-permute-start.9 = (f32[96,768]{1,0:T(8,128)S(1)}, f32[96,768]{1,0:T(8,128)}, u32[]{:S(2)}, u32[]{:S(2)}) collective-permute-start(f32[96,768]{1,0:T(8,128)S(1)} %add.266), channel_id=1, source_target_pairs={{0,16},{2,18},{4,20},{6,22},{8,24},{10,26},{12,28},{14,30},{16,0},... | collective-permute-start | bytes 884744 | tf_op jit(solution)/shard_map/ppermute | solution.py:850
  739.6 20.4 %copy-start.12 = (f32[8,768]{1,0:T(8,128)S(1)}, f32[8,768]{1,0:T(8,128)}, u32[]{:S(2)}) copy-start(f32[8,768]{1,0:T(8,128)} %get-tuple-element.141) | copy-start | bytes 73732
  739.6 20.3 %copy-start.13 = (f32[8,768]{1,0:T(8,128)S(1)}, f32[8,768]{1,0:T(8,128)}, u32[]{:S(2)}) copy-start(f32[8,768]{1,0:T(8,128)} %get-tuple-element.142) | copy-start | bytes 73732
  739.6 16.9 %collective-permute-start.10 = (bf16[2,48,768]{2,1,0:T(8,128)(2,1)S(1)}, bf16[2,48,768]{2,1,0:T(8,128)(2,1)S(1)}, u32[]{:S(2)}, u32[]{:S(2)}) collective-permute-start(bf16[2,48,768]{2,1,0:T(8,128)(2,1)S(1)} %dynamic-slice_bitcast_fusion.4), channel_id=1, source_target_pairs={{0,8},{2,10},{4,12},{6,14},{8,0},{10,2},{12,4},{14,6},{16,24},{18,... | collective-permute-start | bytes 442376 | tf_op jit(solution)/shard_map/ppermute | solution.py:850
  740.1 40.9 %collective-permute-start.17 = (bf16[672,768]{1,0:T(8,128)(2,1)}, bf16[672,768]{1,0:T(8,128)(2,1)S(1)}, u32[]{:S(2)}, u32[]{:S(2)}) collective-permute-start(bf16[672,768]{1,0:T(8,128)(2,1)} %get-tuple-element.149), channel_id=1, source_target_pairs={{1,0},{0,1},{3,2},{2,3},{5,4},{4,5},{7,6},{6,7},{9,8},{8,9},{11,10... | collective-permute-start | bytes 3096584 | tf_op jit(solution)/shard_map/ppermute | solution.py:722
  760.7 1.2 collective-permute-start.12
  761.9 4.1 collective-permute-start.13
  763.4 20.2 %collective-permute-start.16 = (bf16[1,48,768]{2,1,0:T(8,128)(2,1)S(1)}, bf16[1,48,768]{2,1,0:T(8,128)(2,1)S(1)}, u32[]{:S(2)}, u32[]{:S(2)}) collective-permute-start(bf16[1,48,768]{2,1,0:T(8,128)(2,1)S(1)} %constant_dynamic-slice_fusion), channel_id=1, source_target_pairs={{0,16},{2,18},{4,20},{6,22},{8,24},{10,26},{12,28},{14,30},{16,0},... | collective-permute-start | bytes 221192 | tf_op jit(solution)/shard_map/ppermute | solution.py:850
  766.0 17.6 %copy-start.4 = (bf16[1,9,48,384]{3,2,1,0:T(8,128)(2,1)S(1)}, bf16[1,9,48,384]{3,2,1,0:T(8,128)(2,1)}, u32[]{:S(2)}) copy-start(bf16[1,9,48,384]{3,2,1,0:T(8,128)(2,1)} %reduce-scatter.6.cloned.1.call-done) | copy-start | bytes 995332
  766.0 3.9 collective-permute-start.14
  769.9 13.6 %collective-permute-start.15 = (f32[4,768]{1,0:T(4,128)S(1)}, f32[4,768]{1,0:T(4,128)S(1)}, u32[]{:S(2)}, u32[]{:S(2)}) collective-permute-start(f32[4,768]{1,0:T(4,128)S(1)} %add.275), channel_id=1, source_target_pairs={{0,16},{2,18},{4,20},{6,22},{8,24},{10,26},{12,28},{14,30},{16,0},... | collective-permute-start | bytes 36872 | tf_op jit(solution)/shard_map/ppermute | solution.py:850
  782.5 13.3 %copy-start.1 = (bf16[64,8]{0,1:T(8,128)(2,1)S(1)}, bf16[64,8]{0,1:T(8,128)(2,1)}, u32[]{:S(2)}) copy-start(bf16[64,8]{0,1:T(8,128)(2,1)} %param.43) | copy-start | bytes 3076
  786.1 7.5 collective-permute-start.18
  788.7 6.1 collective-permute-start.19
Sparse Core Ops, SparseCore 0:
  381.2 121.8 reduce-scatter.3
  592.8 24.0 reduce-scatter.5
  621.2 63.0 reduce-scatter.7

commit v4 on v3

--- a/solution.py
+++ b/solution.py
@@ -876,17 +876,16 @@
     slab = over_clip(weight_part)[0]
     near_early = meet(early, early_steps[0])
     back0 = back(0, pairs[0], mixed)
-    mixed, slab, early, near_early, back0 = tie((mixed, slab, early, near_early, back0))
+    mixed, slab, early, near_early, pooled, back0 = tie((mixed, slab, early, near_early, pooled, back0))
     early = early + near_early
     near_early = meet(early, early_steps[1])
     slab = lax.psum_scatter(slab, "seq", scatter_dimension=0, tiled=False)
     slab0 = over_clip(back0[3])
+    pooled = pooled[:slots].reshape(clip_count, frames_here, NTOK, width)
+    pooled = [send(pooled[t], t, True) for t in range(clip_count)]
     back1 = back(pairs[0], pairs[1], mixed)
-    slab, slab0, early, near_early, back1 = tie((slab, slab0, early, near_early, back1))
+    slab, slab0, early, near_early, pooled, back1 = tie((slab, slab0, early, near_early, pooled, back1))
     early = early + near_early
-    pooled = pooled[:slots].reshape(clip_count, frames_here, NTOK, width)
-    pooled = gather_back([pooled[t] for t in range(clip_count)], bf16)
-
     grads = [list(one[:3]) for one in (back0, back1)]
     if group > 1:
         both = jnp.zeros((seq_size * rows, 2 * width), bf16)
@@ -905,7 +904,7 @@
     kept, received = part_ways(back1[3].reshape(clip_size, share, -1), clip_steps[0])
     if split:
         size = tile_of(piece, 256)
-        lead = -(-piece // size // 2) * size
+        lead = 2 * size if piece > 2 * size else size
         far0, sums0 = finish(piece, lead, x_low, *rest)
         far0, sums0, x_low, near_early, received = tie((far0, sums0, x_low, near_early, received))
         home0 = send(far0, 1, True)
@@ -914,14 +913,14 @@
     kept, received = part_ways(add_low(kept, received), clip_steps[1])
     if split:
         far1, sums1 = finish(piece + lead, piece - lead, x_low, *rest)
-        far1, sums1, x_low, near_early, received = tie((far1, sums1, x_low, near_early, received))
+        far1, sums1, x_low, near_early, received, home0 = tie((far1, sums1, x_low, near_early, received, home0))
         home1 = send(far1, 1, True)
     early = early + near_early
     near_early = meet(early, early_steps[4])
     kept, received = part_ways(add_low(kept, received), clip_steps[2])
     if split:
         input_grad, late = finish(0, piece, x_low, *rest, place=position % clip_count, places=clip_count)
-        input_grad, late, near_early, received, home0 = tie((input_grad, late, near_early, received, home0))
+        input_grad, late, near_early, received = tie((input_grad, late, near_early, received))
         other = (position + 1) % clip_count
         input_grad = lax.dynamic_update_slice(input_grad, home0.astype(f32)[None], (other, 0, 0))
         late = late + sums0 + sums1
@@ -935,9 +934,14 @@
     for step in clip_steps[3:]:
         slab1 = add_low(*part_ways(slab1, step))
     late = late[:4]
-    for step in clip_steps:
-        late = late + meet(late, step)
-    late, slab1, slab, early = tie((late, slab1, slab, early))
+    for first, *second in zip(clip_steps[::2], clip_steps[1::2]):
+        low, high = first[1], second[0][1]
+        near_sum = late + meet(late, ("clip", low))
+        late = near_sum + (meet(late, ("clip", high)) + meet(late, ("clip", low + high)))
+    if len(clip_steps) % 2:
+        late = late + meet(late, clip_steps[-1])
+    if split:
+        home1, late, slab1, slab, early, pooled = tie((home1, late, slab1, slab, early, pooled))
     for step in seq_steps:
         late = late + meet(late, step)
     qkv = [
@@ -953,6 +957,7 @@
     fc2_grad = slab[4:8].reshape(4 * share, thin).astype(f32)
     out_grad = slab[8].astype(f32)
 
+    pooled = jnp.stack(pooled)[(jnp.arange(clip_count) - position) % clip_count]
     small = early[6]
     map1_grad = early[16 : 16 + map_size].T
     map2_grad = early[16 + map_size :, : map_size // 16 * lanes].reshape(16, map_size // 16, lanes // NTOK, NTOK)

time: 811 us -> 807 us (level)
  waiting for transfers between devices: 18.1 us -> 9.76 us
    ppermute x5, waiting for transfers between devices: 14.7 us -> 6.54 us  [send(): return lax.ppermute(value, 'seq', pairs)]
    ppermute x15 -> x17, starting transfers between devices: 17.5 us -> 19 us  [meet(): lax.ppermute(value, axis, [(i, i ^ bit) for i in range(lax.axis_size(axis...]
  transfers between devices with their start and end apart: 23 -> 25, of which waited for: 7 -> 7; matrix products, arithmetic and copies ran while one was open for 3% -> 4% of each run, Pallas kernels for 49% -> 50%
where the time goes in v4:
time: 807 us; the launch traced here: 800 us
  Pallas kernels  707 us (88%)
  starting transfers between devices  25.5 us (3%)
  local copies, waits for them, and re-layouts  20.2 us (3%)
  other arithmetic  19.3 us (2%)
  between operations  17.4 us (2%)
  waiting for transfers between devices  9.76 us (1%)
    pallas_call x2, Pallas kernels, attend_back(): pl.pallas_call(attend_back_kernel, grid=(pairs, rows // size), in_specs=[...  318 us
    pallas_call x1, Pallas kernels, middle(): pl.pallas_call(middle_kernel, grid=(rows // size,), in_specs=[tile, tile]...  184 us
    pallas_call x1, Pallas kernels, attend(): pl.pallas_call(attend_kernel, grid=(pairs,), in_specs=[pl.BlockSpec((rows...  114 us
    pallas_call x3, Pallas kernels, finish(): pl.pallas_call(finish_kernel, grid_spec=pltpu.PrefetchScalarGridSpec(num_...  33.5 us
    pallas_call x1, Pallas kernels, attend_near(): pl.pallas_call(attend_near_kernel, grid=(pairs,), in_specs=[pl.BlockSpec(...  33.3 us
    pallas_call x2, Pallas kernels, project(): pl.pallas_call(project_kernel, grid_spec=pltpu.PrefetchScalarGridSpec(num...  23.3 us
    ppermute x17, starting transfers between devices, meet(): lax.ppermute(value, axis, [(i, i ^ bit) for i in range(lax.axis_size(axis...  19 us
  transfers between devices with their start and end apart: 25, of which 7 were waited for; matrix products, arithmetic and copies ran while one was open for 4% of the time, Pallas kernels for 50%

profile of v4, /device:TPU:0, one launch (start us, length us, event | category | flops | bytes accessed | tf_op | source)
XLA Modules:
  0.0 799.6 jit_solution(1494357537322937358)
XLA Ops:
  7.4 3.3 dynamic-slice_bitcast_fusion
  10.7 3.0 collective-permute-start
  14.0 0.6 reshape.388.vec
  14.7 0.6 dynamic_slice.47
  16.5 1.3 fusion.17
  18.3 1.1 concatenate.13.kaug
  19.4 11.6 %project.2 = (bf16[3136,2304]{1,0:T(8,128)(2,1)}, bf16[3136,768]{1,0:T(8,128)(2,1)}, bf16[3136,768]{1,0:T(8,128)(2,1)}) custom-call(s32[1]{0:T(128)} %bitcast.2.place, bf16[2,1568,768]{2,1,0:T(8,128)(2,1)} %x.11, f32[14,768]{1,0:T(8,128)} %reshape.388.vec, bf16[768,2304]{1,0:T(8,128)(2,1)} %weight.9), custom_call_target="tpu_custom_call" | custom-call | tf_op jit(solution)/shard_map/project/pallas_call | solution.py:423
  31.1 33.3 %attend_near.1.refs_0_ = f32[12,80,1536]{2,1,0:T(8,128)} custom-call(bf16[3136,2304]{1,0:T(8,128)(2,1)} %get-tuple-element.97.q.k.v.refs_0_, bf16[3136,2304]{1,0:T(8,128)(2,1)} %get-tuple-element.97.q.k.v.refs_0_, bf16[3136,2304]{1,0:T(8,128)(2,1)} %get-tuple-element.97.q.k.v.refs_0_, bf16[3136,128]{1,0:T(8,128)(2,1)} %concatenate.13.kaug), custom_call_target="tpu_custom_call" | custom-call | flops 28991029248 | bytes 11796480 | tf_op jit(solution)/shard_map/attend_near/pallas_call | solution.py:117
  64.7 0.7 pad.18.m1
  65.5 0.6 pad.19.m2
  66.2 1.3 fusion.25
  67.6 0.6 stack.21.aux
  68.3 0.7 maximum_bitcast_fusion.cot
  69.0 1.4 copy-done.2
  70.4 11.7 %project.3 = (bf16[3136,2304]{1,0:T(8,128)(2,1)}, bf16[3136,768]{1,0:T(8,128)(2,1)}, bf16[3136,768]{1,0:T(8,128)(2,1)}) custom-call(s32[1]{0:T(128)} %constant.253.clone.1.place, bf16[1,1568,768]{2,1,0:T(8,128)(2,1)} %bitcast.80, f32[14,768]{1,0:T(8,128)} %reshape.388.vec, ...), custom_call_target="tpu_custom_call", output_to_operand_aliasing={{0}: (4, {}), {1}: (5, {}), {2}: (6, {})} | custom-call | tf_op jit(solution)/shard_map/project/pallas_call | solution.py:423
  82.1 114.5 %attend.1 = (bf16[3136,768]{1,0:T(8,128)(2,1)}, bf16[3136,768]{1,0:T(8,128)(2,1)}) custom-call(bf16[3136,2304]{1,0:T(8,128)(2,1)} %get-tuple-element.123.q.k.v, bf16[3136,2304]{1,0:T(8,128)(2,1)} %get-tuple-element.123.q.k.v, bf16[3136,2304]{1,0:T(8,128)(2,1)} %get-tuple-element.123.q.k.v, bf16[3136,128]{1,0:T(8,128)(2,1)} %concatenate.13.kaug, ...), custom_call_target="tpu_custom_call" | custom-call | flops 120846286848 | bytes 24084480 | tf_op jit(solution)/shard_map/attend/pallas_call | solution.py:204
  196.5 184.4 %middle.1 = (bf16[3136,768]{1,0:T(8,128)(2,1)}, bf16[3136,768]{1,0:T(8,128)(2,1)}, bf16[16,2,9,48,384]{4,3,2,1,0:T(8,128)(2,1)}, f32[96,768]{1,0:T(8,128)}, bf16[128,768]{1,0:T(8,128)(2,1)}) custom-call(bf16[3136,768]{1,0:T(8,128)(2,1)} %get-tuple-element.143.x, bf16[3136,768]{1,0:T(8,128)(2,1)} %get-tuple-element.103.att, f32[8,128]{1,0:T(8,128)} %stack.21.aux, ...), custom_call_target="tpu_custom_call" | custom-call | flops 99883155456 | bytes 28901376 | tf_op jit(solution)/shard_map/middle/pallas_call | solution.py:583
  381.0 0.6 copy-done.10
  381.7 0.7 select_convert_fusion.1.kaug_t
  382.4 210.1 %attend_back.2 = (bf16[3136,512]{1,0:T(8,128)(2,1)}, bf16[3136,512]{1,0:T(8,128)(2,1)}, bf16[3136,512]{1,0:T(8,128)(2,1)}, bf16[768,1536]{1,0:T(8,128)(2,1)}) custom-call(bf16[3136,2304]{1,0:T(8,128)(2,1)} %get-tuple-element.123.q.k.v, bf16[3136,768]{1,0:T(8,128)(2,1)} %get-tuple-element.108.do, bf16[3136,768]{1,0:T(8,128)(2,1)} %get-tuple-element.103.att, ...), custom_call_target="tpu_custom_call" | custom-call | flops 157351936000 | bytes 48168960 | tf_op jit(solution)/shard_map/attend_back/pallas_call | solution.py:325
  592.7 1.1 add.280
  593.7 1.9 collective-permute-start.3
  595.9 108.3 %attend_back.3 = (bf16[3136,256]{1,0:T(8,128)(2,1)}, bf16[3136,256]{1,0:T(8,128)(2,1)}, bf16[3136,256]{1,0:T(8,128)(2,1)}, bf16[768,768]{1,0:T(8,128)(2,1)}) custom-call(bf16[3136,2304]{1,0:T(8,128)(2,1)} %get-tuple-element.123.q.k.v, bf16[3136,768]{1,0:T(8,128)(2,1)} %get-tuple-element.108.do, bf16[3136,768]{1,0:T(8,128)(2,1)} %get-tuple-element.103.att, ...), custom_call_target="tpu_custom_call" | custom-call | flops 78675968000 | bytes 48168960 | tf_op jit(solution)/shard_map/attend_back/pallas_call | solution.py:325
  704.3 1.1 dynamic-slice_bitcast_fusion.1
  705.7 0.6 pad_clamp_fusion
  706.3 1.9 collective-permute-start.5
  708.3 1.0 reshape.393
  709.3 6.8 finish.3
  716.1 1.0 add.284
  717.1 1.7 collective-permute-start.7
  719.0 1.6 collective-permute-start.8
  720.6 1.5 collective-permute-start.9
  722.1 11.8 %finish.4 = (bf16[1120,768]{1,0:T(8,128)(2,1)}, f32[8,768]{1,0:T(8,128)}) custom-call(s32[1]{0:T(128)} %constant.253.clone.1.place, bf16[3136,768]{1,0:T(8,128)(2,1)} %get-tuple-element.143.x, bf16[3136,768]{1,0:T(8,128)(2,1)} %get-tuple-element.104.g1, f32[14,768]{1,0:T(8,128)} %reshape.388.vec, bf16[768,2304]{1,0:T(8,128)(2,1)} %weight.9, ...), custom_call_target="tpu_custom_call" | custom-call | flops 7927234560 | bytes 8601600 | tf_op jit(solution)/shard_map/finish/pallas_call | solution.py:658
  734.0 3.2 collective-permute-done.9
  737.2 1.5 collective-permute-start.10
  738.7 1.0 add.289
  739.7 2.7 collective-permute-start.11
  742.4 1.0 fusion.1
  744.0 14.9 %finish.5 = (f32[2,1568,768]{2,1,0:T(8,128)}, f32[8,768]{1,0:T(8,128)}) custom-call(s32[1]{0:T(128)} %bitcast.2.place, bf16[3136,768]{1,0:T(8,128)(2,1)} %get-tuple-element.143.x, bf16[3136,768]{1,0:T(8,128)(2,1)} %get-tuple-element.104.g1, f32[14,768]{1,0:T(8,128)} %reshape.388.vec, bf16[768,2304]{1,0:T(8,128)(2,1)} %weight.9, ...), custom_call_target="tpu_custom_call" | custom-call | flops 11098128384 | bytes 12042240 | tf_op jit(solution)/shard_map/finish/pallas_call | solution.py:658
  758.9 0.8 slice_add_fusion
  759.7 1.0 collective-permute-start.14
  760.7 1.1 collective-permute-start.13
  762.3 1.1 collective-permute-done.14
  763.9 1.1 collective-permute-start.17
  765.0 2.9 collective-permute-start.18
  767.9 1.2 convert_dynamic-update-slice_fusion.1
  769.1 1.0 add.308
  770.5 1.1 collective-permute-done.16
  771.6 3.3 collective-permute-done.10
  774.9 0.6 bitcast_convert_fusion.1
  775.6 0.6 slice_reduce_fusion.4
  776.2 0.7 slice_bitcast_fusion
  777.4 1.5 collective-permute-start.20
  780.2 0.7 bitcast_convert_fusion
  781.0 0.9 pad_maximum_fusion.1
  781.9 2.0 convert_dynamic-update-slice_fusion
  783.9 0.6 slice_reduce_fusion.10
  784.5 0.7 copy.82
  785.3 0.6 reshape.396
  786.0 0.7 reshape.398
  787.3 1.4 gather_fusion
  789.4 0.7 add.311
  790.1 0.6 slice_reduce_fusion
  791.0 0.7 copy.84
  (144 shorter events, 7.3 us)
Async XLA Ops:
  7.2 58.2 %copy-start = (bf16[64,8]{0,1:T(8,128)(2,1)S(1)}, bf16[64,8]{0,1:T(8,128)(2,1)}, u32[]{:S(2)}) copy-start(bf16[64,8]{0,1:T(8,128)(2,1)} %param.43) | copy-start | bytes 3076
  7.2 6.5 copy-start.5
  7.2 6.6 copy-start.14
  7.2 6.6 copy-start.15
  7.2 6.6 copy-start.16
  7.3 6.6 copy-start.17
  7.3 6.6 copy-start.18
  7.3 6.6 copy-start.19
  7.3 6.6 copy-start.20
  7.3 6.7 copy-start.21
  7.3 6.7 copy-start.22
  7.3 6.7 copy-start.23
  7.3 6.7 copy-start.11
  7.3 7.3 copy-start.25
  7.3 7.9 copy-start.26
  7.4 585.2 %reduce-scatter.4.cloned.1.call-start = ((), (), s32[]{:S(2)}) async-start(), calls=%async_computation.3 | async-start | bytes 11280384 | tf_op jit(solution)/shard_map/reduce_scatter | solution.py:839
  10.7 58.3 %collective-permute-start = (bf16[1568,768]{1,0:T(8,128)(2,1)}, bf16[1568,768]{1,0:T(8,128)(2,1)S(1)}, u32[]{:S(2)}, u32[]{:S(2)}) collective-permute-start(bf16[1568,768]{1,0:T(8,128)(2,1)} %dynamic-slice_bitcast_fusion), channel_id=1, source_target_pairs={{0,1},{1,0},{2,3},{3,2},{4,5},{5,4},{6,7},{7,6},{8,9},{9,8},{10,11... | collective-permute-start | bytes 7225352 | tf_op jit(solution)/shard_map/ppermute | solution.py:722
  13.7 54.6 %collective-permute-start.1 = (bf16[8,8,768]{2,1,0:T(8,128)(2,1)S(1)}, bf16[8,8,768]{2,1,0:T(8,128)(2,1)S(1)}, u32[]{:S(2)}, u32[]{:S(2)}) collective-permute-start(bf16[8,8,768]{2,1,0:T(8,128)(2,1)S(1)} %get-tuple-element.183), channel_id=1, source_target_pairs={{0,1},{1,0},{2,3},{3,2},{4,5},{5,4},{6,7},{7,6},{8,9},{9,8},{10,11... | collective-permute-start | bytes 294920 | tf_op jit(solution)/shard_map/ppermute | solution.py:722
  17.8 13.2 %copy-start.9 = (bf16[3136]{0:T(1024)(128)(2,1)}, bf16[3136]{0:T(1024)(128)(2,1)S(1)}, u32[]{:S(2)}) copy-start(bf16[3136]{0:T(1024)(128)(2,1)S(1)} %fusion.17) | copy-start | bytes 18820
  31.1 33.4 %copy-start.24 = (f32[8]{0:T(128)S(1)}, f32[8]{0:T(128)}, u32[]{:S(2)}) copy-start(f32[8]{0:T(128)} %param.44) | copy-start | bytes 100
  31.1 33.5 %copy-start.7 = (bf16[768,64]{0,1:T(8,128)(2,1)S(1)}, bf16[768,64]{0,1:T(8,128)(2,1)}, u32[]{:S(2)}) copy-start(bf16[768,64]{0,1:T(8,128)(2,1)} %param.41) | copy-start | bytes 294916
  31.1 36.4 %copy-start.27 = (f32[64]{0:T(128)S(1)}, f32[64]{0:T(128)}, u32[]{:S(2)}) copy-start(f32[64]{0:T(128)} %param.42) | copy-start | bytes 772
  69.0 1.4 copy-start.2
  381.0 0.7 copy-start.10
  381.0 323.3 %reduce-scatter.6.cloned.1.call-start = ((), (), s32[]{:S(2)}) async-start(), calls=%async_computation.4 | async-start | bytes 995328 | tf_op jit(solution)/shard_map/reduce_scatter | solution.py:882
  382.4 210.1 %collective-permute-start.2 = (f32[96,768]{1,0:T(8,128)}, f32[96,768]{1,0:T(8,128)}, u32[]{:S(2)}, u32[]{:S(2)}) collective-permute-start(f32[96,768]{1,0:T(8,128)} %get-tuple-element.120), channel_id=1, source_target_pairs={{0,2},{2,0},{4,6},{6,4},{8,10},{10,8},{12,14},{14,12},{16,18},{18,... | collective-permute-start | bytes 884744 | tf_op jit(solution)/shard_map/ppermute | solution.py:850
  382.4 213.3 %copy-start.6 = (bf16[128,768]{1,0:T(8,128)(2,1)S(1)}, bf16[128,768]{1,0:T(8,128)(2,1)}, u32[]{:S(2)}) copy-start(bf16[128,768]{1,0:T(8,128)(2,1)} %get-tuple-element.122) | copy-start | bytes 589828
  592.6 111.7 %reduce-scatter.8.cloned.1.call-start = ((), (), s32[]{:S(2)}) async-start(), calls=%async_computation.5 | async-start | bytes 2506752 | tf_op jit(solution)/shard_map/reduce_scatter | solution.py:839
  593.7 110.5 %collective-permute-start.3 = (f32[96,768]{1,0:T(8,128)S(1)}, f32[96,768]{1,0:T(8,128)S(1)}, u32[]{:S(2)}, u32[]{:S(2)}) collective-permute-start(f32[96,768]{1,0:T(8,128)S(1)} %add.280), channel_id=1, source_target_pairs={{0,1},{1,0},{2,3},{3,2},{4,5},{5,4},{6,7},{7,6},{8,9},{9,8},{10,11... | collective-permute-start | bytes 884744 | tf_op jit(solution)/shard_map/ppermute | solution.py:850
  595.7 108.6 %collective-permute-start.4 = (bf16[8,8,768]{2,1,0:T(8,128)(2,1)S(1)}, bf16[8,8,768]{2,1,0:T(8,128)(2,1)S(1)}, u32[]{:S(2)}, u32[]{:S(2)}) collective-permute-start(bf16[8,8,768]{2,1,0:T(8,128)(2,1)S(1)} %get-tuple-element.180), channel_id=1, source_target_pairs={{1,0},{0,1},{3,2},{2,3},{5,4},{4,5},{7,6},{6,7},{9,8},{8,9},{11,10... | collective-permute-start | bytes 294920 | tf_op jit(solution)/shard_map/ppermute | solution.py:722
  704.3 1.4 copy-start.8
  705.5 10.6 %collective-permute-start.6 = (bf16[8,48,768]{2,1,0:T(8,128)(2,1)S(1)}, bf16[8,48,768]{2,1,0:T(8,128)(2,1)S(1)}, u32[]{:S(2)}, u32[]{:S(2)}) collective-permute-start(bf16[8,48,768]{2,1,0:T(8,128)(2,1)S(1)} %dynamic-slice_bitcast_fusion.1), channel_id=1, source_target_pairs={{0,2},{2,0},{4,6},{6,4},{8,10},{10,8},{12,14},{14,12},{16,18},{18,... | collective-permute-start | bytes 1769480 | tf_op jit(solution)/shard_map/ppermute | solution.py:850
  706.3 9.8 %collective-permute-start.5 = (f32[96,768]{1,0:T(8,128)S(1)}, f32[96,768]{1,0:T(8,128)}, u32[]{:S(2)}, u32[]{:S(2)}) collective-permute-start(f32[96,768]{1,0:T(8,128)S(1)} %add.281), channel_id=1, source_target_pairs={{0,4},{2,6},{4,0},{6,2},{8,12},{10,14},{12,8},{14,10},{16,20},{18,... | collective-permute-start | bytes 884744 | tf_op jit(solution)/shard_map/ppermute | solution.py:850
  709.3 9.6 %copy-start.3 = (bf16[768,768]{1,0:T(8,128)(2,1)S(1)}, bf16[768,768]{1,0:T(8,128)(2,1)}, u32[]{:S(2)}) copy-start(bf16[768,768]{1,0:T(8,128)(2,1)} %get-tuple-element.135) | copy-start | bytes 3538948
  717.1 16.8 %collective-permute-start.7 = (f32[96,768]{1,0:T(8,128)S(1)}, f32[96,768]{1,0:T(8,128)}, u32[]{:S(2)}, u32[]{:S(2)}) collective-permute-start(f32[96,768]{1,0:T(8,128)S(1)} %add.284), channel_id=1, source_target_pairs={{0,8},{2,10},{4,12},{6,14},{8,0},{10,2},{12,4},{14,6},{16,24},{18,... | collective-permute-start | bytes 884744 | tf_op jit(solution)/shard_map/ppermute | solution.py:850
  719.0 14.9 %collective-permute-start.8 = (bf16[4,48,768]{2,1,0:T(8,128)(2,1)S(1)}, bf16[4,48,768]{2,1,0:T(8,128)(2,1)}, u32[]{:S(2)}, u32[]{:S(2)}) collective-permute-start(bf16[4,48,768]{2,1,0:T(8,128)(2,1)S(1)} %dynamic-slice_bitcast_fusion.2), channel_id=1, source_target_pairs={{0,4},{2,6},{4,0},{6,2},{8,12},{10,14},{12,8},{14,10},{16,20},{18,... | collective-permute-start | bytes 884744 | tf_op jit(solution)/shard_map/ppermute | solution.py:850
  720.6 16.5 %collective-permute-start.9 = (bf16[448,768]{1,0:T(8,128)(2,1)}, bf16[448,768]{1,0:T(8,128)(2,1)S(1)}, u32[]{:S(2)}, u32[]{:S(2)}) collective-permute-start(bf16[448,768]{1,0:T(8,128)(2,1)} %get-tuple-element.141), channel_id=1, source_target_pairs={{1,0},{0,1},{3,2},{2,3},{5,4},{4,5},{7,6},{6,7},{9,8},{8,9},{11,10... | collective-permute-start | bytes 2064392 | tf_op jit(solution)/shard_map/ppermute | solution.py:722
  737.2 37.7 %collective-permute-start.10 = (bf16[1120,768]{1,0:T(8,128)(2,1)}, bf16[1120,768]{1,0:T(8,128)(2,1)S(1)}, u32[]{:S(2)}, u32[]{:S(2)}) collective-permute-start(bf16[1120,768]{1,0:T(8,128)(2,1)} %get-tuple-element.142), channel_id=1, source_target_pairs={{1,0},{0,1},{3,2},{2,3},{5,4},{4,5},{7,6},{6,7},{9,8},{8,9},{11,10... | collective-permute-start | bytes 5160968 | tf_op jit(solution)/shard_map/ppermute | solution.py:722
  739.7 19.2 %collective-permute-start.11 = (f32[96,768]{1,0:T(8,128)S(1)}, f32[96,768]{1,0:T(8,128)}, u32[]{:S(2)}, u32[]{:S(2)}) collective-permute-start(f32[96,768]{1,0:T(8,128)S(1)} %add.289), channel_id=1, source_target_pairs={{0,16},{2,18},{4,20},{6,22},{8,24},{10,26},{12,28},{14,30},{16,0},... | collective-permute-start | bytes 884744 | tf_op jit(solution)/shard_map/ppermute | solution.py:850
  743.5 15.4 %copy-start.12 = (f32[8,768]{1,0:T(8,128)S(1)}, f32[8,768]{1,0:T(8,128)}, u32[]{:S(2)}) copy-start(f32[8,768]{1,0:T(8,128)} %get-tuple-element.149) | copy-start | bytes 73732
  743.5 15.4 %copy-start.13 = (f32[8,768]{1,0:T(8,128)S(1)}, f32[8,768]{1,0:T(8,128)}, u32[]{:S(2)}) copy-start(f32[8,768]{1,0:T(8,128)} %get-tuple-element.150) | copy-start | bytes 73732
  743.5 15.4 %collective-permute-start.12 = (bf16[2,48,768]{2,1,0:T(8,128)(2,1)S(1)}, bf16[2,48,768]{2,1,0:T(8,128)(2,1)S(1)}, u32[]{:S(2)}, u32[]{:S(2)}) collective-permute-start(bf16[2,48,768]{2,1,0:T(8,128)(2,1)S(1)} %dynamic-slice_bitcast_fusion.4), channel_id=1, source_target_pairs={{0,8},{2,10},{4,12},{6,14},{8,0},{10,2},{12,4},{14,6},{16,24},{18,... | collective-permute-start | bytes 442376 | tf_op jit(solution)/shard_map/ppermute | solution.py:850
  758.9 16.0 %copy-start.4 = (bf16[1,9,48,384]{3,2,1,0:T(8,128)(2,1)S(1)}, bf16[1,9,48,384]{3,2,1,0:T(8,128)(2,1)}, u32[]{:S(2)}) copy-start(bf16[1,9,48,384]{3,2,1,0:T(8,128)(2,1)} %reduce-scatter.6.cloned.1.call-done) | copy-start | bytes 995332
  759.7 3.7 collective-permute-start.14
  760.7 3.1 collective-permute-start.15
  760.7 3.1 collective-permute-start.13
  761.9 9.7 %collective-permute-start.19 = (bf16[1,48,768]{2,1,0:T(8,128)(2,1)S(1)}, bf16[1,48,768]{2,1,0:T(8,128)(2,1)S(1)}, u32[]{:S(2)}, u32[]{:S(2)}) collective-permute-start(bf16[1,48,768]{2,1,0:T(8,128)(2,1)S(1)} %constant_dynamic-slice_fusion), channel_id=1, source_target_pairs={{0,16},{2,18},{4,20},{6,22},{8,24},{10,26},{12,28},{14,30},{16,0},... | collective-permute-start | bytes 221192 | tf_op jit(solution)/shard_map/ppermute | solution.py:850
  763.9 6.2 collective-permute-start.17
  765.0 5.5 collective-permute-start.18
  767.9 3.7 collective-permute-start.16
  777.4 11.9 %collective-permute-start.20 = (f32[4,768]{1,0:T(4,128)S(1)}, f32[4,768]{1,0:T(4,128)}, u32[]{:S(2)}, u32[]{:S(2)}) collective-permute-start(f32[4,768]{1,0:T(4,128)S(1)} %add_add_fusion), channel_id=1, source_target_pairs={{0,1},{1,0},{2,3},{3,2},{4,5},{5,4},{6,7},{7,6},{8,9},{9,8},{10,11... | collective-permute-start | bytes 36872 | tf_op jit(solution)/shard_map/ppermute | solution.py:850
  779.6 11.1 %collective-permute-start.21 = (bf16[1,48,1152]{2,0,1:T(2,128)(2,1)S(1)}, bf16[1,48,1152]{2,0,1:T(2,128)(2,1)S(1)}, u32[]{:S(2)}, u32[]{:S(2)}) collective-permute-start(bf16[1,48,1152]{2,0,1:T(2,128)(2,1)S(1)} %dynamic-slice_bitcast_fusion.3), channel_id=1, source_target_pairs={{0,1},{1,0},{2,3},{3,2},{4,5},{5,4},{6,7},{7,6},{8,9},{9,8},{10,11... | collective-permute-start | bytes 331784 | tf_op jit(solution)/shard_map/ppermute | solution.py:850
  781.0 10.8 %copy-start.1 = (bf16[64,8]{0,1:T(8,128)(2,1)S(1)}, bf16[64,8]{0,1:T(8,128)(2,1)}, u32[]{:S(2)}) copy-start(bf16[64,8]{0,1:T(8,128)(2,1)} %param.43) | copy-start | bytes 3076
Sparse Core Ops, SparseCore 0:
  381.1 121.8 reduce-scatter.3
  592.7 20.8 reduce-scatter.5
  617.8 64.4 reduce-scatter.7

commit v5 on v4

--- a/solution.py
+++ b/solution.py
@@ -754,14 +754,12 @@
 
     key_ids = jnp.arange(keys, dtype=jnp.int32)
     key_inside = placed(key_ids % rows, key_ids // rows)
-    lane16 = jnp.arange(HEAD)
     key_mask = jnp.where(key_inside, 0.0, masked_score)
-    kaug = jnp.where(lane16[None, :] < 3, 1.0, jnp.where(lane16[None, :] == 3, key_mask[:, None], 0.0)).astype(bf16)
-    kaug = jnp.concatenate([kaug, jnp.zeros_like(kaug)], axis=1)
+    lane = jnp.arange(128)[None, :]
+    kaug = jnp.where(lane < 3, 1.0, jnp.where(lane == 3, key_mask[:, None], 0.0)).astype(bf16)
     sub16 = jnp.arange(16)[:, None]
     wide_mask = jnp.pad(key_mask, (0, up(keys, TILE) - keys), constant_values=masked_score)
     kaug_t = jnp.where(sub16 < 3, 1.0, jnp.where(sub16 == 3, wide_mask[None, :], 0.0)).astype(bf16)
-
     vec = jnp.concatenate(
         [
             norm1_gain,
@@ -900,27 +898,24 @@
                 at += pairs[n] * 128
     grads = [grad for one in grads for grad in one]
     rest = (grad_low, vec, qkv_weight, grads)
-    near_early = meet(early, early_steps[2])
-    kept, received = part_ways(back1[3].reshape(clip_size, share, -1), clip_steps[0])
     if split:
         size = tile_of(piece, 256)
         lead = 2 * size if piece > 2 * size else size
         far0, sums0 = finish(piece, lead, x_low, *rest)
-        far0, sums0, x_low, near_early, received = tie((far0, sums0, x_low, near_early, received))
         home0 = send(far0, 1, True)
-    early = early + near_early
-    near_early = meet(early, early_steps[3])
-    kept, received = part_ways(add_low(kept, received), clip_steps[1])
-    if split:
+        far0, x_low = tie((far0, x_low))
         far1, sums1 = finish(piece + lead, piece - lead, x_low, *rest)
-        far1, sums1, x_low, near_early, received, home0 = tie((far1, sums1, x_low, near_early, received, home0))
         home1 = send(far1, 1, True)
-    early = early + near_early
-    near_early = meet(early, early_steps[4])
-    kept, received = part_ways(add_low(kept, received), clip_steps[2])
+        x_low, home0, far1, early, slab1 = tie((x_low, home0, far1, early, back1[3]))
+    else:
+        slab1 = back1[3]
+    near_early = meet(early, early_steps[2])
+    kept, received = part_ways(slab1.reshape(clip_size, share, -1), clip_steps[0])
     if split:
         input_grad, late = finish(0, piece, x_low, *rest, place=position % clip_count, places=clip_count)
-        input_grad, late, near_early, received = tie((input_grad, late, near_early, received))
+        input_grad, late, near_early, received, slab, slab0, pooled = tie(
+            (input_grad, late, near_early, received, slab, slab0, pooled)
+        )
         other = (position + 1) % clip_count
         input_grad = lax.dynamic_update_slice(input_grad, home0.astype(f32)[None], (other, 0, 0))
         late = late + sums0 + sums1
@@ -928,10 +923,10 @@
         local, late = finish(0, rows, x_low, *rest)
         input_grad = gather_back([local[t * piece : (t + 1) * piece] for t in range(clip_count)], f32)
     early = early + near_early
-    for step in early_steps[5:]:
+    for step in early_steps[3:]:
         early = early + meet(early, step)
     slab1 = add_low(kept, received)
-    for step in clip_steps[3:]:
+    for step in clip_steps[1:]:
         slab1 = add_low(*part_ways(slab1, step))
     late = late[:4]
     for first, *second in zip(clip_steps[::2], clip_steps[1::2]):
@@ -940,23 +935,10 @@
         late = near_sum + (meet(late, ("clip", high)) + meet(late, ("clip", low + high)))
     if len(clip_steps) % 2:
         late = late + meet(late, clip_steps[-1])
-    if split:
-        home1, late, slab1, slab, early, pooled = tie((home1, late, slab1, slab, early, pooled))
-    for step in seq_steps:
-        late = late + meet(late, step)
-    qkv = [
-        part.reshape(share, count, 3, 128).transpose(0, 2, 1, 3) for part, count in zip((slab0, slab1), pairs)
-    ]
-    qkv = jnp.concatenate(qkv, axis=2).reshape(share, seq_size, -1).transpose(1, 0, 2)
-    for step in seq_steps:
-        qkv = add_low(*part_ways(qkv, step))
-    qkv_grad = qkv[0].astype(f32)
-    if split:
-        input_grad = lax.dynamic_update_slice(input_grad, home1.astype(f32)[None], (other, lead, 0))
+
     fc1_grad = slab[:4].transpose(1, 0, 2).reshape(share, 4 * thin).astype(f32)
     fc2_grad = slab[4:8].reshape(4 * share, thin).astype(f32)
     out_grad = slab[8].astype(f32)
-
     pooled = jnp.stack(pooled)[(jnp.arange(clip_count) - position) % clip_count]
     small = early[6]
     map1_grad = early[16 : 16 + map_size].T
@@ -964,6 +946,27 @@
     map2_grad = jnp.sum(map2_grad, axis=2).transpose(1, 0, 2).reshape(map_size, NTOK)
     map2_bias_grad = jnp.sum(small[128:256].reshape(-1, NTOK), axis=0)
     penalty = jnp.sum(small[256:384]) / pair_count / slots_all
+    done = (
+        [fc1_grad, fc2_grad, out_grad, pooled, map1_grad, map2_grad, map2_bias_grad, penalty, small[:map_size]]
+        + [early[n] for n in range(6)]
+        + [early[8:12].reshape(-1)]
+    )
+    qkv = [
+        part.reshape(share, count, 3, 128).transpose(0, 2, 1, 3) for part, count in zip((slab0, slab1), pairs)
+    ]
+    qkv = jnp.concatenate(qkv, axis=2).reshape(share, seq_size, -1).transpose(1, 0, 2)
+    if split:
+        home1, late, qkv, done = tie((home1, late, qkv, done))
+    for step in seq_steps:
+        late = late + meet(late, step)
+    for step in seq_steps:
+        qkv = add_low(*part_ways(qkv, step))
+    qkv_grad = qkv[0].astype(f32)
+    if split:
+        input_grad = lax.dynamic_update_slice(input_grad, home1.astype(f32)[None], (other, lead, 0))
+    fc1_grad, fc2_grad, out_grad, pooled, map1_grad, map2_grad, map2_bias_grad, penalty, map1_bias_grad = done[:9]
+    early = done[9:15]
+    fc1_bias_grad = done[15]
     return (
         pooled,
         penalty,
@@ -978,13 +981,13 @@
         early[1],
         early[2],
         fc1_grad,
-        early[8:12].reshape(-1),
+        fc1_bias_grad,
         fc2_grad,
         early[3],
         early[4],
         early[5],
         map1_grad,
-        small[:map_size],
+        map1_bias_grad,
         map2_grad,
         map2_bias_grad,
     )

time: 807 us -> 825 us (1.022)
  waiting for transfers between devices: 9.76 us -> 28.1 us
    ppermute x17, waiting for transfers between devices: 3.11 us -> 23 us  [meet(): lax.ppermute(value, axis, [(i, i ^ bit) for i in range(lax.axis_size(axis...]
  transfers between devices with their start and end apart: 25 -> 25, of which waited for: 7 -> 7; matrix products, arithmetic and copies ran while one was open for 4% -> 4% of each run, Pallas kernels for 50% -> 48%
where the time goes in v5:
time: 825 us; the launch traced here: 818 us
  Pallas kernels  708 us (86%)
  waiting for transfers between devices  28.1 us (3%)
  starting transfers between devices  26.1 us (3%)
  local copies, waits for them, and re-layouts  20.1 us (2%)
  other arithmetic  19.2 us (2%)
  between operations  17.4 us (2%)
    pallas_call x2, Pallas kernels, attend_back(): pl.pallas_call(attend_back_kernel, grid=(pairs, rows // size), in_specs=[...  319 us
    pallas_call x1, Pallas kernels, middle(): pl.pallas_call(middle_kernel, grid=(rows // size,), in_specs=[tile, tile]...  184 us
    pallas_call x1, Pallas kernels, attend(): pl.pallas_call(attend_kernel, grid=(pairs,), in_specs=[pl.BlockSpec((rows...  114 us
    pallas_call x3, Pallas kernels, finish(): pl.pallas_call(finish_kernel, grid_spec=pltpu.PrefetchScalarGridSpec(num_...  33.5 us
    pallas_call x1, Pallas kernels, attend_near(): pl.pallas_call(attend_near_kernel, grid=(pairs,), in_specs=[pl.BlockSpec(...  33.3 us
    pallas_call x2, Pallas kernels, project(): pl.pallas_call(project_kernel, grid_spec=pltpu.PrefetchScalarGridSpec(num...  23.3 us
    ppermute x17, waiting for transfers between devices, meet(): lax.ppermute(value, axis, [(i, i ^ bit) for i in range(lax.axis_size(axis...  23 us
    ppermute x17, starting transfers between devices, meet(): lax.ppermute(value, axis, [(i, i ^ bit) for i in range(lax.axis_size(axis...  20.5 us
  transfers between devices with their start and end apart: 25, of which 7 were waited for; matrix products, arithmetic and copies ran while one was open for 4% of the time, Pallas kernels for 48%

profile of v5, /device:TPU:0, one launch (start us, length us, event | category | flops | bytes accessed | tf_op | source)
XLA Modules:
  0.0 818.4 jit_solution(9751575206692696552)
XLA Ops:
  7.4 3.3 dynamic-slice_bitcast_fusion
  10.7 3.0 collective-permute-start
  14.0 0.6 reshape.375.vec
  14.7 0.6 dynamic_slice.47
  16.5 1.3 fusion.15
  17.8 11.7 %project.2 = (bf16[3136,2304]{1,0:T(8,128)(2,1)}, bf16[3136,768]{1,0:T(8,128)(2,1)}, bf16[3136,768]{1,0:T(8,128)(2,1)}) custom-call(s32[1]{0:T(128)} %bitcast.2.place, bf16[2,1568,768]{2,1,0:T(8,128)(2,1)} %x.9, f32[14,768]{1,0:T(8,128)} %reshape.375.vec, bf16[768,2304]{1,0:T(8,128)(2,1)} %weight.9), custom_call_target="tpu_custom_call" | custom-call | tf_op jit(solution)/shard_map/project/pallas_call | solution.py:423
  29.5 1.4 select_convert_fusion.kaug
  30.9 33.3 %attend_near.1.refs_0_ = f32[12,80,1536]{2,1,0:T(8,128)} custom-call(bf16[3136,2304]{1,0:T(8,128)(2,1)} %get-tuple-element.107.q.k.v.refs_0_, bf16[3136,2304]{1,0:T(8,128)(2,1)} %get-tuple-element.107.q.k.v.refs_0_, bf16[3136,2304]{1,0:T(8,128)(2,1)} %get-tuple-element.107.q.k.v.refs_0_, bf16[3136,128]{1,0:T(8,128)(2,1)} %select_convert_fusion.kaug), custom_call_target="tpu_custom_call" | custom-call | flops 28991029248 | bytes 11796480 | tf_op jit(solution)/shard_map/attend_near/pallas_call | solution.py:117
  64.6 0.7 pad.17.m1
  65.4 0.6 pad.18.m2
  66.0 1.3 fusion.23
  67.4 0.6 stack.21.aux
  68.3 0.7 maximum_bitcast_fusion.cot
  69.0 1.4 copy-done.2
  70.4 11.7 %project.3 = (bf16[3136,2304]{1,0:T(8,128)(2,1)}, bf16[3136,768]{1,0:T(8,128)(2,1)}, bf16[3136,768]{1,0:T(8,128)(2,1)}) custom-call(s32[1]{0:T(128)} %constant.252.clone.1.place, bf16[1,1568,768]{2,1,0:T(8,128)(2,1)} %bitcast.76, f32[14,768]{1,0:T(8,128)} %reshape.375.vec, ...), custom_call_target="tpu_custom_call", output_to_operand_aliasing={{0}: (4, {}), {1}: (5, {}), {2}: (6, {})} | custom-call | tf_op jit(solution)/shard_map/project/pallas_call | solution.py:423
  82.0 114.5 %attend.1 = (bf16[3136,768]{1,0:T(8,128)(2,1)}, bf16[3136,768]{1,0:T(8,128)(2,1)}) custom-call(bf16[3136,2304]{1,0:T(8,128)(2,1)} %get-tuple-element.133.q.k.v, bf16[3136,2304]{1,0:T(8,128)(2,1)} %get-tuple-element.133.q.k.v, bf16[3136,2304]{1,0:T(8,128)(2,1)} %get-tuple-element.133.q.k.v, bf16[3136,128]{1,0:T(8,128)(2,1)} %select_convert_fusion.kaug, ...), custom_call_target="tpu_custom_call" | custom-call | flops 120846286848 | bytes 24084480 | tf_op jit(solution)/shard_map/attend/pallas_call | solution.py:204
  196.5 184.4 %middle.1 = (bf16[3136,768]{1,0:T(8,128)(2,1)}, bf16[3136,768]{1,0:T(8,128)(2,1)}, bf16[16,2,9,48,384]{4,3,2,1,0:T(8,128)(2,1)}, f32[96,768]{1,0:T(8,128)}, bf16[128,768]{1,0:T(8,128)(2,1)}) custom-call(bf16[3136,768]{1,0:T(8,128)(2,1)} %get-tuple-element.147.x, bf16[3136,768]{1,0:T(8,128)(2,1)} %get-tuple-element.113.att, f32[8,128]{1,0:T(8,128)} %stack.21.aux, ...), custom_call_target="tpu_custom_call" | custom-call | flops 99883155456 | bytes 28901376 | tf_op jit(solution)/shard_map/middle/pallas_call | solution.py:583
  381.0 0.6 copy-done.14
  381.7 0.7 select_convert_fusion.1.kaug_t
  382.4 210.1 %attend_back.2 = (bf16[3136,512]{1,0:T(8,128)(2,1)}, bf16[3136,512]{1,0:T(8,128)(2,1)}, bf16[3136,512]{1,0:T(8,128)(2,1)}, bf16[768,1536]{1,0:T(8,128)(2,1)}) custom-call(bf16[3136,2304]{1,0:T(8,128)(2,1)} %get-tuple-element.133.q.k.v, bf16[3136,768]{1,0:T(8,128)(2,1)} %get-tuple-element.118.do, bf16[3136,768]{1,0:T(8,128)(2,1)} %get-tuple-element.113.att, ...), custom_call_target="tpu_custom_call" | custom-call | flops 157351936000 | bytes 48168960 | tf_op jit(solution)/shard_map/attend_back/pallas_call | solution.py:325
  592.7 1.1 add.278
  593.8 1.8 collective-permute-start.3
  595.6 0.7 slice_bitcast_fusion.1
  596.6 108.4 %attend_back.3 = (bf16[3136,256]{1,0:T(8,128)(2,1)}, bf16[3136,256]{1,0:T(8,128)(2,1)}, bf16[3136,256]{1,0:T(8,128)(2,1)}, bf16[768,768]{1,0:T(8,128)(2,1)}) custom-call(bf16[3136,2304]{1,0:T(8,128)(2,1)} %get-tuple-element.133.q.k.v, bf16[3136,768]{1,0:T(8,128)(2,1)} %get-tuple-element.118.do, bf16[3136,768]{1,0:T(8,128)(2,1)} %get-tuple-element.113.att, ...), custom_call_target="tpu_custom_call" | custom-call | flops 78675968000 | bytes 48168960 | tf_op jit(solution)/shard_map/attend_back/pallas_call | solution.py:325
  705.1 6.8 finish.3
  712.0 1.8 collective-permute-start.6
  713.8 11.8 %finish.4 = (bf16[1120,768]{1,0:T(8,128)(2,1)}, f32[8,768]{1,0:T(8,128)}) custom-call(s32[1]{0:T(128)} %constant.252.clone.1.place, bf16[3136,768]{1,0:T(8,128)(2,1)} %get-tuple-element.147.x, bf16[3136,768]{1,0:T(8,128)(2,1)} %get-tuple-element.114.g1, f32[14,768]{1,0:T(8,128)} %reshape.375.vec, bf16[768,2304]{1,0:T(8,128)(2,1)} %weight.9, ...), custom_call_target="tpu_custom_call" | custom-call | flops 7927234560 | bytes 8601600 | tf_op jit(solution)/shard_map/finish/pallas_call | solution.py:658
  726.0 4.7 collective-permute-done.6
  730.7 1.7 collective-permute-start.7
  732.4 0.9 dynamic-slice_bitcast_fusion.1
  733.3 14.9 %finish.5 = (f32[2,1568,768]{2,1,0:T(8,128)}, f32[8,768]{1,0:T(8,128)}) custom-call(s32[1]{0:T(128)} %bitcast.2.place, bf16[3136,768]{1,0:T(8,128)(2,1)} %get-tuple-element.147.x, bf16[3136,768]{1,0:T(8,128)(2,1)} %get-tuple-element.114.g1, f32[14,768]{1,0:T(8,128)} %reshape.375.vec, bf16[768,2304]{1,0:T(8,128)(2,1)} %weight.9, ...), custom_call_target="tpu_custom_call" | custom-call | flops 11098128384 | bytes 12042240 | tf_op jit(solution)/shard_map/finish/pallas_call | solution.py:658
  748.3 0.8 slice_add_fusion
  749.3 1.5 collective-permute-start.11
  751.2 0.6 bitcast_convert_fusion.1
  751.9 1.2 fusion
  753.1 0.8 dynamic-slice_bitcast_fusion.2
  754.2 0.7 bitcast_convert_fusion
  754.9 1.0 reshape.378
  756.0 0.7 copy.82
  756.7 1.0 add.306
  757.7 1.2 gather_fusion
  758.9 2.3 convert_dynamic-update-slice_fusion.1
  761.2 2.0 collective-permute-done.15
  763.3 1.6 collective-permute-start.18
  764.8 1.0 fusion.1
  766.4 2.7 collective-permute-start.13
  769.1 1.3 collective-permute-start.14
  770.5 4.5 collective-permute-done.16
  774.9 1.6 collective-permute-start.12
  776.6 2.9 collective-permute-start.17
  779.6 1.8 collective-permute-start.19
  781.4 8.0 collective-permute-done.17
  789.9 5.1 collective-permute-done.19
  795.0 1.0 add.308
  796.2 0.7 reshape.384
  796.9 0.6 slice_reduce_fusion.10
  798.1 0.6 reshape.386
  799.4 0.6 slice_reduce_fusion.4
  800.5 0.7 slice_bitcast_fusion
  801.2 1.5 collective-permute-start.20
  803.5 2.0 convert_dynamic-update-slice_fusion
  805.6 0.6 slice_reduce_fusion
  806.2 3.3 collective-permute-done.21
  809.8 0.7 copy.84
  (151 shorter events, 7.0 us)
Async XLA Ops:
  7.2 57.3 %copy-start = (bf16[64,8]{0,1:T(8,128)(2,1)S(1)}, bf16[64,8]{0,1:T(8,128)(2,1)}, u32[]{:S(2)}) copy-start(bf16[64,8]{0,1:T(8,128)(2,1)} %param.43) | copy-start | bytes 3076
  7.2 6.4 copy-start.8
  7.2 6.5 copy-start.18
  7.2 6.6 copy-start.19
  7.2 6.6 copy-start.20
  7.3 6.6 copy-start.21
  7.3 6.6 copy-start.22
  7.3 6.6 copy-start.23
  7.3 6.6 copy-start.24
  7.3 6.6 copy-start.25
  7.3 6.7 copy-start.26
  7.3 6.7 copy-start.27
  7.3 6.7 copy-start.15
  7.3 7.3 copy-start.29
  7.3 7.9 copy-start.30
  7.4 585.1 %reduce-scatter.4.cloned.1.call-start = ((), (), s32[]{:S(2)}) async-start(), calls=%async_computation.3 | async-start | bytes 11280384 | tf_op jit(solution)/shard_map/reduce_scatter | solution.py:837
  10.7 58.3 %collective-permute-start = (bf16[1568,768]{1,0:T(8,128)(2,1)}, bf16[1568,768]{1,0:T(8,128)(2,1)S(1)}, u32[]{:S(2)}, u32[]{:S(2)}) collective-permute-start(bf16[1568,768]{1,0:T(8,128)(2,1)} %dynamic-slice_bitcast_fusion), channel_id=1, source_target_pairs={{0,1},{1,0},{2,3},{3,2},{4,5},{5,4},{6,7},{7,6},{8,9},{9,8},{10,11... | collective-permute-start | bytes 7225352 | tf_op jit(solution)/shard_map/ppermute | solution.py:722
  13.7 54.6 %collective-permute-start.1 = (bf16[8,8,768]{2,1,0:T(8,128)(2,1)S(1)}, bf16[8,8,768]{2,1,0:T(8,128)(2,1)S(1)}, u32[]{:S(2)}, u32[]{:S(2)}) collective-permute-start(bf16[8,8,768]{2,1,0:T(8,128)(2,1)S(1)} %get-tuple-element.203), channel_id=1, source_target_pairs={{0,1},{1,0},{2,3},{3,2},{4,5},{5,4},{6,7},{7,6},{8,9},{9,8},{10,11... | collective-permute-start | bytes 294920 | tf_op jit(solution)/shard_map/ppermute | solution.py:722
  17.8 11.7 %copy-start.13 = (bf16[3136]{0:T(1024)(128)(2,1)}, bf16[3136]{0:T(1024)(128)(2,1)S(1)}, u32[]{:S(2)}) copy-start(bf16[3136]{0:T(1024)(128)(2,1)S(1)} %fusion.15) | copy-start | bytes 18820
  30.9 33.4 %copy-start.28 = (f32[8]{0:T(128)S(1)}, f32[8]{0:T(128)}, u32[]{:S(2)}) copy-start(f32[8]{0:T(128)} %param.44) | copy-start | bytes 100
  30.9 33.5 %copy-start.10 = (bf16[768,64]{0,1:T(8,128)(2,1)S(1)}, bf16[768,64]{0,1:T(8,128)(2,1)}, u32[]{:S(2)}) copy-start(bf16[768,64]{0,1:T(8,128)(2,1)} %param.41) | copy-start | bytes 294916
  30.9 36.4 %copy-start.31 = (f32[64]{0:T(128)S(1)}, f32[64]{0:T(128)}, u32[]{:S(2)}) copy-start(f32[64]{0:T(128)} %param.42) | copy-start | bytes 772
  69.0 1.4 copy-start.2
  380.9 0.7 copy-start.14
  381.0 324.1 %reduce-scatter.6.cloned.1.call-start = ((), (), s32[]{:S(2)}) async-start(), calls=%async_computation.4 | async-start | bytes 995328 | tf_op jit(solution)/shard_map/reduce_scatter | solution.py:880
  382.4 210.1 %collective-permute-start.2 = (f32[96,768]{1,0:T(8,128)}, f32[96,768]{1,0:T(8,128)}, u32[]{:S(2)}, u32[]{:S(2)}) collective-permute-start(f32[96,768]{1,0:T(8,128)} %get-tuple-element.130), channel_id=1, source_target_pairs={{0,2},{2,0},{4,6},{6,4},{8,10},{10,8},{12,14},{14,12},{16,18},{18,... | collective-permute-start | bytes 884744 | tf_op jit(solution)/shard_map/ppermute | solution.py:848
  382.4 213.2 %copy-start.9 = (bf16[128,768]{1,0:T(8,128)(2,1)S(1)}, bf16[128,768]{1,0:T(8,128)(2,1)}, u32[]{:S(2)}) copy-start(bf16[128,768]{1,0:T(8,128)(2,1)} %get-tuple-element.132) | copy-start | bytes 589828
  592.5 112.6 %reduce-scatter.8.cloned.1.call-start = ((), (), s32[]{:S(2)}) async-start(), calls=%async_computation.5 | async-start | bytes 2506752 | tf_op jit(solution)/shard_map/reduce_scatter | solution.py:837
  593.8 111.2 %collective-permute-start.3 = (f32[96,768]{1,0:T(8,128)S(1)}, f32[96,768]{1,0:T(8,128)S(1)}, u32[]{:S(2)}, u32[]{:S(2)}) collective-permute-start(f32[96,768]{1,0:T(8,128)S(1)} %add.278), channel_id=1, source_target_pairs={{0,1},{1,0},{2,3},{3,2},{4,5},{5,4},{6,7},{7,6},{8,9},{9,8},{10,11... | collective-permute-start | bytes 884744 | tf_op jit(solution)/shard_map/ppermute | solution.py:848
  596.3 108.7 %collective-permute-start.4 = (bf16[8,8,768]{2,1,0:T(8,128)(2,1)S(1)}, bf16[8,8,768]{2,1,0:T(8,128)(2,1)S(1)}, u32[]{:S(2)}, u32[]{:S(2)}) collective-permute-start(bf16[8,8,768]{2,1,0:T(8,128)(2,1)S(1)} %get-tuple-element.200), channel_id=1, source_target_pairs={{1,0},{0,1},{3,2},{2,3},{5,4},{4,5},{7,6},{6,7},{9,8},{8,9},{11,10... | collective-permute-start | bytes 294920 | tf_op jit(solution)/shard_map/ppermute | solution.py:722
  705.0 6.9 copy-start.11
  705.1 6.9 copy-start.6
  711.9 14.0 %copy-start.7 = (f32[96,768]{1,0:T(8,128)S(1)}, f32[96,768]{1,0:T(8,128)}, u32[]{:S(2)}) copy-start(f32[96,768]{1,0:T(8,128)} %copy-done.6) | copy-start | bytes 884740
  712.0 20.4 %copy-start.3 = (bf16[768,768]{1,0:T(8,128)(2,1)S(1)}, bf16[768,768]{1,0:T(8,128)(2,1)}, u32[]{:S(2)}) copy-start(bf16[768,768]{1,0:T(8,128)(2,1)} %get-tuple-element.151) | copy-start | bytes 3538948
  712.0 18.7 %collective-permute-start.6 = (bf16[448,768]{1,0:T(8,128)(2,1)}, bf16[448,768]{1,0:T(8,128)(2,1)}, u32[]{:S(2)}, u32[]{:S(2)}) collective-permute-start(bf16[448,768]{1,0:T(8,128)(2,1)} %get-tuple-element.141), channel_id=1, source_target_pairs={{1,0},{0,1},{3,2},{2,3},{5,4},{4,5},{7,6},{6,7},{9,8},{8,9},{11,10... | collective-permute-start | bytes 2064392 | tf_op jit(solution)/shard_map/ppermute | solution.py:722
  725.6 75.6 %collective-permute-start.5 = (bf16[1120,768]{1,0:T(8,128)(2,1)}, bf16[1120,768]{1,0:T(8,128)(2,1)S(1)}, u32[]{:S(2)}, u32[]{:S(2)}) collective-permute-start(bf16[1120,768]{1,0:T(8,128)(2,1)} %get-tuple-element.143), channel_id=1, source_target_pairs={{1,0},{0,1},{3,2},{2,3},{5,4},{4,5},{7,6},{6,7},{9,8},{8,9},{11,10... | collective-permute-start | bytes 5160968 | tf_op jit(solution)/shard_map/ppermute | solution.py:722
  730.7 17.6 %collective-permute-start.7 = (f32[96,768]{1,0:T(8,128)S(1)}, f32[96,768]{1,0:T(8,128)}, u32[]{:S(2)}, u32[]{:S(2)}) collective-permute-start(f32[96,768]{1,0:T(8,128)S(1)} %add.279), channel_id=1, source_target_pairs={{0,4},{2,6},{4,0},{6,2},{8,12},{10,14},{12,8},{14,10},{16,20},{18,... | collective-permute-start | bytes 884744 | tf_op jit(solution)/shard_map/ppermute | solution.py:848
  733.2 15.0 %copy-start.16 = (f32[8,768]{1,0:T(8,128)S(1)}, f32[8,768]{1,0:T(8,128)}, u32[]{:S(2)}) copy-start(f32[8,768]{1,0:T(8,128)} %get-tuple-element.157) | copy-start | bytes 73732
  733.3 15.0 %copy-start.17 = (f32[8,768]{1,0:T(8,128)S(1)}, f32[8,768]{1,0:T(8,128)}, u32[]{:S(2)}) copy-start(f32[8,768]{1,0:T(8,128)} %get-tuple-element.158) | copy-start | bytes 73732
  733.3 17.9 %copy-start.5 = (bf16[1,9,48,384]{3,2,1,0:T(8,128)(2,1)S(1)}, bf16[1,9,48,384]{3,2,1,0:T(8,128)(2,1)}, u32[]{:S(2)}) copy-start(bf16[1,9,48,384]{3,2,1,0:T(8,128)(2,1)} %reduce-scatter.6.cloned.1.call-done) | copy-start | bytes 995332
  733.3 15.0 %collective-permute-start.8 = (bf16[8,48,768]{2,1,0:T(8,128)(2,1)}, bf16[8,48,768]{2,1,0:T(8,128)(2,1)S(1)}, u32[]{:S(2)}, u32[]{:S(2)}) collective-permute-start(bf16[8,48,768]{2,1,0:T(8,128)(2,1)} %dynamic-slice_bitcast_fusion.1), channel_id=1, source_target_pairs={{0,2},{2,0},{4,6},{6,4},{8,10},{10,8},{12,14},{14,12},{16,18},{18,... | collective-permute-start | bytes 1769480 | tf_op jit(solution)/shard_map/ppermute | solution.py:848
  748.2 6.7 copy-start.4
  748.2 6.7 copy-start.12
  749.0 16.9 %collective-permute-start.10 = (f32[4,768]{1,0:T(4,128)S(1)}, f32[4,768]{1,0:T(4,128)S(1)}, u32[]{:S(2)}, u32[]{:S(2)}) collective-permute-start(f32[4,768]{1,0:T(4,128)S(1)} %slice_add_fusion), channel_id=1, source_target_pairs={{0,4},{2,6},{4,0},{6,2},{8,12},{10,14},{12,8},{14,10},{16,20},{18,... | collective-permute-start | bytes 36872 | tf_op jit(solution)/shard_map/ppermute | solution.py:848
  749.3 17.1 %collective-permute-start.11 = (f32[4,768]{1,0:T(4,128)S(1)}, f32[4,768]{1,0:T(4,128)S(1)}, u32[]{:S(2)}, u32[]{:S(2)}) collective-permute-start(f32[4,768]{1,0:T(4,128)S(1)} %slice_add_fusion), channel_id=1, source_target_pairs={{0,6},{2,4},{4,2},{6,0},{8,14},{10,12},{12,10},{14,8},{16,22},{18,... | collective-permute-start | bytes 36872 | tf_op jit(solution)/shard_map/ppermute | solution.py:848
  750.8 15.6 %collective-permute-start.9 = (f32[4,768]{1,0:T(4,128)S(1)}, f32[4,768]{1,0:T(4,128)S(1)}, u32[]{:S(2)}, u32[]{:S(2)}) collective-permute-start(f32[4,768]{1,0:T(4,128)S(1)} %slice_add_fusion), channel_id=1, source_target_pairs={{0,2},{2,0},{4,6},{6,4},{8,10},{10,8},{12,14},{14,12},{16,18},{18,... | collective-permute-start | bytes 36872 | tf_op jit(solution)/shard_map/ppermute | solution.py:848
  753.9 9.4 %collective-permute-start.15 = (bf16[4,48,768]{2,1,0:T(8,128)(2,1)}, bf16[4,48,768]{2,1,0:T(8,128)(2,1)}, u32[]{:S(2)}, u32[]{:S(2)}) collective-permute-start(bf16[4,48,768]{2,1,0:T(8,128)(2,1)} %dynamic-slice_bitcast_fusion.2), channel_id=1, source_target_pairs={{0,4},{2,6},{4,0},{6,2},{8,12},{10,14},{12,8},{14,10},{16,20},{18,... | collective-permute-start | bytes 884744 | tf_op jit(solution)/shard_map/ppermute | solution.py:848
  763.3 16.3 %collective-permute-start.18 = (f32[96,768]{1,0:T(8,128)S(1)}, f32[96,768]{1,0:T(8,128)S(1)}, u32[]{:S(2)}, u32[]{:S(2)}) collective-permute-start(f32[96,768]{1,0:T(8,128)S(1)} %add.306), channel_id=1, source_target_pairs={{0,8},{2,10},{4,12},{6,14},{8,0},{10,2},{12,4},{14,6},{16,24},{18,... | collective-permute-start | bytes 884744 | tf_op jit(solution)/shard_map/ppermute | solution.py:848
  765.9 9.0 %collective-permute-start.16 = (bf16[2,48,768]{2,1,0:T(8,128)(2,1)S(1)}, bf16[2,48,768]{2,1,0:T(8,128)(2,1)S(1)}, u32[]{:S(2)}, u32[]{:S(2)}) collective-permute-start(bf16[2,48,768]{2,1,0:T(8,128)(2,1)S(1)} %dynamic-slice_bitcast_fusion.3), channel_id=1, source_target_pairs={{0,8},{2,10},{4,12},{6,14},{8,0},{10,2},{12,4},{14,6},{16,24},{18,... | collective-permute-start | bytes 442376 | tf_op jit(solution)/shard_map/ppermute | solution.py:848
  766.4 10.1 %collective-permute-start.13 = (f32[4,768]{1,0:T(4,128)S(1)}, f32[4,768]{1,0:T(4,128)S(1)}, u32[]{:S(2)}, u32[]{:S(2)}) collective-permute-start(f32[4,768]{1,0:T(4,128)S(1)} %add_add_fusion.1), channel_id=1, source_target_pairs={{0,16},{2,18},{4,20},{6,22},{8,24},{10,26},{12,28},{14,30},{16,0},... | collective-permute-start | bytes 36872 | tf_op jit(solution)/shard_map/ppermute | solution.py:848
  769.1 10.4 %collective-permute-start.14 = (f32[4,768]{1,0:T(4,128)S(1)}, f32[4,768]{1,0:T(4,128)S(1)}, u32[]{:S(2)}, u32[]{:S(2)}) collective-permute-start(f32[4,768]{1,0:T(4,128)S(1)} %add_add_fusion.1), channel_id=1, source_target_pairs={{0,24},{2,26},{4,28},{6,30},{8,16},{10,18},{12,20},{14,22},{16,8},... | collective-permute-start | bytes 36872 | tf_op jit(solution)/shard_map/ppermute | solution.py:848
  774.9 4.6 collective-permute-start.12
  776.6 12.8 %collective-permute-start.17 = (bf16[1,48,768]{2,1,0:T(8,128)(2,1)S(1)}, bf16[1,48,768]{2,1,0:T(8,128)(2,1)S(1)}, u32[]{:S(2)}, u32[]{:S(2)}) collective-permute-start(bf16[1,48,768]{2,1,0:T(8,128)(2,1)S(1)} %constant_dynamic-slice_fusion.1), channel_id=1, source_target_pairs={{0,16},{2,18},{4,20},{6,22},{8,24},{10,26},{12,28},{14,30},{16,0},... | collective-permute-start | bytes 221192 | tf_op jit(solution)/shard_map/ppermute | solution.py:848
  779.6 15.4 %collective-permute-start.19 = (f32[96,768]{1,0:T(8,128)S(1)}, f32[96,768]{1,0:T(8,128)}, u32[]{:S(2)}, u32[]{:S(2)}) collective-permute-start(f32[96,768]{1,0:T(8,128)S(1)} %add.307), channel_id=1, source_target_pairs={{0,16},{2,18},{4,20},{6,22},{8,24},{10,26},{12,28},{14,30},{16,0},... | collective-permute-start | bytes 884744 | tf_op jit(solution)/shard_map/ppermute | solution.py:848
  800.0 10.5 %copy-start.1 = (bf16[64,8]{0,1:T(8,128)(2,1)S(1)}, bf16[64,8]{0,1:T(8,128)(2,1)}, u32[]{:S(2)}) copy-start(bf16[64,8]{0,1:T(8,128)(2,1)} %param.43) | copy-start | bytes 3076
  801.2 4.3 collective-permute-start.20
  803.0 6.5 collective-permute-start.21
Sparse Core Ops, SparseCore 0:
  381.1 121.6 reduce-scatter.3
  592.7 20.8 reduce-scatter.5
  617.8 64.4 reduce-scatter.7

commit v6 on v4

--- a/solution.py
+++ b/solution.py
@@ -754,10 +754,9 @@
 
     key_ids = jnp.arange(keys, dtype=jnp.int32)
     key_inside = placed(key_ids % rows, key_ids // rows)
-    lane16 = jnp.arange(HEAD)
+    lane16 = jnp.arange(128)
     key_mask = jnp.where(key_inside, 0.0, masked_score)
     kaug = jnp.where(lane16[None, :] < 3, 1.0, jnp.where(lane16[None, :] == 3, key_mask[:, None], 0.0)).astype(bf16)
-    kaug = jnp.concatenate([kaug, jnp.zeros_like(kaug)], axis=1)
     sub16 = jnp.arange(16)[:, None]
     wide_mask = jnp.pad(key_mask, (0, up(keys, TILE) - keys), constant_values=masked_score)
     kaug_t = jnp.where(sub16 < 3, 1.0, jnp.where(sub16 == 3, wide_mask[None, :], 0.0)).astype(bf16)
@@ -920,7 +919,9 @@
     kept, received = part_ways(add_low(kept, received), clip_steps[2])
     if split:
         input_grad, late = finish(0, piece, x_low, *rest, place=position % clip_count, places=clip_count)
-        input_grad, late, near_early, received = tie((input_grad, late, near_early, received))
+        input_grad, late, near_early, received, slab, pooled = tie(
+            (input_grad, late, near_early, received, slab, pooled)
+        )
         other = (position + 1) % clip_count
         input_grad = lax.dynamic_update_slice(input_grad, home0.astype(f32)[None], (other, 0, 0))
         late = late + sums0 + sums1
@@ -941,7 +942,7 @@
     if len(clip_steps) % 2:
         late = late + meet(late, clip_steps[-1])
     if split:
-        home1, late, slab1, slab, early, pooled = tie((home1, late, slab1, slab, early, pooled))
+        home1, late, slab1, early = tie((home1, late, slab1, early))
     for step in seq_steps:
         late = late + meet(late, step)
     qkv = [

time: 807 us -> 822 us (1.019)
  waiting for transfers between devices: 9.76 us -> 27.2 us
    ppermute x5, waiting for transfers between devices: 6.54 us -> 24 us  [send(): return lax.ppermute(value, 'seq', pairs)]
  transfers between devices with their start and end apart: 25 -> 25, of which waited for: 7 -> 5; matrix products, arithmetic and copies ran while one was open for 4% -> 3% of each run, Pallas kernels for 50% -> 49%
where the time goes in v6:
time: 822 us; the launch traced here: 816 us
  Pallas kernels  708 us (86%)
  waiting for transfers between devices  27.2 us (3%)
  starting transfers between devices  25.3 us (3%)
  local copies, waits for them, and re-layouts  20.2 us (2%)
  other arithmetic  18 us (2%)
  between operations  17.5 us (2%)
    pallas_call x2, Pallas kernels, attend_back(): pl.pallas_call(attend_back_kernel, grid=(pairs, rows // size), in_specs=[...  318 us
    pallas_call x1, Pallas kernels, middle(): pl.pallas_call(middle_kernel, grid=(rows // size,), in_specs=[tile, tile]...  184 us
    pallas_call x1, Pallas kernels, attend(): pl.pallas_call(attend_kernel, grid=(pairs,), in_specs=[pl.BlockSpec((rows...  114 us
    pallas_call x3, Pallas kernels, finish(): pl.pallas_call(finish_kernel, grid_spec=pltpu.PrefetchScalarGridSpec(num_...  33.5 us
    pallas_call x1, Pallas kernels, attend_near(): pl.pallas_call(attend_near_kernel, grid=(pairs,), in_specs=[pl.BlockSpec(...  33.3 us
    ppermute x5, waiting for transfers between devices, send(): return lax.ppermute(value, 'seq', pairs)  24 us
    pallas_call x2, Pallas kernels, project(): pl.pallas_call(project_kernel, grid_spec=pltpu.PrefetchScalarGridSpec(num...  23.3 us
    ppermute x17, starting transfers between devices, meet(): lax.ppermute(value, axis, [(i, i ^ bit) for i in range(lax.axis_size(axis...  18.6 us
  transfers between devices with their start and end apart: 25, of which 5 were waited for; matrix products, arithmetic and copies ran while one was open for 3% of the time, Pallas kernels for 49%

profile of v6, /device:TPU:0, one launch (start us, length us, event | category | flops | bytes accessed | tf_op | source)
XLA Modules:
  0.0 815.6 jit_solution(2813738172331739559)
XLA Ops:
  7.4 3.3 dynamic-slice_bitcast_fusion
  10.7 3.0 collective-permute-start
  14.0 0.6 reshape.389.vec
  14.7 0.6 dynamic_slice.47
  15.2 0.6 dynamic_slice.46
  16.5 1.3 fusion.17
  17.8 11.7 %project.2 = (bf16[3136,2304]{1,0:T(8,128)(2,1)}, bf16[3136,768]{1,0:T(8,128)(2,1)}, bf16[3136,768]{1,0:T(8,128)(2,1)}) custom-call(s32[1]{0:T(128)} %bitcast.place, bf16[2,1568,768]{2,1,0:T(8,128)(2,1)} %x.9, f32[14,768]{1,0:T(8,128)} %reshape.389.vec, bf16[768,2304]{1,0:T(8,128)(2,1)} %weight.9), custom_call_target="tpu_custom_call" | custom-call | tf_op jit(solution)/shard_map/project/pallas_call | solution.py:423
  29.5 1.4 select_convert_fusion.kaug
  30.9 33.3 %attend_near.1.refs_0_ = f32[12,80,1536]{2,1,0:T(8,128)} custom-call(bf16[3136,2304]{1,0:T(8,128)(2,1)} %get-tuple-element.97.q.k.v.refs_0_, bf16[3136,2304]{1,0:T(8,128)(2,1)} %get-tuple-element.97.q.k.v.refs_0_, bf16[3136,2304]{1,0:T(8,128)(2,1)} %get-tuple-element.97.q.k.v.refs_0_, bf16[3136,128]{1,0:T(8,128)(2,1)} %select_convert_fusion.kaug), custom_call_target="tpu_custom_call" | custom-call | flops 28991029248 | bytes 11796480 | tf_op jit(solution)/shard_map/attend_near/pallas_call | solution.py:117
  64.6 0.7 pad.17.m1
  65.4 0.6 pad.18.m2
  66.0 1.3 fusion.25
  67.4 0.6 stack.21.aux
  68.3 0.7 maximum_bitcast_fusion.cot
  69.0 1.4 copy-done.2
  70.4 11.7 %project.3 = (bf16[3136,2304]{1,0:T(8,128)(2,1)}, bf16[3136,768]{1,0:T(8,128)(2,1)}, bf16[3136,768]{1,0:T(8,128)(2,1)}) custom-call(s32[1]{0:T(128)} %constant.256.clone.1.place, bf16[1,1568,768]{2,1,0:T(8,128)(2,1)} %bitcast.80, f32[14,768]{1,0:T(8,128)} %reshape.389.vec, ...), custom_call_target="tpu_custom_call", output_to_operand_aliasing={{0}: (4, {}), {1}: (5, {}), {2}: (6, {})} | custom-call | tf_op jit(solution)/shard_map/project/pallas_call | solution.py:423
  82.0 114.5 %attend.1 = (bf16[3136,768]{1,0:T(8,128)(2,1)}, bf16[3136,768]{1,0:T(8,128)(2,1)}) custom-call(bf16[3136,2304]{1,0:T(8,128)(2,1)} %get-tuple-element.123.q.k.v, bf16[3136,2304]{1,0:T(8,128)(2,1)} %get-tuple-element.123.q.k.v, bf16[3136,2304]{1,0:T(8,128)(2,1)} %get-tuple-element.123.q.k.v, bf16[3136,128]{1,0:T(8,128)(2,1)} %select_convert_fusion.kaug, ...), custom_call_target="tpu_custom_call" | custom-call | flops 120846286848 | bytes 24084480 | tf_op jit(solution)/shard_map/attend/pallas_call | solution.py:204
  196.5 184.4 %middle.1 = (bf16[3136,768]{1,0:T(8,128)(2,1)}, bf16[3136,768]{1,0:T(8,128)(2,1)}, bf16[16,2,9,48,384]{4,3,2,1,0:T(8,128)(2,1)}, f32[96,768]{1,0:T(8,128)}, bf16[128,768]{1,0:T(8,128)(2,1)}) custom-call(bf16[3136,768]{1,0:T(8,128)(2,1)} %get-tuple-element.142.x, bf16[3136,768]{1,0:T(8,128)(2,1)} %get-tuple-element.103.att, f32[8,128]{1,0:T(8,128)} %stack.21.aux, ...), custom_call_target="tpu_custom_call" | custom-call | flops 99883155456 | bytes 28901376 | tf_op jit(solution)/shard_map/middle/pallas_call | solution.py:583
  381.0 0.6 copy-done.14
  381.7 0.7 select_convert_fusion.1.kaug_t
  382.4 210.1 %attend_back.2 = (bf16[3136,512]{1,0:T(8,128)(2,1)}, bf16[3136,512]{1,0:T(8,128)(2,1)}, bf16[3136,512]{1,0:T(8,128)(2,1)}, bf16[768,1536]{1,0:T(8,128)(2,1)}) custom-call(bf16[3136,2304]{1,0:T(8,128)(2,1)} %get-tuple-element.123.q.k.v, bf16[3136,768]{1,0:T(8,128)(2,1)} %get-tuple-element.108.do, bf16[3136,768]{1,0:T(8,128)(2,1)} %get-tuple-element.103.att, ...), custom_call_target="tpu_custom_call" | custom-call | flops 157351936000 | bytes 48168960 | tf_op jit(solution)/shard_map/attend_back/pallas_call | solution.py:325
  592.6 1.1 add.278
  593.7 1.8 collective-permute-start.3
  595.9 108.4 %attend_back.3 = (bf16[3136,256]{1,0:T(8,128)(2,1)}, bf16[3136,256]{1,0:T(8,128)(2,1)}, bf16[3136,256]{1,0:T(8,128)(2,1)}, bf16[768,768]{1,0:T(8,128)(2,1)}) custom-call(bf16[3136,2304]{1,0:T(8,128)(2,1)} %get-tuple-element.123.q.k.v, bf16[3136,768]{1,0:T(8,128)(2,1)} %get-tuple-element.108.do, bf16[3136,768]{1,0:T(8,128)(2,1)} %get-tuple-element.103.att, ...), custom_call_target="tpu_custom_call" | custom-call | flops 78675968000 | bytes 48168960 | tf_op jit(solution)/shard_map/attend_back/pallas_call | solution.py:325
  704.4 0.6 copy-done.11
  704.9 1.1 dynamic-slice_bitcast_fusion.1
  706.3 1.7 collective-permute-start.5
  708.0 1.0 reshape.393
  709.0 6.8 finish.3
  715.9 0.7 copy-done.6
  716.6 1.0 add.282
  717.6 1.7 collective-permute-start.7
  719.5 1.5 collective-permute-start.8
  720.9 1.5 collective-permute-start.9
  722.5 11.8 %finish.4 = (bf16[1120,768]{1,0:T(8,128)(2,1)}, f32[8,768]{1,0:T(8,128)}) custom-call(s32[1]{0:T(128)} %constant.256.clone.1.place, bf16[3136,768]{1,0:T(8,128)(2,1)} %get-tuple-element.142.x, bf16[3136,768]{1,0:T(8,128)(2,1)} %get-tuple-element.104.g1, f32[14,768]{1,0:T(8,128)} %reshape.389.vec, bf16[768,2304]{1,0:T(8,128)(2,1)} %weight.9, ...), custom_call_target="tpu_custom_call" | custom-call | flops 7927234560 | bytes 8601600 | tf_op jit(solution)/shard_map/finish/pallas_call | solution.py:658
  734.3 3.2 collective-permute-done.9
  737.5 1.0 add.287
  738.5 2.7 collective-permute-start.10
  741.9 14.9 %finish.5 = (f32[2,1568,768]{2,1,0:T(8,128)}, f32[8,768]{1,0:T(8,128)}) custom-call(s32[1]{0:T(128)} %bitcast.place, bf16[3136,768]{1,0:T(8,128)(2,1)} %get-tuple-element.142.x, bf16[3136,768]{1,0:T(8,128)(2,1)} %get-tuple-element.104.g1, f32[14,768]{1,0:T(8,128)} %reshape.389.vec, bf16[768,2304]{1,0:T(8,128)(2,1)} %weight.9, ...), custom_call_target="tpu_custom_call" | custom-call | flops 11098128384 | bytes 12042240 | tf_op jit(solution)/shard_map/finish/pallas_call | solution.py:658
  756.8 1.6 collective-permute-start.12
  758.4 0.8 slice_add_fusion
  759.2 1.1 collective-permute-start.14
  760.4 1.0 collective-permute-start.13
  761.4 0.6 bitcast_convert_fusion.1
  762.1 0.9 fusion.2
  763.0 0.7 bitcast_convert_fusion
  763.8 1.2 convert_dynamic-update-slice_fusion.1
  765.2 2.8 collective-permute-start.17
  768.0 1.3 collective-permute-start.18
  769.5 1.0 add.308
  770.5 0.7 copy.82
  771.3 1.2 gather_fusion
  772.5 0.9 collective-permute-done.18
  773.5 20.5 %collective-permute-done.12 = bf16[1120,768]{1,0:T(8,128)(2,1)S(1)} collective-permute-done((bf16[1120,768]{1,0:T(8,128)(2,1)}, bf16[1120,768]{1,0:T(8,128)(2,1)S(1)}, u32[]{:S(2)}, u32[]{:S(2)}) %collective-permute-start.12) | collective-permute-done | bytes 1720352 | tf_op jit(solution)/shard_map/ppermute | solution.py:722
  794.0 0.6 slice_reduce_fusion.4
  794.7 0.7 slice_bitcast_fusion
  795.9 1.6 collective-permute-start.20
  797.9 2.0 convert_dynamic-update-slice_fusion
  800.2 0.6 slice_reduce_fusion.10
  801.2 0.6 reshape.396
  802.0 0.7 reshape.398
  804.0 0.6 slice_reduce_fusion
  804.6 2.1 collective-permute-done.21
  807.0 0.7 copy.84
  (151 shorter events, 5.8 us)
Async XLA Ops:
  7.2 57.3 %copy-start = (bf16[64,8]{0,1:T(8,128)(2,1)S(1)}, bf16[64,8]{0,1:T(8,128)(2,1)}, u32[]{:S(2)}) copy-start(bf16[64,8]{0,1:T(8,128)(2,1)} %param.43) | copy-start | bytes 3076
  7.2 6.4 copy-start.7
  7.2 6.5 copy-start.18
  7.2 6.6 copy-start.19
  7.2 6.6 copy-start.20
  7.3 6.6 copy-start.21
  7.3 6.6 copy-start.22
  7.3 6.6 copy-start.23
  7.3 6.6 copy-start.24
  7.3 6.6 copy-start.25
  7.3 6.7 copy-start.26
  7.3 6.7 copy-start.27
  7.3 6.7 copy-start.15
  7.3 7.3 copy-start.29
  7.3 7.9 copy-start.30
  7.4 585.1 %reduce-scatter.4.cloned.1.call-start = ((), (), s32[]{:S(2)}) async-start(), calls=%async_computation.3 | async-start | bytes 11280384 | tf_op jit(solution)/shard_map/reduce_scatter | solution.py:838
  10.7 58.3 %collective-permute-start = (bf16[1568,768]{1,0:T(8,128)(2,1)}, bf16[1568,768]{1,0:T(8,128)(2,1)S(1)}, u32[]{:S(2)}, u32[]{:S(2)}) collective-permute-start(bf16[1568,768]{1,0:T(8,128)(2,1)} %dynamic-slice_bitcast_fusion), channel_id=1, source_target_pairs={{0,1},{1,0},{2,3},{3,2},{4,5},{5,4},{6,7},{7,6},{8,9},{9,8},{10,11... | collective-permute-start | bytes 7225352 | tf_op jit(solution)/shard_map/ppermute | solution.py:722
  13.7 54.6 %collective-permute-start.1 = (bf16[8,8,768]{2,1,0:T(8,128)(2,1)S(1)}, bf16[8,8,768]{2,1,0:T(8,128)(2,1)S(1)}, u32[]{:S(2)}, u32[]{:S(2)}) collective-permute-start(bf16[8,8,768]{2,1,0:T(8,128)(2,1)S(1)} %get-tuple-element.183), channel_id=1, source_target_pairs={{0,1},{1,0},{2,3},{3,2},{4,5},{5,4},{6,7},{7,6},{8,9},{9,8},{10,11... | collective-permute-start | bytes 294920 | tf_op jit(solution)/shard_map/ppermute | solution.py:722
  17.8 11.7 %copy-start.13 = (bf16[3136]{0:T(1024)(128)(2,1)}, bf16[3136]{0:T(1024)(128)(2,1)S(1)}, u32[]{:S(2)}) copy-start(bf16[3136]{0:T(1024)(128)(2,1)S(1)} %fusion.17) | copy-start | bytes 18820
  30.9 33.4 %copy-start.28 = (f32[8]{0:T(128)S(1)}, f32[8]{0:T(128)}, u32[]{:S(2)}) copy-start(f32[8]{0:T(128)} %param.44) | copy-start | bytes 100
  30.9 33.5 %copy-start.10 = (bf16[768,64]{0,1:T(8,128)(2,1)S(1)}, bf16[768,64]{0,1:T(8,128)(2,1)}, u32[]{:S(2)}) copy-start(bf16[768,64]{0,1:T(8,128)(2,1)} %param.41) | copy-start | bytes 294916
  30.9 36.4 %copy-start.31 = (f32[64]{0:T(128)S(1)}, f32[64]{0:T(128)}, u32[]{:S(2)}) copy-start(f32[64]{0:T(128)} %param.42) | copy-start | bytes 772
  69.0 1.4 copy-start.2
  380.9 0.7 copy-start.14
  381.0 323.4 %reduce-scatter.6.cloned.1.call-start = ((), (), s32[]{:S(2)}) async-start(), calls=%async_computation.4 | async-start | bytes 995328 | tf_op jit(solution)/shard_map/reduce_scatter | solution.py:881
  382.4 210.1 %collective-permute-start.2 = (f32[96,768]{1,0:T(8,128)}, f32[96,768]{1,0:T(8,128)}, u32[]{:S(2)}, u32[]{:S(2)}) collective-permute-start(f32[96,768]{1,0:T(8,128)} %get-tuple-element.120), channel_id=1, source_target_pairs={{0,2},{2,0},{4,6},{6,4},{8,10},{10,8},{12,14},{14,12},{16,18},{18,... | collective-permute-start | bytes 884744 | tf_op jit(solution)/shard_map/ppermute | solution.py:849
  382.4 213.1 %copy-start.8 = (bf16[128,768]{1,0:T(8,128)(2,1)S(1)}, bf16[128,768]{1,0:T(8,128)(2,1)}, u32[]{:S(2)}) copy-start(bf16[128,768]{1,0:T(8,128)(2,1)} %get-tuple-element.122) | copy-start | bytes 589828
  592.5 111.8 %reduce-scatter.8.cloned.1.call-start = ((), (), s32[]{:S(2)}) async-start(), calls=%async_computation.5 | async-start | bytes 2506752 | tf_op jit(solution)/shard_map/reduce_scatter | solution.py:838
  593.7 110.6 %collective-permute-start.3 = (f32[96,768]{1,0:T(8,128)S(1)}, f32[96,768]{1,0:T(8,128)S(1)}, u32[]{:S(2)}, u32[]{:S(2)}) collective-permute-start(f32[96,768]{1,0:T(8,128)S(1)} %add.278), channel_id=1, source_target_pairs={{0,1},{1,0},{2,3},{3,2},{4,5},{5,4},{6,7},{7,6},{8,9},{9,8},{10,11... | collective-permute-start | bytes 884744 | tf_op jit(solution)/shard_map/ppermute | solution.py:849
  595.5 108.8 %collective-permute-start.4 = (bf16[8,8,768]{2,1,0:T(8,128)(2,1)S(1)}, bf16[8,8,768]{2,1,0:T(8,128)(2,1)S(1)}, u32[]{:S(2)}, u32[]{:S(2)}) collective-permute-start(bf16[8,8,768]{2,1,0:T(8,128)(2,1)S(1)} %get-tuple-element.180), channel_id=1, source_target_pairs={{1,0},{0,1},{3,2},{2,3},{5,4},{4,5},{7,6},{6,7},{9,8},{8,9},{11,10... | collective-permute-start | bytes 294920 | tf_op jit(solution)/shard_map/ppermute | solution.py:722
  704.3 0.6 copy-start.11
  706.0 9.8 %collective-permute-start.6 = (bf16[8,48,768]{2,1,0:T(8,128)(2,1)S(1)}, bf16[8,48,768]{2,1,0:T(8,128)(2,1)S(1)}, u32[]{:S(2)}, u32[]{:S(2)}) collective-permute-start(bf16[8,48,768]{2,1,0:T(8,128)(2,1)S(1)} %dynamic-slice_bitcast_fusion.1), channel_id=1, source_target_pairs={{0,2},{2,0},{4,6},{6,4},{8,10},{10,8},{12,14},{14,12},{16,18},{18,... | collective-permute-start | bytes 1769480 | tf_op jit(solution)/shard_map/ppermute | solution.py:849
  706.3 9.5 %collective-permute-start.5 = (f32[96,768]{1,0:T(8,128)S(1)}, f32[96,768]{1,0:T(8,128)S(1)}, u32[]{:S(2)}, u32[]{:S(2)}) collective-permute-start(f32[96,768]{1,0:T(8,128)S(1)} %add.279), channel_id=1, source_target_pairs={{0,4},{2,6},{4,0},{6,2},{8,12},{10,14},{12,8},{14,10},{16,20},{18,... | collective-permute-start | bytes 884744 | tf_op jit(solution)/shard_map/ppermute | solution.py:849
  709.0 10.3 %copy-start.3 = (bf16[768,768]{1,0:T(8,128)(2,1)S(1)}, bf16[768,768]{1,0:T(8,128)(2,1)}, u32[]{:S(2)}) copy-start(bf16[768,768]{1,0:T(8,128)(2,1)} %get-tuple-element.135) | copy-start | bytes 3538948
  715.8 0.7 copy-start.6
  717.6 16.7 %collective-permute-start.7 = (f32[96,768]{1,0:T(8,128)S(1)}, f32[96,768]{1,0:T(8,128)S(1)}, u32[]{:S(2)}, u32[]{:S(2)}) collective-permute-start(f32[96,768]{1,0:T(8,128)S(1)} %add.282), channel_id=1, source_target_pairs={{0,8},{2,10},{4,12},{6,14},{8,0},{10,2},{12,4},{14,6},{16,24},{18,... | collective-permute-start | bytes 884744 | tf_op jit(solution)/shard_map/ppermute | solution.py:849
  719.5 14.9 %collective-permute-start.8 = (bf16[4,48,768]{2,1,0:T(8,128)(2,1)S(1)}, bf16[4,48,768]{2,1,0:T(8,128)(2,1)S(1)}, u32[]{:S(2)}, u32[]{:S(2)}) collective-permute-start(bf16[4,48,768]{2,1,0:T(8,128)(2,1)S(1)} %dynamic-slice_bitcast_fusion.2), channel_id=1, source_target_pairs={{0,4},{2,6},{4,0},{6,2},{8,12},{10,14},{12,8},{14,10},{16,20},{18,... | collective-permute-start | bytes 884744 | tf_op jit(solution)/shard_map/ppermute | solution.py:849
  720.9 16.6 %collective-permute-start.9 = (bf16[448,768]{1,0:T(8,128)(2,1)}, bf16[448,768]{1,0:T(8,128)(2,1)S(1)}, u32[]{:S(2)}, u32[]{:S(2)}) collective-permute-start(bf16[448,768]{1,0:T(8,128)(2,1)} %get-tuple-element.141), channel_id=1, source_target_pairs={{1,0},{0,1},{3,2},{2,3},{5,4},{4,5},{7,6},{6,7},{9,8},{8,9},{11,10... | collective-permute-start | bytes 2064392 | tf_op jit(solution)/shard_map/ppermute | solution.py:722
  734.3 3.2 copy-start.5
  738.5 19.9 %collective-permute-start.10 = (f32[96,768]{1,0:T(8,128)S(1)}, f32[96,768]{1,0:T(8,128)}, u32[]{:S(2)}, u32[]{:S(2)}) collective-permute-start(f32[96,768]{1,0:T(8,128)S(1)} %add.287), channel_id=1, source_target_pairs={{0,16},{2,18},{4,20},{6,22},{8,24},{10,26},{12,28},{14,30},{16,0},... | collective-permute-start | bytes 884744 | tf_op jit(solution)/shard_map/ppermute | solution.py:849
  741.4 17.1 %copy-start.16 = (f32[8,768]{1,0:T(8,128)S(1)}, f32[8,768]{1,0:T(8,128)}, u32[]{:S(2)}) copy-start(f32[8,768]{1,0:T(8,128)} %get-tuple-element.154) | copy-start | bytes 73732
  741.4 17.1 %copy-start.17 = (f32[8,768]{1,0:T(8,128)S(1)}, f32[8,768]{1,0:T(8,128)}, u32[]{:S(2)}) copy-start(f32[8,768]{1,0:T(8,128)} %get-tuple-element.155) | copy-start | bytes 73732
  741.4 20.0 %copy-start.4 = (bf16[1,9,48,384]{3,2,1,0:T(8,128)(2,1)S(1)}, bf16[1,9,48,384]{3,2,1,0:T(8,128)(2,1)}, u32[]{:S(2)}) copy-start(bf16[1,9,48,384]{3,2,1,0:T(8,128)(2,1)} %reduce-scatter.6.cloned.1.call-done) | copy-start | bytes 995332
  741.4 17.0 %collective-permute-start.11 = (bf16[2,48,768]{2,1,0:T(8,128)(2,1)S(1)}, bf16[2,48,768]{2,1,0:T(8,128)(2,1)S(1)}, u32[]{:S(2)}, u32[]{:S(2)}) collective-permute-start(bf16[2,48,768]{2,1,0:T(8,128)(2,1)S(1)} %dynamic-slice_bitcast_fusion.4), channel_id=1, source_target_pairs={{0,8},{2,10},{4,12},{6,14},{8,0},{10,2},{12,4},{14,6},{16,24},{18,... | collective-permute-start | bytes 442376 | tf_op jit(solution)/shard_map/ppermute | solution.py:849
  756.8 12.7 %copy-start.12 = (bf16[8,8,768]{2,1,0:T(8,128)(2,1)S(1)}, bf16[8,8,768]{2,1,0:T(8,128)(2,1)}, u32[]{:S(2)}) copy-start(bf16[8,8,768]{2,1,0:T(8,128)(2,1)} %copy-done.11) | copy-start | bytes 294916
  756.8 37.3 %collective-permute-start.12 = (bf16[1120,768]{1,0:T(8,128)(2,1)}, bf16[1120,768]{1,0:T(8,128)(2,1)S(1)}, u32[]{:S(2)}, u32[]{:S(2)}) collective-permute-start(bf16[1120,768]{1,0:T(8,128)(2,1)} %get-tuple-element.152), channel_id=1, source_target_pairs={{1,0},{0,1},{3,2},{2,3},{5,4},{4,5},{7,6},{6,7},{9,8},{8,9},{11,10... | collective-permute-start | bytes 5160968 | tf_op jit(solution)/shard_map/ppermute | solution.py:722
  758.4 1.9 copy-start.9
  759.2 5.9 collective-permute-start.14
  760.4 4.8 collective-permute-start.15
  760.4 4.8 collective-permute-start.13
  764.9 8.5 %collective-permute-start.19 = (bf16[1,48,768]{2,1,0:T(8,128)(2,1)S(1)}, bf16[1,48,768]{2,1,0:T(8,128)(2,1)S(1)}, u32[]{:S(2)}, u32[]{:S(2)}) collective-permute-start(bf16[1,48,768]{2,1,0:T(8,128)(2,1)S(1)} %constant_dynamic-slice_fusion), channel_id=1, source_target_pairs={{0,16},{2,18},{4,20},{6,22},{8,24},{10,26},{12,28},{14,30},{16,0},... | collective-permute-start | bytes 221192 | tf_op jit(solution)/shard_map/ppermute | solution.py:849
  765.2 7.3 collective-permute-start.17
  768.0 5.5 collective-permute-start.18
  769.2 4.2 collective-permute-start.16
  795.9 8.1 collective-permute-start.20
  797.8 10.0 %copy-start.1 = (bf16[64,8]{0,1:T(8,128)(2,1)S(1)}, bf16[64,8]{0,1:T(8,128)(2,1)}, u32[]{:S(2)}) copy-start(bf16[64,8]{0,1:T(8,128)(2,1)} %param.43) | copy-start | bytes 3076
  800.8 5.9 collective-permute-start.21
Sparse Core Ops, SparseCore 0:
  381.1 121.6 reduce-scatter.3
  592.7 20.7 reduce-scatter.5
  617.7 64.4 reduce-scatter.7
